TPU v7x, 32 devices: a whole 2x2x4 slice. The times are simulated.
32 devices in a mesh: groups: 1, expert: 32 (over z, y, x, core), cuts: 1.
Axes of the slice: x: 2, y: 2, z: 4, core: 2. Of those that a mesh axis runs over, the one named last changes fastest.
Arguments:
- tokens: bfloat16 [512, 2048], P(('groups', 'expert', 'cuts')), may hold values from -6 to 6
- routes: int32 [512, 8], P(('groups', 'expert', 'cuts')), may hold values from 0 to 31, all different within a row; in each aligned block of 16 rows (0 to 15, 16 to 31, ...) at most 8 rows name the same one
- gate_values: bfloat16 [512, 8], P(('groups', 'expert', 'cuts')), may hold values from 0.049804688 to 1
- expert_in: bfloat16 [32, 2048, 768], P('expert', None, 'cuts'), may hold values from -0.125 to 0.125
- expert_out: bfloat16 [32, 768, 2048], P('expert', 'cuts'), may hold values from -0.21875 to 0.21875
- queries: bfloat16 [32, 8192], P(('groups', 'expert')), may hold values from -4.5 to 4.5
- cached_keys: bfloat16 [32, 1536, 512], P(('groups', 'expert'), 'cuts'), may hold values from -4.5 to 4.5
- cached_values: bfloat16 [32, 1536, 512], P(('groups', 'expert'), 'cuts'), may hold values from -6 to 6
- lengths: int32 [32], P(('groups', 'expert')), may hold values from 1 to 1536, as said below
Outputs:
- moe_out: bfloat16 [512, 2048], P(('groups', 'expert', 'cuts'))
- attention_out: bfloat16 [32, 8192], P(('groups', 'expert'))
Inputs may be any that keep to these rules, and one draw needn't show every extreme that they name: `routes`: each row names 8 different experts. In each aligned block of 16 rows (the rows of one device) no expert is named by more than 8 rows, a bound that some block reaches. `lengths`: within each group, some sequence has exactly 1536 live positions.
All inputs are finite; a program needn't handle non-finite values.
Results may differ from a plain program's by a relative error of at most 0.0057.
Values may be sent and summed in bfloat16 or wider, within the bound.
No kernel may reach another device: no remote copies, remote signals or barrier semaphores. Data moves between devices by JAX's collectives and lax.ppermute only.
A program may use at most 64 MiB of HBM per device.

v0:
```python
import math

import jax
import jax.numpy as jnp
from jax import lax
from jax.sharding import PartitionSpec as P

KVH = 4
HD = 128


def attend_local(queries, cached_keys, cached_values, lengths):
    seq_count = queries.shape[0]
    half_span = cached_keys.shape[1]
    group = queries.shape[1] // (KVH * HD)
    first_pos = lax.axis_index("cuts") * half_span
    positions = first_pos + jnp.arange(half_span, dtype=jnp.int32)
    in_cache = (positions[None, :] < lengths[:, None])[:, None, None, :]
    query_blocks = queries.reshape(seq_count, KVH, group, HD)
    key_blocks = cached_keys.reshape(seq_count, half_span, KVH, HD)
    value_blocks = cached_values.reshape(seq_count, half_span, KVH, HD)
    scores = jnp.einsum(
        "skqd,spkd->skqp", query_blocks, key_blocks, preferred_element_type=jnp.float32
    ) / math.sqrt(HD)
    masked = jnp.where(in_cache, scores, jnp.float32(-1e30))
    local_top = jnp.max(masked, axis=-1)
    row_top = lax.pmax(local_top, "cuts")
    weights = jnp.exp(masked - row_top[..., None]).astype(jnp.bfloat16)
    weight_total = jnp.sum(weights.astype(jnp.float32), axis=-1)
    summed = jnp.einsum(
        "skqp,spkd->skqd", weights, value_blocks, preferred_element_type=jnp.float32
    )
    weight_total, summed = lax.psum((weight_total, summed), "cuts")
    return (
        (summed / weight_total[..., None]).reshape(seq_count, KVH * group * HD).astype(jnp.bfloat16)
    )


def route_experts(tokens, routes, gate_values, expert_in, expert_out):
    tok_rows, width = tokens.shape
    top_count = routes.shape[1]
    experts_here = lax.axis_size("expert")
    capacity = min(tok_rows, 2 * tok_rows * top_count // experts_here)
    expert_ids = jnp.arange(experts_here, dtype=jnp.int32)
    chosen = routes[:, :, None] == expert_ids[None, None, :]
    member = jnp.sum(chosen, axis=1).astype(jnp.float32)
    gate_here = jnp.sum(
        jnp.where(chosen, gate_values.astype(jnp.float32)[:, :, None], jnp.float32(0.0)), axis=1
    )
    earlier = (jnp.arange(tok_rows)[:, None] > jnp.arange(tok_rows)[None, :]).astype(jnp.float32)
    slot_index = jnp.dot(earlier, member, precision=lax.Precision.HIGHEST)
    placed = (slot_index[:, :, None] == jnp.arange(capacity, dtype=jnp.float32)[None, None, :]) & (
        member[:, :, None] > 0.5
    )
    send_matrix = placed.astype(jnp.bfloat16).reshape(tok_rows, experts_here * capacity)
    combine_matrix = (
        (placed.astype(jnp.float32) * gate_here[:, :, None])
        .astype(jnp.bfloat16)
        .reshape(tok_rows, experts_here * capacity)
    )
    outgoing = jnp.einsum("tr,td->rd", send_matrix, tokens, preferred_element_type=jnp.float32)
    outgoing = outgoing.astype(jnp.bfloat16).reshape(experts_here, capacity, width)
    arrived = lax.all_to_all(outgoing, "expert", split_axis=0, concat_axis=0, tiled=True)
    slot_rows = arrived.reshape(-1, width)
    hidden = jax.nn.silu(
        jnp.dot(
            lax.all_gather(slot_rows, "cuts", axis=0, tiled=True),
            expert_in[0],
            preferred_element_type=jnp.float32,
        )
    ).astype(jnp.bfloat16)
    produced = lax.psum_scatter(
        jnp.dot(hidden, expert_out[0], preferred_element_type=jnp.float32),
        "cuts",
        scatter_dimension=0,
        tiled=True,
    ).astype(jnp.bfloat16)
    returned = lax.all_to_all(
        produced.reshape(arrived.shape), "expert", split_axis=0, concat_axis=0, tiled=True
    )
    combined = jnp.dot(
        combine_matrix,
        returned.reshape(experts_here * capacity, width),
        preferred_element_type=jnp.float32,
    )
    return combined.astype(jnp.bfloat16)


def on_device(
    tokens, routes, gate_values, expert_in, expert_out, queries, cached_keys, cached_values, lengths
):
    moe_out = route_experts(tokens, routes, gate_values, expert_in, expert_out)
    attention_out = attend_local(queries, cached_keys, cached_values, lengths)
    return (moe_out, attention_out)


def solution(mesh):
    in_specs = (
        P(("groups", "expert", "cuts"), None),
        P(("groups", "expert", "cuts"), None),
        P(("groups", "expert", "cuts"), None),
        P("expert", None, "cuts"),
        P("expert", "cuts", None),
        P(("groups", "expert"), None),
        P(("groups", "expert"), "cuts", None),
        P(("groups", "expert"), "cuts", None),
        P(("groups", "expert")),
    )
    out_specs = (P(("groups", "expert", "cuts"), None), P(("groups", "expert"), None))
    return jax.shard_map(
        on_device, mesh=mesh, in_specs=in_specs, out_specs=out_specs, check_vma=False
    )
```

profile of v0, /device:TPU:0, one launch (start us, length us, event | category | flops | bytes accessed | tf_op | source)
XLA Modules:
  0.0 74.3 jit_solution(15196955188387818472)
XLA Ops:
  0.6 0.0 copy-start
  0.6 0.9 %copy.30 = s32[16,8]{1,0:T(8,128)S(1)} copy(s32[16,8]{0,1:T(8,128)} %param.10) | data formatting | bytes 1024 | tf_op args[1]
  1.6 0.1 convert_reduce_fusion.1
  1.7 0.2 fusion.44
  1.9 0.1 copy.32
  2.0 0.0 copy-start.1
  2.0 0.1 eq.45
  2.1 1.3 %fusion.7 = bf16[32,8,2048]{2,1,0:T(8,128)(2,1)S(1)} fusion(bf16[16,2048]{1,0:T(8,128)(2,1)} %param.9, f32[256]{0:T(256)S(1)} %eq.45, f32[16,32]{0,1:T(8,128)S(1)} %fusion.44, pred[16,32]{0,1:T(8,128)(4,1)S(1)} %copy.32), kind=kOutput, calls=%fused_computation.6 | convolution fusion | flops 17309696 | bytes 1117696 | tf_op jit(solution)/shard_map/tr,td->rd/dot_general | solution.py:61
  3.4 33.4 %all_to_all.10 = bf16[32,8,2048]{2,1,0:T(8,128)(2,1)} all-to-all(bf16[32,8,2048]{2,1,0:T(8,128)(2,1)S(1)} %fusion.7), channel_id=1, replica_groups=mesh['groups'=1,'expert'=32,'cuts'=1] {'expert'}, dimensions={0} | all-to-all | bytes 2097152 | tf_op jit(solution)/shard_map/all_to_all | solution.py:63
  36.8 0.0 copy-done.1
  36.8 0.0 copy-done
  36.8 5.3 %fusion.8 = bf16[32,8,2048]{2,1,0:T(8,128)(2,1)} fusion(bf16[1,768,2048]{2,1,0:T(8,128)(2,1)S(1)} %copy-done, bf16[1,2048,768]{2,1,0:T(8,128)(2,1)} %param.12, bf16[32,8,2048]{2,1,0:T(8,128)(2,1)} %all_to_all.10), kind=kOutput, calls=%fused_computation.7 | convolution fusion | flops 1612120064 | bytes 8388608 | tf_op jit(solution)/shard_map/dot_general | solution.py:73
  42.2 0.0 copy-start.3
  42.2 3.7 %all-to-all-start.1 = ((bf16[32,8,2048]{2,1,0:T(8,128)(2,1)}), bf16[32,8,2048]{2,1,0:T(8,128)(2,1)}, u32[]{:S(2)}, u32[]{:S(2)}) async-start(bf16[32,8,2048]{2,1,0:T(8,128)(2,1)} %fusion.8), calls=%async_computation.1 | async-start | bytes 2097152 | tf_op jit(solution)/shard_map/all_to_all | solution.py:78
  45.9 0.0 copy-done.3
  45.9 0.1 copy.33
  46.0 0.1 select_reduce_fusion
  46.1 0.7 copy.34
  46.8 3.5 %reshape.94 = bf16[1536,4,128]{2,1,0:T(4,128)(2,1)} reshape(bf16[1,1536,512]{2,1,0:T(8,128)(2,1)} %param.15) | data formatting | bytes 3145728 | tf_op jit(solution)/shard_map/reshape.3
  51.0 0.0 copy-start.2
  51.0 3.5 %reshape.95 = bf16[1536,4,128]{2,1,0:T(4,128)(2,1)} reshape(bf16[1,1536,512]{2,1,0:T(8,128)(2,1)} %param.16) | data formatting | bytes 3145728 | tf_op jit(solution)/shard_map/reshape.7
  54.5 0.0 copy-done.2
  54.5 0.7 reduce.4
  55.2 1.9 %fusion.11 = f32[4,16,1536]{2,1,0:T(8,128)S(1)} fusion(bf16[4,16,128]{2,1,0:T(8,128)(2,1)} %bitcast.47, bf16[1536,4,128]{2,1,0:T(4,128)(2,1)} %reshape.94, pred[1536]{0:T(1024)(128)(4,1)S(1)} %iota_compare_fusion.2), kind=kOutput, calls=%fused_computation.9 | convolution fusion | flops 25362432 | bytes 1984000 | tf_op jit(solution)/shard_map/skqd,spkd->skqp/dot_general | solution.py:22
  57.2 0.8 %convert_reduce_fusion = f32[4,16]{1,0:T(4,128)} fusion(f32[4,16,1536]{2,1,0:T(8,128)S(1)} %fusion.11), kind=kOutput, calls=%fused_computation.19 | output fusion | flops 394751 | bytes 393472 | tf_op jit(solution)/shard_map/sub | solution.py:28
  58.0 2.4 %fusion.19 = bf16[4,16,128]{2,1,0:T(8,128)(2,1)} fusion(bf16[1536,4,128]{2,1,0:T(4,128)(2,1)} %reshape.95, f32[4,16]{1,0:T(4,128)} %convert_reduce_fusion, f32[4,16,1536]{2,1,0:T(8,128)S(1)} %fusion.11), kind=kOutput, calls=%fused_computation.16 | convolution fusion | flops 25380416 | bytes 1982720 | tf_op jit(solution)/shard_map/skqp,spkd->skqd/dot_general | solution.py:30
  60.4 1.3 %convert_element_type.64 = bf16[1,8192]{1,0:T(2,128)(2,1)} reshape(bf16[4,16,128]{2,1,0:T(8,128)(2,1)} %fusion.19) | data formatting | bytes 32768 | tf_op jit(solution)/shard_map/convert_element_type | solution.py:35
  61.7 10.4 %all-to-all-done.1 = bf16[32,8,2048]{2,1,0:T(8,128)(2,1)} async-done(((bf16[32,8,2048]{2,1,0:T(8,128)(2,1)}), bf16[32,8,2048]{2,1,0:T(8,128)(2,1)}, u32[]{:S(2)}, u32[]{:S(2)}) %all-to-all-start.1) | async-done | bytes 1048608 | tf_op jit(solution)/shard_map/all_to_all | solution.py:78
  72.1 2.2 %fusion.12 = bf16[16,2048]{1,0:T(8,128)(2,1)} fusion(bf16[32,8,2048]{2,1,0:T(8,128)(2,1)} %all-to-all-done.1, bf16[16,32]{0,1:T(8,128)(2,1)} %copy.34, f32[16,32]{0,1:T(8,128)S(1)} %fusion.44, pred[16,32]{0,1:T(8,128)(4,1)} %copy-done.1), kind=kOutput, calls=%fused_computation.11 | convolution fusion | flops 16822272 | bytes 1117696 | tf_op jit(solution)/shard_map/dot_general | solution.py:81
  (3 shorter events, 0.0 us)
Async XLA Ops:
  0.6 36.2 %copy-start = (bf16[1,768,2048]{2,1,0:T(8,128)(2,1)S(1)}, bf16[1,768,2048]{2,1,0:T(8,128)(2,1)}, u32[]{:S(2)}) copy-start(bf16[1,768,2048]{2,1,0:T(8,128)(2,1)} %param.13) | copy-start | bytes 9437188
  2.0 34.9 %copy-start.1 = (pred[16,32]{0,1:T(8,128)(4,1)}, pred[16,32]{0,1:T(8,128)(4,1)S(1)}, u32[]{:S(2)}) copy-start(pred[16,32]{0,1:T(8,128)(4,1)S(1)} %copy.32) | copy-start | bytes 1540
  42.2 3.8 %copy-start.3 = (bf16[16,8]{0,1:T(8,128)(2,1)S(1)}, bf16[16,8]{0,1:T(8,128)(2,1)}, u32[]{:S(2)}) copy-start(bf16[16,8]{0,1:T(8,128)(2,1)} %param.11) | copy-start | bytes 772
  42.2 30.0 %all-to-all-start.1 = ((bf16[32,8,2048]{2,1,0:T(8,128)(2,1)}), bf16[32,8,2048]{2,1,0:T(8,128)(2,1)}, u32[]{:S(2)}, u32[]{:S(2)}) async-start(bf16[32,8,2048]{2,1,0:T(8,128)(2,1)} %fusion.8), calls=%async_computation.1 | async-start | bytes 2097152 | tf_op jit(solution)/shard_map/all_to_all | solution.py:78
  51.0 3.5 %copy-start.2 = (bf16[1,8192]{1,0:T(2,128)(2,1)S(1)}, bf16[1,8192]{1,0:T(2,128)(2,1)}, u32[]{:S(2)}) copy-start(bf16[1,8192]{1,0:T(2,128)(2,1)} %param.14) | copy-start | bytes 49156
where the time goes:
time: 74.8 us; the launch traced here: 74.3 us
  blocking collectives  33.4 us (45%)
  matrix products  13.4 us (18%)
  waiting for transfers between devices  10.4 us (14%)
  local copies, waits for them, and re-layouts  10.3 us (14%)
  starting transfers between devices  3.75 us (5%)
  other arithmetic  1.75 us (2%)
  between operations  1.36 us (2%)
    all_to_all x1, blocking collectives, route_experts(): lax.all_to_all(outgoing, 'expert', split_axis=0, concat_axis=0, tiled=True)  33.4 us
    all_to_all x1, waiting for transfers between devices, route_experts(): lax.all_to_all(produced.reshape(arrived.shape), 'expert', split_axis=0, c...  10.4 us
    another operation x2, local copies, waits for them, and re-layouts  7.03 us
    dot_general x1, matrix products, route_experts(): jnp.dot(hidden, expert_out[0], preferred_element_type=jnp.float32)  5.33 us
    all_to_all x1, starting transfers between devices, route_experts(): lax.all_to_all(produced.reshape(arrived.shape), 'expert', split_axis=0, c...  3.75 us
    dot_general x1, matrix products, attend_local(): jnp.einsum('skqp,spkd->skqd', weights, value_blocks, preferred_element_ty...  2.42 us
    dot_general x1, matrix products, route_experts(): jnp.dot(combine_matrix, returned.reshape(experts_here * capacity, width),...  2.17 us
    dot_general x1, matrix products, attend_local(): jnp.einsum('skqd,spkd->skqp', query_blocks, key_blocks, preferred_element...  1.94 us
  transfers between devices with their start and end apart: 1, of which 1 were waited for; matrix products, arithmetic and copies ran while one was open for 20% of the time, Pallas kernels for 0%

commit v1 on v0

--- a/solution.py
+++ b/solution.py
@@ -1,8 +1,11 @@
+import functools
 import math
 
 import jax
 import jax.numpy as jnp
 from jax import lax
+from jax.experimental import pallas as pl
+from jax.experimental.pallas import tpu as pltpu
 from jax.sharding import PartitionSpec as P
 
 KVH = 4
@@ -86,15 +89,153 @@
     return combined.astype(jnp.bfloat16)
 
 
+LANES = 128
+VMEM = pl.BlockSpec(memory_space=pltpu.VMEM)
+SMEM = pl.BlockSpec(memory_space=pltpu.SMEM)
+
+
+def attend_kernel(lengths_ref, query_ref, key_ref, value_ref, out_ref):
+    head_count = query_ref.shape[0]
+    span = key_ref.shape[0]
+    group = head_count // KVH
+    live = lax.broadcasted_iota(jnp.int32, (group, span), 1) < lengths_ref[0]
+    for k in range(KVH):
+        rows = slice(k * group, (k + 1) * group)
+        columns = slice(k * HD, (k + 1) * HD)
+        scores = lax.dot_general(
+            query_ref[rows, :],
+            key_ref[:, columns],
+            (((1,), (1,)), ((), ())),
+            preferred_element_type=jnp.float32,
+        ) * (1.0 / math.sqrt(HD))
+        masked = jnp.where(live, scores, jnp.float32(-1e30))
+        top = jnp.max(masked, axis=1, keepdims=True)
+        weights = jnp.exp(masked - top).astype(jnp.bfloat16)
+        total = jnp.sum(weights.astype(jnp.float32), axis=1, keepdims=True)
+        summed = jnp.dot(weights, value_ref[:, columns], preferred_element_type=jnp.float32)
+        out_ref[rows, :] = (summed / total).astype(out_ref.dtype)
+
+
+def attend_whole(queries, cached_keys, cached_values, lengths):
+    seq_count, width = queries.shape
+    head_count = width // HD
+    span = cached_keys.shape[1]
+    outs = []
+    for s in range(seq_count):
+        outs.append(
+            pl.pallas_call(
+                attend_kernel,
+                out_shape=jax.ShapeDtypeStruct((head_count, HD), jnp.bfloat16),
+                in_specs=[SMEM, VMEM, VMEM, VMEM],
+                out_specs=VMEM,
+                compiler_params=pltpu.CompilerParams(vmem_limit_bytes=16 << 20),
+                cost_estimate=pl.CostEstimate(
+                    flops=4 * head_count * HD * span,
+                    bytes_accessed=4 * span * KVH * HD,
+                    transcendentals=head_count * span,
+                ),
+                name="attention",
+            )(
+                lengths[s : s + 1],
+                queries[s].reshape(head_count, HD),
+                cached_keys[s],
+                cached_values[s],
+            ).reshape(1, width)
+        )
+    return jnp.concatenate(outs, axis=0) if seq_count > 1 else outs[0]
+
+
+def expert_kernel(expert_ref, rows_ref, in_ref, out_proj_ref, result_ref):
+    width = in_ref.shape[0]
+    gates = rows_ref[:, width:].astype(jnp.float32)
+    lane = lax.broadcasted_iota(jnp.int32, gates.shape, 1)
+    gate = jnp.sum(jnp.where(lane == expert_ref[0], gates, 0.0), axis=1, keepdims=True)
+    pre = jnp.dot(rows_ref[:, :width], in_ref[...], preferred_element_type=jnp.float32)
+    hidden = (pre / (1.0 + jnp.exp(-pre))).astype(jnp.bfloat16)
+    produced = jnp.dot(hidden, out_proj_ref[...], preferred_element_type=jnp.float32)
+    result_ref[...] = (produced * gate).astype(result_ref.dtype)
+
+
+def run_expert(expert, rows, expert_in, expert_out, kind):
+    count = rows.shape[0]
+    width, units = expert_in.shape
+    return pl.pallas_call(
+        expert_kernel,
+        out_shape=jax.ShapeDtypeStruct((count, width), kind),
+        in_specs=[SMEM, VMEM, VMEM, VMEM],
+        out_specs=VMEM,
+        compiler_params=pltpu.CompilerParams(vmem_limit_bytes=24 << 20),
+        cost_estimate=pl.CostEstimate(
+            flops=4 * count * width * units,
+            bytes_accessed=6 * count * width,
+            transcendentals=count * units,
+        ),
+        name="expert",
+    )(expert, rows, expert_in, expert_out)
+
+
+def swap(block, distance):
+    count = lax.axis_size("expert")
+    return lax.ppermute(block, "expert", [(i, i ^ distance) for i in range(count)])
+
+
+def route_spread(tokens, routes, gate_values, expert_in, expert_out):
+    tok_rows, width = tokens.shape
+    experts_here = lax.axis_size("expert")
+    far = [8 * k for k in range(1, experts_here // 8)]
+    near = [2, 4, 6]
+    wide = jnp.float32
+    lanes = jnp.arange(-(-experts_here // LANES) * LANES, dtype=jnp.int32)
+    chosen = routes[:, :, None] == lanes[None, None, :]
+    gates = jnp.sum(jnp.where(chosen, gate_values[:, :, None].astype(wide), 0.0), axis=1)
+    own = jnp.concatenate([tokens, gates.astype(jnp.bfloat16)], axis=1)
+    expert = lax.axis_index("expert").astype(jnp.int32).reshape(1)
+
+    column = jnp.concatenate([own] + [swap(own, d) for d in far], axis=0)
+    size = column.shape[0]
+    arrived = [column] + [swap(column, d) for d in near]
+    partial = []
+    for first in (0, 2):
+        rows = jnp.concatenate(arrived[first : first + 2], axis=0)
+        other = swap(rows, 1)
+        kept = run_expert(expert, rows, expert_in[0], expert_out[0], wide)
+        sent = run_expert(expert, other, expert_in[0], expert_out[0], jnp.bfloat16)
+        back = swap(sent, 1)
+        total = kept + back.astype(wide)
+        partial += [total[:size], total[size:]]
+    total = partial[0]
+    for block, d in zip(partial[1:], near):
+        total = total + swap(block.astype(jnp.bfloat16), d).astype(wide)
+    final = total[:tok_rows]
+    for i, d in enumerate(far):
+        block = total[(i + 1) * tok_rows : (i + 2) * tok_rows].astype(jnp.bfloat16)
+        final = final + swap(block, d).astype(wide)
+    return final.astype(jnp.bfloat16)
+
+
 def on_device(
-    tokens, routes, gate_values, expert_in, expert_out, queries, cached_keys, cached_values, lengths
+    spread,
+    tokens,
+    routes,
+    gate_values,
+    expert_in,
+    expert_out,
+    queries,
+    cached_keys,
+    cached_values,
+    lengths,
 ):
-    moe_out = route_experts(tokens, routes, gate_values, expert_in, expert_out)
-    attention_out = attend_local(queries, cached_keys, cached_values, lengths)
+    whole_cache = lax.axis_size("cuts") == 1
+    attend = attend_whole if whole_cache else attend_local
+    attention_out = attend(queries, cached_keys, cached_values, lengths)
+    route = route_spread if spread else route_experts
+    moe_out = route(tokens, routes, gate_values, expert_in, expert_out)
     return (moe_out, attention_out)
 
 
 def solution(mesh):
+    sizes = dict(mesh.shape)
+    spread = sizes["cuts"] == 1 and sizes["expert"] in (8, 16, 32)
     in_specs = (
         P(("groups", "expert", "cuts"), None),
         P(("groups", "expert", "cuts"), None),
@@ -108,5 +249,9 @@
     )
     out_specs = (P(("groups", "expert", "cuts"), None), P(("groups", "expert"), None))
     return jax.shard_map(
-        on_device, mesh=mesh, in_specs=in_specs, out_specs=out_specs, check_vma=False
-    )
+        functools.partial(on_device, spread),
+        mesh=mesh,
+        in_specs=in_specs,
+        out_specs=out_specs,
+        check_vma=False,
+    )

time: 74.8 us -> 68.1 us (0.910)
  blocking collectives: 33.4 us -> 0 us
  waiting for transfers between devices: 10.4 us -> 29.7 us
  starting transfers between devices: 3.75 us -> 17.9 us
  matrix products: 13.4 us -> 0 us
  Pallas kernels: 0 us -> 6.57 us
  local copies, waits for them, and re-layouts: 10.3 us -> 6.56 us
  other arithmetic: 1.75 us -> 5.37 us
    all_to_all x1 -> x0, blocking collectives: 33.4 us -> none  [route_experts(): lax.all_to_all(outgoing, 'expert', split_axis=0, concat_axis=0, tiled=True)]
    ppermute x0 -> x16, waiting for transfers between devices: none -> 29.7 us  [swap(): lax.ppermute(block, 'expert', [(i, i ^ distance) for i in range(count)])]
    ppermute x0 -> x16, starting transfers between devices: none -> 17.9 us  [swap(): lax.ppermute(block, 'expert', [(i, i ^ distance) for i in range(count)])]
    dot_general x6 -> x0, matrix products: 13.4 us -> none  [the longest x1 5.33 us: route_experts(): jnp.dot(hidden, expert_out[0], preferred_element_type=jnp.float32)]
    all_to_all x1 -> x0, waiting for transfers between devices: 10.4 us -> none  [route_experts(): lax.all_to_all(produced.reshape(arrived.shape), 'expert', split_axis=0, c...]
    another operation x2 -> x0, local copies, waits for them, and re-layouts: 7.03 us -> none
    pallas_call x0 -> x5, Pallas kernels: none -> 6.57 us  [the longest x4 5.09 us: run_expert(): pl.pallas_call(expert_kernel, out_shape=jax.ShapeDtypeStruct((count, widt...]
    unnamed x9 -> x16, local copies, waits for them, and re-layouts: 0.93 us -> 5.67 us
  transfers between devices with their start and end apart: 1 -> 16, of which waited for: 1 -> 9; matrix products, arithmetic and copies ran while one was open for 20% -> 3% of each run, Pallas kernels for 0% -> 10%
where the time goes in v1:
time: 68.1 us; the launch traced here: 67.6 us
  waiting for transfers between devices  29.7 us (44%)
  starting transfers between devices  17.9 us (26%)
  Pallas kernels  6.57 us (10%)
  local copies, waits for them, and re-layouts  6.56 us (10%)
  other arithmetic  5.37 us (8%)
  between operations  1.46 us (2%)
    ppermute x16, waiting for transfers between devices, swap(): lax.ppermute(block, 'expert', [(i, i ^ distance) for i in range(count)])  29.7 us
    ppermute x16, starting transfers between devices, swap(): lax.ppermute(block, 'expert', [(i, i ^ distance) for i in range(count)])  17.9 us
    unnamed x16, local copies, waits for them, and re-layouts  5.67 us
    pallas_call x4, Pallas kernels, run_expert(): pl.pallas_call(expert_kernel, out_shape=jax.ShapeDtypeStruct((count, widt...  5.09 us
    unnamed x2, other arithmetic  1.7 us
    convert_element_type x1, other arithmetic, route_spread(): return final.astype(jnp.bfloat16)  1.57 us
    pallas_call x1, Pallas kernels, attend_whole(): pl.pallas_call(attend_kernel, out_shape=jax.ShapeDtypeStruct((head_count,...  1.48 us
  transfers between devices with their start and end apart: 16, of which 9 were waited for; matrix products, arithmetic and copies ran while one was open for 3% of the time, Pallas kernels for 10%

profile of v1, /device:TPU:0, one launch (start us, length us, event | category | flops | bytes accessed | tf_op | source)
XLA Modules:
  0.0 67.6 jit_solution(9018549995372353909)
XLA Ops:
  0.6 0.8 %copy.14 = f32[16,8]{1,0:T(8,128)S(1)} copy(bf16[16,8]{0,1:T(8,128)(2,1)} %param.11) | data formatting | bytes 768 | tf_op jit(solution)/shard_map/convert_element_type | solution.py:190
  1.4 0.8 %copy.13 = s32[16,8]{1,0:T(8,128)S(1)} copy(s32[16,8]{0,1:T(8,128)} %param.10) | data formatting | bytes 1024 | tf_op args[1]
  2.1 0.1 select_reduce_fusion
  2.3 0.9 %constant_dynamic-update-slice_fusion.4 = (bf16[128,2176]{1,0:T(8,128)(2,1)S(1)}, bf16[16,2176]{1,0:T(8,128)(2,1)S(1)}) fusion(bf16[16,128]{1,0:T(8,128)(2,1)S(1)} %select_reduce_fusion, bf16[16,2048]{1,0:T(8,128)(2,1)} %param.9), kind=kLoop, calls=%fused_computation.19 | loop fusion | flops 139263 | bytes 208896
  3.1 5.1 %collective-permute-start.2 = (bf16[16,2176]{1,0:T(8,128)(2,1)S(1)}, bf16[16,2176]{1,0:T(8,128)(2,1)S(1)}, u32[]{:S(2)}, u32[]{:S(2)}) collective-permute-start(bf16[16,2176]{1,0:T(8,128)(2,1)S(1)} %get-tuple-element.10), channel_id=1, source_target_pairs={{0,24},{1,25},{2,26},{3,27},{4,28},{5,29},{6,30},{7,31},{8,16},{9,... | collective-permute-start | bytes 208904 | tf_op jit(solution)/shard_map/ppermute | solution.py:179
  8.2 0.0 collective-permute-start.1
  8.2 0.6 collective-permute-start
  8.9 2.0 %collective-permute-done.2 = bf16[16,2176]{1,0:T(8,128)(2,1)S(1)} collective-permute-done((bf16[16,2176]{1,0:T(8,128)(2,1)S(1)}, bf16[16,2176]{1,0:T(8,128)(2,1)S(1)}, u32[]{:S(2)}, u32[]{:S(2)}) %collective-permute-start.2) | collective-permute-done | bytes 69664 | tf_op jit(solution)/shard_map/ppermute | solution.py:179
  10.9 3.2 %collective-permute-done.1 = bf16[16,2176]{1,0:T(8,128)(2,1)S(1)} collective-permute-done((bf16[16,2176]{1,0:T(8,128)(2,1)S(1)}, bf16[16,2176]{1,0:T(8,128)(2,1)S(1)}, u32[]{:S(2)}, u32[]{:S(2)}) %collective-permute-start.1) | collective-permute-done | bytes 69664 | tf_op jit(solution)/shard_map/ppermute | solution.py:179
  14.1 0.9 %pad_maximum_fusion = bf16[64,2176]{1,0:T(8,128)(2,1)S(1)} fusion(bf16[16,2176]{1,0:T(8,128)(2,1)S(1)} %collective-permute-done.2, bf16[16,2176]{1,0:T(8,128)(2,1)S(1)} %collective-permute-done.1, bf16[16,2176]{1,0:T(8,128)(2,1)S(1)} %collective-permute-done, bf16[16,128]{1,0:T(8,128)(2,1)S(1)} %select_reduce_fusion, bf16[16,2048]{1,0:T(8,128)(2,1)} %param.9), kind=kLoop, calls=%fused_computation.6 | loop fusion | flops 1392640 | bytes 557056 | tf_op jit(solution)/shard_map/concatenate | solution.py:194
  15.0 1.6 %collective-permute-start.7 = (bf16[64,2176]{1,0:T(8,128)(2,1)S(1)}, bf16[64,2176]{1,0:T(8,128)(2,1)S(1)}, u32[]{:S(2)}, u32[]{:S(2)}) collective-permute-start(bf16[64,2176]{1,0:T(8,128)(2,1)S(1)} %pad_maximum_fusion), channel_id=1, source_target_pairs={{0,4},{1,5},{2,6},{3,7},{4,0},{5,1},{6,2},{7,3},{8,12},{9,13},{10,... | collective-permute-start | bytes 835592 | tf_op jit(solution)/shard_map/ppermute | solution.py:179
  16.6 1.4 %collective-permute-start.8 = (bf16[64,2176]{1,0:T(8,128)(2,1)S(1)}, bf16[64,2176]{1,0:T(8,128)(2,1)S(1)}, u32[]{:S(2)}, u32[]{:S(2)}) collective-permute-start(bf16[64,2176]{1,0:T(8,128)(2,1)S(1)} %pad_maximum_fusion), channel_id=1, source_target_pairs={{0,6},{1,7},{2,4},{3,5},{4,2},{5,3},{6,0},{7,1},{8,14},{9,15},{10,... | collective-permute-start | bytes 835592 | tf_op jit(solution)/shard_map/ppermute | solution.py:179
  18.0 0.5 collective-permute-start.3
  18.6 10.6 %collective-permute-done.7 = bf16[64,2176]{1,0:T(8,128)(2,1)S(1)} collective-permute-done((bf16[64,2176]{1,0:T(8,128)(2,1)S(1)}, bf16[64,2176]{1,0:T(8,128)(2,1)S(1)}, u32[]{:S(2)}, u32[]{:S(2)}) %collective-permute-start.7) | collective-permute-done | bytes 278560 | tf_op jit(solution)/shard_map/ppermute | solution.py:179
  29.3 0.1 collective-permute-start.9
  29.4 1.1 %collective-permute-done.3 = bf16[64,2176]{1,0:T(8,128)(2,1)S(1)} collective-permute-done((bf16[64,2176]{1,0:T(8,128)(2,1)S(1)}, bf16[64,2176]{1,0:T(8,128)(2,1)S(1)}, u32[]{:S(2)}, u32[]{:S(2)}) %collective-permute-start.3) | collective-permute-done | bytes 278560 | tf_op jit(solution)/shard_map/ppermute | solution.py:179
  30.5 0.1 collective-permute-start.4
  30.6 0.7 %collective-permute-done.9.rows_ref = bf16[128,2176]{1,0:T(8,128)(2,1)S(1)} collective-permute-done((bf16[128,2176]{1,0:T(8,128)(2,1)S(1)}, bf16[128,2176]{1,0:T(8,128)(2,1)S(1)}, u32[]{:S(2)}, u32[]{:S(2)}) %collective-permute-start.9) | collective-permute-done | bytes 557088 | tf_op jit(solution)/shard_map/ppermute | solution.py:179
  31.3 1.9 %copy-done = bf16[1,2048,768]{2,1,0:T(8,128)(2,1)S(1)} copy-done((bf16[1,2048,768]{2,1,0:T(8,128)(2,1)S(1)}, bf16[1,2048,768]{2,1,0:T(8,128)(2,1)}, u32[]{:S(2)}) %copy-start) | copy-done | bytes 3145752
  33.2 1.9 %copy-done.2 = bf16[1,768,2048]{2,1,0:T(8,128)(2,1)S(1)} copy-done((bf16[1,768,2048]{2,1,0:T(8,128)(2,1)S(1)}, bf16[1,768,2048]{2,1,0:T(8,128)(2,1)}, u32[]{:S(2)}) %copy-start.2) | copy-done | bytes 3145752
  35.1 1.3 %expert.7 = bf16[128,2048]{1,0:T(8,128)(2,1)S(1)} custom-call(s32[1]{0:T(128)} %bitcast.expert_ref, bf16[128,2176]{1,0:T(8,128)(2,1)S(1)} %collective-permute-done.9.rows_ref, bf16[2048,768]{1,0:T(8,128)(2,1)S(1)} %bitcast.11, bf16[768,2048]{1,0:T(8,128)(2,1)S(1)} %bitcast.15), custom_call_target="tpu_custom_call" | custom-call | flops 805306368 | bytes 1572864 | tf_op jit(solution)/shard_map/expert/pallas_call | solution.py:162
  36.3 0.2 collective-permute-start.10
  36.5 0.4 copy-done.1
  37.0 1.3 %expert.6 = f32[128,2048]{1,0:T(8,128)S(1)} custom-call(s32[1]{0:T(128)} %bitcast.expert_ref, bf16[128,2176]{1,0:T(8,128)(2,1)S(1)} %constant_dynamic-update-slice_fusion.5.rows_ref, bf16[2048,768]{1,0:T(8,128)(2,1)S(1)} %bitcast.12, bf16[768,2048]{1,0:T(8,128)(2,1)S(1)} %bitcast.16), custom_call_target="tpu_custom_call" | custom-call | flops 805306368 | bytes 1572864 | tf_op jit(solution)/shard_map/expert/pallas_call | solution.py:162
  38.2 1.3 %expert.4 = f32[128,2048]{1,0:T(8,128)S(1)} custom-call(s32[1]{0:T(128)} %bitcast.expert_ref, bf16[128,2176]{1,0:T(8,128)(2,1)S(1)} %constant_dynamic-update-slice_fusion.rows_ref, bf16[2048,768]{1,0:T(8,128)(2,1)S(1)} %bitcast.13, bf16[768,2048]{1,0:T(8,128)(2,1)S(1)} %bitcast.17), custom_call_target="tpu_custom_call" | custom-call | flops 805306368 | bytes 1572864 | tf_op jit(solution)/shard_map/expert/pallas_call | solution.py:162
  39.5 0.0 collective-permute-done.4.rows_ref
  39.5 1.3 %expert.5 = bf16[128,2048]{1,0:T(8,128)(2,1)S(1)} custom-call(s32[1]{0:T(128)} %bitcast.expert_ref, bf16[128,2176]{1,0:T(8,128)(2,1)S(1)} %collective-permute-done.4.rows_ref, bf16[2048,768]{1,0:T(8,128)(2,1)S(1)} %bitcast.14, bf16[768,2048]{1,0:T(8,128)(2,1)S(1)} %bitcast.18), custom_call_target="tpu_custom_call" | custom-call | flops 805306368 | bytes 1572864 | tf_op jit(solution)/shard_map/expert/pallas_call | solution.py:162
  40.8 0.2 collective-permute-start.5
  41.0 0.1 add_convert_fusion
  41.1 0.0 copy-start.3
  41.1 0.0 copy-start.4
  41.2 2.7 %collective-permute-start.12 = (bf16[64,2048]{1,0:T(8,128)(2,1)S(1)}, bf16[64,2048]{1,0:T(8,128)(2,1)S(1)}, u32[]{:S(2)}, u32[]{:S(2)}) collective-permute-start(bf16[64,2048]{1,0:T(8,128)(2,1)S(1)} %get-tuple-element.5), channel_id=1, source_target_pairs={{0,6},{1,7},{2,4},{3,5},{4,2},{5,3},{6,0},{7,1},{8,14},{9,15},{10,... | collective-permute-start | bytes 786440 | tf_op jit(solution)/shard_map/ppermute | solution.py:179
  43.9 0.5 collective-permute-start.11
  44.4 0.1 convert_add_fusion
  44.6 0.4 collective-permute-start.6
  45.0 6.4 %collective-permute-done.12 = bf16[64,2048]{1,0:T(8,128)(2,1)S(1)} collective-permute-done((bf16[64,2048]{1,0:T(8,128)(2,1)S(1)}, bf16[64,2048]{1,0:T(8,128)(2,1)S(1)}, u32[]{:S(2)}, u32[]{:S(2)}) %collective-permute-start.12) | collective-permute-done | bytes 262176 | tf_op jit(solution)/shard_map/ppermute | solution.py:179
  51.3 5.1 %collective-permute-done.11 = bf16[64,2048]{1,0:T(8,128)(2,1)S(1)} collective-permute-done((bf16[64,2048]{1,0:T(8,128)(2,1)S(1)}, bf16[64,2048]{1,0:T(8,128)(2,1)S(1)}, u32[]{:S(2)}, u32[]{:S(2)}) %collective-permute-start.11) | collective-permute-done | bytes 262176 | tf_op jit(solution)/shard_map/ppermute | solution.py:179
  56.4 0.3 collective-permute-done.6
  56.7 0.9 %fusion.5 = (bf16[64,2048]{1,0:T(8,128)(2,1)S(1)}, f32[64,2048]{1,0:T(8,128)}) fusion(bf16[64,2048]{1,0:T(8,128)(2,1)S(1)} %collective-permute-done.12, bf16[64,2048]{1,0:T(8,128)(2,1)S(1)} %collective-permute-done.11, bf16[64,2048]{1,0:T(8,128)(2,1)S(1)} %collective-permute-done.6, f32[128,2048]{1,0:T(8,128)S(1)} %convert_add_fusion), kind=kLoop, calls=%fused_computation.22 | loop fusion | flops 917504 | bytes 2097152 | tf_op jit(solution)/shard_map/convert.2
  57.6 1.5 %collective-permute-start.15 = (bf16[16,2048]{1,0:T(8,128)(2,1)S(1)}, bf16[16,2048]{1,0:T(8,128)(2,1)S(1)}, u32[]{:S(2)}, u32[]{:S(2)}) collective-permute-start(bf16[16,2048]{1,0:T(8,128)(2,1)S(1)} %get-tuple-element.7), channel_id=1, source_target_pairs={{0,24},{1,25},{2,26},{3,27},{4,28},{5,29},{6,30},{7,31},{8,16},{9,... | collective-permute-start | bytes 196616 | tf_op jit(solution)/shard_map/ppermute | solution.py:179
  59.1 3.0 %collective-permute-start.13 = (bf16[16,2048]{1,0:T(8,128)(2,1)S(1)}, bf16[16,2048]{1,0:T(8,128)(2,1)S(1)}, u32[]{:S(2)}, u32[]{:S(2)}) collective-permute-start(bf16[16,2048]{1,0:T(8,128)(2,1)S(1)} %get-tuple-element.6), channel_id=1, source_target_pairs={{0,8},{1,9},{2,10},{3,11},{4,12},{5,13},{6,14},{7,15},{8,0},{9,1},... | collective-permute-start | bytes 196616 | tf_op jit(solution)/shard_map/ppermute | solution.py:179
  62.7 0.8 %reduce = bf16[8192]{0:T(1024)(128)(2,1)S(1)} reduce(bf16[1,8192]{1,0:T(2,128)(2,1)} %param.14, bf16[]{:T(256)} %constant.15), dimensions={0}, to_apply=%param.14.reduce_sub_computation | reduce | bytes 32770 | tf_op args[5]
  63.6 1.5 %attention.1 = bf16[64,128]{1,0:T(8,128)(2,1)S(1)} custom-call(s32[1]{0:T(128)S(6)} %copy.23.lengths_ref, bf16[64,128]{1,0:T(8,128)(2,1)S(1)} %bitcast.21, bf16[1536,512]{1,0:T(8,128)(2,1)S(1)} %bitcast.19, bf16[1536,512]{1,0:T(8,128)(2,1)S(1)} %bitcast.20), custom_call_target="tpu_custom_call" | custom-call | flops 50331648 | bytes 3145728 | tf_op jit(solution)/shard_map/attention/pallas_call | solution.py:126
  65.1 0.7 copy.17
  65.7 0.0 collective-permute-done.15
  65.7 0.3 collective-permute-done.14
  66.0 0.0 collective-permute-done.13
  66.0 1.6 %fusion.4 = bf16[16,2048]{1,0:T(8,128)(2,1)} fusion(f32[64,2048]{1,0:T(8,128)} %get-tuple-element.3, bf16[16,2048]{1,0:T(8,128)(2,1)S(1)} %collective-permute-done.15, bf16[16,2048]{1,0:T(8,128)(2,1)S(1)} %collective-permute-done.14, bf16[16,2048]{1,0:T(8,128)(2,1)S(1)} %collective-permute-done.13), kind=kLoop, calls=%fused_computation.10 | loop fusion | flops 229376 | bytes 393216 | tf_op jit(solution)/shard_map/convert_element_type | solution.py:213
  (19 shorter events, 0.2 us)
Async XLA Ops:
  3.1 7.8 %collective-permute-start.2 = (bf16[16,2176]{1,0:T(8,128)(2,1)S(1)}, bf16[16,2176]{1,0:T(8,128)(2,1)S(1)}, u32[]{:S(2)}, u32[]{:S(2)}) collective-permute-start(bf16[16,2176]{1,0:T(8,128)(2,1)S(1)} %get-tuple-element.10), channel_id=1, source_target_pairs={{0,24},{1,25},{2,26},{3,27},{4,28},{5,29},{6,30},{7,31},{8,16},{9,... | collective-permute-start | bytes 208904 | tf_op jit(solution)/shard_map/ppermute | solution.py:179
  8.2 5.9 %collective-permute-start.1 = (bf16[16,2176]{1,0:T(8,128)(2,1)S(1)}, bf16[16,2176]{1,0:T(8,128)(2,1)S(1)}, u32[]{:S(2)}, u32[]{:S(2)}) collective-permute-start(bf16[16,2176]{1,0:T(8,128)(2,1)S(1)} %get-tuple-element.10), channel_id=1, source_target_pairs={{0,16},{1,17},{2,18},{3,19},{4,20},{5,21},{6,22},{7,23},{8,24},{9,... | collective-permute-start | bytes 208904 | tf_op jit(solution)/shard_map/ppermute | solution.py:179
  8.2 5.9 %collective-permute-start = (bf16[16,2176]{1,0:T(8,128)(2,1)S(1)}, bf16[16,2176]{1,0:T(8,128)(2,1)S(1)}, u32[]{:S(2)}, u32[]{:S(2)}) collective-permute-start(bf16[16,2176]{1,0:T(8,128)(2,1)S(1)} %get-tuple-element.10), channel_id=1, source_target_pairs={{0,8},{1,9},{2,10},{3,11},{4,12},{5,13},{6,14},{7,15},{8,0},{9,1},... | collective-permute-start | bytes 208904 | tf_op jit(solution)/shard_map/ppermute | solution.py:179
  15.0 14.2 %collective-permute-start.7 = (bf16[64,2176]{1,0:T(8,128)(2,1)S(1)}, bf16[64,2176]{1,0:T(8,128)(2,1)S(1)}, u32[]{:S(2)}, u32[]{:S(2)}) collective-permute-start(bf16[64,2176]{1,0:T(8,128)(2,1)S(1)} %pad_maximum_fusion), channel_id=1, source_target_pairs={{0,4},{1,5},{2,6},{3,7},{4,0},{5,1},{6,2},{7,3},{8,12},{9,13},{10,... | collective-permute-start | bytes 835592 | tf_op jit(solution)/shard_map/ppermute | solution.py:179
  16.6 12.6 %collective-permute-start.8 = (bf16[64,2176]{1,0:T(8,128)(2,1)S(1)}, bf16[64,2176]{1,0:T(8,128)(2,1)S(1)}, u32[]{:S(2)}, u32[]{:S(2)}) collective-permute-start(bf16[64,2176]{1,0:T(8,128)(2,1)S(1)} %pad_maximum_fusion), channel_id=1, source_target_pairs={{0,6},{1,7},{2,4},{3,5},{4,2},{5,3},{6,0},{7,1},{8,14},{9,15},{10,... | collective-permute-start | bytes 835592 | tf_op jit(solution)/shard_map/ppermute | solution.py:179
  18.0 12.5 %collective-permute-start.3 = (bf16[64,2176]{1,0:T(8,128)(2,1)S(1)}, bf16[64,2176]{1,0:T(8,128)(2,1)S(1)}, u32[]{:S(2)}, u32[]{:S(2)}) collective-permute-start(bf16[64,2176]{1,0:T(8,128)(2,1)S(1)} %pad_maximum_fusion), channel_id=1, source_target_pairs={{0,2},{1,3},{2,0},{3,1},{4,6},{5,7},{6,4},{7,5},{8,10},{9,11},{10,... | collective-permute-start | bytes 835592 | tf_op jit(solution)/shard_map/ppermute | solution.py:179
  29.3 2.0 %collective-permute-start.9 = (bf16[128,2176]{1,0:T(8,128)(2,1)S(1)}, bf16[128,2176]{1,0:T(8,128)(2,1)S(1)}, u32[]{:S(2)}, u32[]{:S(2)}) collective-permute-start(bf16[128,2176]{1,0:T(8,128)(2,1)S(1)} %constant_dynamic-update-slice_fusion.5.rows_ref), channel_id=1, source_target_pairs={{0,1},{1,0},{2,3},{3,2},{4,5},{5,4},{6,7},{7,6},{8,9},{9,8},{10,11... | collective-permute-start | bytes 1671176 | tf_op jit(solution)/shard_map/ppermute | solution.py:179
  30.5 9.0 %collective-permute-start.4 = (bf16[128,2176]{1,0:T(8,128)(2,1)S(1)}, bf16[128,2176]{1,0:T(8,128)(2,1)S(1)}, u32[]{:S(2)}, u32[]{:S(2)}) collective-permute-start(bf16[128,2176]{1,0:T(8,128)(2,1)S(1)} %constant_dynamic-update-slice_fusion.rows_ref), channel_id=1, source_target_pairs={{0,1},{1,0},{2,3},{3,2},{4,5},{5,4},{6,7},{7,6},{8,9},{9,8},{10,11... | collective-permute-start | bytes 1671176 | tf_op jit(solution)/shard_map/ppermute | solution.py:179
  31.3 1.9 %copy-start = (bf16[1,2048,768]{2,1,0:T(8,128)(2,1)S(1)}, bf16[1,2048,768]{2,1,0:T(8,128)(2,1)}, u32[]{:S(2)}) copy-start(bf16[1,2048,768]{2,1,0:T(8,128)(2,1)} %param.12) | copy-start | bytes 9437188
  33.2 1.9 %copy-start.2 = (bf16[1,768,2048]{2,1,0:T(8,128)(2,1)S(1)}, bf16[1,768,2048]{2,1,0:T(8,128)(2,1)}, u32[]{:S(2)}) copy-start(bf16[1,768,2048]{2,1,0:T(8,128)(2,1)} %param.13) | copy-start | bytes 9437188
  35.1 1.9 %copy-start.1 = (bf16[1,2048,768]{2,1,0:T(8,128)(2,1)S(1)}, bf16[1,2048,768]{2,1,0:T(8,128)(2,1)}, u32[]{:S(2)}) copy-start(bf16[1,2048,768]{2,1,0:T(8,128)(2,1)} %param.12) | copy-start | bytes 9437188
  36.3 4.7 %collective-permute-start.10 = (bf16[128,2048]{1,0:T(8,128)(2,1)S(1)}, bf16[128,2048]{1,0:T(8,128)(2,1)S(1)}, u32[]{:S(2)}, u32[]{:S(2)}) collective-permute-start(bf16[128,2048]{1,0:T(8,128)(2,1)S(1)} %expert.7), channel_id=1, source_target_pairs={{0,1},{1,0},{2,3},{3,2},{4,5},{5,4},{6,7},{7,6},{8,9},{9,8},{10,11... | collective-permute-start | bytes 1572872 | tf_op jit(solution)/shard_map/ppermute | solution.py:179
  40.8 3.6 %collective-permute-start.5 = (bf16[128,2048]{1,0:T(8,128)(2,1)S(1)}, bf16[128,2048]{1,0:T(8,128)(2,1)S(1)}, u32[]{:S(2)}, u32[]{:S(2)}) collective-permute-start(bf16[128,2048]{1,0:T(8,128)(2,1)S(1)} %expert.5), channel_id=1, source_target_pairs={{0,1},{1,0},{2,3},{3,2},{4,5},{5,4},{6,7},{7,6},{8,9},{9,8},{10,11... | collective-permute-start | bytes 1572872 | tf_op jit(solution)/shard_map/ppermute | solution.py:179
  41.1 22.5 %copy-start.3 = (bf16[1,1536,512]{2,1,0:T(8,128)(2,1)S(1)}, bf16[1,1536,512]{2,1,0:T(8,128)(2,1)}, u32[]{:S(2)}) copy-start(bf16[1,1536,512]{2,1,0:T(8,128)(2,1)} %param.15) | copy-start | bytes 4718596
  41.1 22.4 %copy-start.4 = (bf16[1,1536,512]{2,1,0:T(8,128)(2,1)S(1)}, bf16[1,1536,512]{2,1,0:T(8,128)(2,1)}, u32[]{:S(2)}) copy-start(bf16[1,1536,512]{2,1,0:T(8,128)(2,1)} %param.16) | copy-start | bytes 4718596
  41.2 10.1 %collective-permute-start.12 = (bf16[64,2048]{1,0:T(8,128)(2,1)S(1)}, bf16[64,2048]{1,0:T(8,128)(2,1)S(1)}, u32[]{:S(2)}, u32[]{:S(2)}) collective-permute-start(bf16[64,2048]{1,0:T(8,128)(2,1)S(1)} %get-tuple-element.5), channel_id=1, source_target_pairs={{0,6},{1,7},{2,4},{3,5},{4,2},{5,3},{6,0},{7,1},{8,14},{9,15},{10,... | collective-permute-start | bytes 786440 | tf_op jit(solution)/shard_map/ppermute | solution.py:179
  43.9 12.4 %collective-permute-start.11 = (bf16[64,2048]{1,0:T(8,128)(2,1)S(1)}, bf16[64,2048]{1,0:T(8,128)(2,1)S(1)}, u32[]{:S(2)}, u32[]{:S(2)}) collective-permute-start(bf16[64,2048]{1,0:T(8,128)(2,1)S(1)} %get-tuple-element.4), channel_id=1, source_target_pairs={{0,4},{1,5},{2,6},{3,7},{4,0},{5,1},{6,2},{7,3},{8,12},{9,13},{10,... | collective-permute-start | bytes 786440 | tf_op jit(solution)/shard_map/ppermute | solution.py:179
  44.6 12.1 %collective-permute-start.6 = (bf16[64,2048]{1,0:T(8,128)(2,1)S(1)}, bf16[64,2048]{1,0:T(8,128)(2,1)S(1)}, u32[]{:S(2)}, u32[]{:S(2)}) collective-permute-start(bf16[64,2048]{1,0:T(8,128)(2,1)S(1)} %slice.59), channel_id=1, source_target_pairs={{0,2},{1,3},{2,0},{3,1},{4,6},{5,7},{6,4},{7,5},{8,10},{9,11},{10,... | collective-permute-start | bytes 786440 | tf_op jit(solution)/shard_map/ppermute | solution.py:179
  57.6 8.1 %collective-permute-start.15 = (bf16[16,2048]{1,0:T(8,128)(2,1)S(1)}, bf16[16,2048]{1,0:T(8,128)(2,1)S(1)}, u32[]{:S(2)}, u32[]{:S(2)}) collective-permute-start(bf16[16,2048]{1,0:T(8,128)(2,1)S(1)} %get-tuple-element.7), channel_id=1, source_target_pairs={{0,24},{1,25},{2,26},{3,27},{4,28},{5,29},{6,30},{7,31},{8,16},{9,... | collective-permute-start | bytes 196616 | tf_op jit(solution)/shard_map/ppermute | solution.py:179
  59.1 6.9 %collective-permute-start.14 = (bf16[16,2048]{1,0:T(8,128)(2,1)S(1)}, bf16[16,2048]{1,0:T(8,128)(2,1)S(1)}, u32[]{:S(2)}, u32[]{:S(2)}) collective-permute-start(bf16[16,2048]{1,0:T(8,128)(2,1)S(1)} %get-tuple-element.8), channel_id=1, source_target_pairs={{0,16},{1,17},{2,18},{3,19},{4,20},{5,21},{6,22},{7,23},{8,24},{9,... | collective-permute-start | bytes 196616 | tf_op jit(solution)/shard_map/ppermute | solution.py:179
  59.1 6.9 %collective-permute-start.13 = (bf16[16,2048]{1,0:T(8,128)(2,1)S(1)}, bf16[16,2048]{1,0:T(8,128)(2,1)S(1)}, u32[]{:S(2)}, u32[]{:S(2)}) collective-permute-start(bf16[16,2048]{1,0:T(8,128)(2,1)S(1)} %get-tuple-element.6), channel_id=1, source_target_pairs={{0,8},{1,9},{2,10},{3,11},{4,12},{5,13},{6,14},{7,15},{8,0},{9,1},... | collective-permute-start | bytes 196616 | tf_op jit(solution)/shard_map/ppermute | solution.py:179

commit v2 on v0

--- a/solution.py
+++ b/solution.py
@@ -1,8 +1,11 @@
+import functools
 import math
 
 import jax
 import jax.numpy as jnp
 from jax import lax
+from jax.experimental import pallas as pl
+from jax.experimental.pallas import tpu as pltpu
 from jax.sharding import PartitionSpec as P
 
 KVH = 4
@@ -86,6 +89,241 @@
     return combined.astype(jnp.bfloat16)
 
 
+LANES = 128
+VMEM = pl.BlockSpec(memory_space=pltpu.VMEM)
+SMEM = pl.BlockSpec(memory_space=pltpu.SMEM)
+ANYWHERE = pl.BlockSpec(memory_space=pl.ANY)
+HBM = pl.BlockSpec(memory_space=pltpu.HBM)
+
+
+def far_off(x):
+    return pltpu.with_memory_space_constraint(x, pltpu.HBM)
+
+
+def label_kernel(tokens_hbm, routes_hbm, gates_hbm, own_ref, routes_ref, gates_ref, sems):
+    tok_rows, width = tokens_hbm.shape
+    lanes = own_ref.shape[1] - width
+    copies = [
+        pltpu.make_async_copy(tokens_hbm, own_ref.at[:, pl.ds(0, width)], sems.at[0]),
+        pltpu.make_async_copy(routes_hbm, routes_ref, sems.at[1]),
+        pltpu.make_async_copy(gates_hbm, gates_ref, sems.at[2]),
+    ]
+    for copy in copies:
+        copy.start()
+    copies[1].wait()
+    copies[2].wait()
+    routes = routes_ref[...]
+    gates = gates_ref[...].astype(jnp.float32)
+    ids = lax.broadcasted_iota(jnp.int32, (lanes, tok_rows), 0)
+    spread = jnp.zeros((lanes, tok_rows), jnp.float32)
+    for k in range(routes.shape[0]):
+        spread += jnp.where(ids == routes[k : k + 1, :], gates[k : k + 1, :], 0.0)
+    places = (tok_rows, tok_rows)
+    same = lax.broadcasted_iota(jnp.int32, places, 0) == lax.broadcasted_iota(jnp.int32, places, 1)
+    turned = lax.dot_general(
+        same.astype(jnp.bfloat16),
+        spread.astype(jnp.bfloat16),
+        (((1,), (1,)), ((), ())),
+        preferred_element_type=jnp.float32,
+    )
+    own_ref[:, width:] = turned.astype(own_ref.dtype)
+    copies[0].wait()
+
+
+def label_tokens(tokens, routes, gate_values, experts):
+    tok_rows, width = tokens.shape
+    lanes = -(-experts // LANES) * LANES
+    return pl.pallas_call(
+        label_kernel,
+        out_shape=jax.ShapeDtypeStruct((tok_rows, width + lanes), jnp.bfloat16),
+        in_specs=[HBM] * 3,
+        out_specs=VMEM,
+        scratch_shapes=[
+            pltpu.VMEM(routes.shape[::-1], routes.dtype),
+            pltpu.VMEM(gate_values.shape[::-1], gate_values.dtype),
+            pltpu.SemaphoreType.DMA((3,)),
+        ],
+        compiler_params=pltpu.CompilerParams(vmem_limit_bytes=4 << 20),
+        name="label",
+    )(far_off(tokens), far_off(routes.T), far_off(gate_values.T))
+
+
+def attend_kernel(
+    lengths_ref, query_ref, key_hbm, value_hbm, in_hbm, proj_hbm, out_ref, in_ref, proj_ref,
+    key_ref, value_ref, sems
+):
+    pairs = ((key_hbm, key_ref), (value_hbm, value_ref), (in_hbm, in_ref), (proj_hbm, proj_ref))
+    copies = [pltpu.make_async_copy(a, b, sems.at[i]) for i, (a, b) in enumerate(pairs)]
+    for copy in copies:
+        copy.start()
+    head_count = query_ref.shape[1] // HD
+    span = key_ref.shape[0]
+    group = head_count // KVH
+    query = query_ref[...].astype(jnp.float32)
+    heads = [query[:, i * HD : (i + 1) * HD] for i in range(head_count)]
+    live = lax.broadcasted_iota(jnp.int32, (group, span), 1) < lengths_ref[0]
+    copies[0].wait()
+    for k in range(KVH):
+        rows = slice(k * group, (k + 1) * group)
+        columns = slice(k * HD, (k + 1) * HD)
+        scores = lax.dot_general(
+            jnp.concatenate(heads[rows], axis=0).astype(jnp.bfloat16),
+            key_ref[:, columns],
+            (((1,), (1,)), ((), ())),
+            preferred_element_type=jnp.float32,
+        ) * (1.0 / math.sqrt(HD))
+        masked = jnp.where(live, scores, jnp.float32(-1e30))
+        top = jnp.max(masked, axis=1, keepdims=True)
+        weights = jnp.exp(masked - top).astype(jnp.bfloat16)
+        total = jnp.sum(weights.astype(jnp.float32), axis=1, keepdims=True)
+        if k == 0:
+            copies[1].wait()
+        summed = jnp.dot(weights, value_ref[:, columns], preferred_element_type=jnp.float32)
+        out_ref[rows, :] = (summed / total).astype(out_ref.dtype)
+    copies[2].wait()
+    copies[3].wait()
+
+
+def attend_and_fetch(queries, cached_keys, cached_values, lengths, expert_in, expert_out):
+    width = queries.shape[1]
+    head_count = width // HD
+    span = cached_keys.shape[1]
+    attended, near_in, near_out = pl.pallas_call(
+        attend_kernel,
+        out_shape=[
+            jax.ShapeDtypeStruct((head_count, HD), jnp.bfloat16),
+            pltpu.VMEM(expert_in.shape[1:], jnp.bfloat16),
+            pltpu.VMEM(expert_out.shape[1:], jnp.bfloat16),
+        ],
+        in_specs=[SMEM, VMEM] + [HBM] * 4,
+        out_specs=[VMEM] * 3,
+        scratch_shapes=[
+            pltpu.VMEM(cached_keys.shape[1:], jnp.bfloat16),
+            pltpu.VMEM(cached_values.shape[1:], jnp.bfloat16),
+            pltpu.SemaphoreType.DMA((4,)),
+        ],
+        compiler_params=pltpu.CompilerParams(vmem_limit_bytes=14 << 20),
+        cost_estimate=pl.CostEstimate(
+            flops=4 * head_count * HD * span,
+            bytes_accessed=4 * span * KVH * HD + 4 * expert_in.size + 4 * expert_out.size,
+            transcendentals=head_count * span,
+        ),
+        name="attention",
+    )(
+        lengths,
+        queries,
+        *(far_off(a[0]) for a in (cached_keys, cached_values, expert_in, expert_out)),
+    )
+    return attended, near_in, near_out
+
+
+def stack_kernel(*refs):
+    parts, out_ref = refs[:-2], refs[-1]
+    size = parts[0].shape[0]
+    for i, part in enumerate(parts):
+        out_ref[i * size : (i + 1) * size, :] = part[...]
+
+
+def stack_rows(parts, after):
+    size, width = parts[0].shape
+    return pl.pallas_call(
+        stack_kernel,
+        out_shape=jax.ShapeDtypeStruct((size * len(parts), width), parts[0].dtype),
+        in_specs=[VMEM] * len(parts) + [ANYWHERE],
+        out_specs=VMEM,
+        compiler_params=pltpu.CompilerParams(vmem_limit_bytes=4 << 20),
+        name="stack",
+    )(*parts, after)
+
+
+def expert_kernel(part_count, *refs):
+    parts, (in_ref, proj_ref), results = (
+        refs[:part_count], refs[part_count : part_count + 2], refs[part_count + 2 :]
+    )
+    width = in_ref.shape[0]
+    rows = jnp.concatenate([part[:, :width] for part in parts], axis=0)
+    gates = jnp.concatenate([part[:, width:] for part in parts], axis=0).astype(jnp.float32)
+    lane = lax.broadcasted_iota(jnp.int32, gates.shape, 1)
+    gate = jnp.sum(jnp.where(lane == lax.axis_index("expert"), gates, 0.0), axis=1, keepdims=True)
+    pre = jnp.dot(rows, in_ref[...], preferred_element_type=jnp.float32)
+    hidden = (pre / (1.0 + jnp.exp(-pre))).astype(jnp.bfloat16)
+    produced = jnp.dot(hidden, proj_ref[...], preferred_element_type=jnp.float32) * gate
+    first = 0
+    for result in results:
+        size = result.shape[0]
+        result[...] = produced[first : first + size].astype(result.dtype)
+        first += size
+
+
+def run_expert(parts, near_in, near_out, results):
+    count = sum(part.shape[0] for part in parts)
+    width, units = near_in.shape
+    return pl.pallas_call(
+        functools.partial(expert_kernel, len(parts)),
+        out_shape=[jax.ShapeDtypeStruct((size, width), kind) for size, kind in results],
+        in_specs=[VMEM] * (len(parts) + 2),
+        out_specs=[VMEM] * len(results),
+        compiler_params=pltpu.CompilerParams(vmem_limit_bytes=14 << 20),
+        cost_estimate=pl.CostEstimate(
+            flops=4 * count * width * units,
+            bytes_accessed=6 * count * width,
+            transcendentals=count * units,
+        ),
+        name="expert",
+    )(*parts, hold(near_in), hold(near_out))
+
+
+def hold(x):
+    return pltpu.with_memory_space_constraint(x, pltpu.VMEM)
+
+
+def swap(block, distance):
+    count = lax.axis_size("expert")
+    return lax.ppermute(block, "expert", [(i, i ^ distance) for i in range(count)])
+
+
+def spread_step(
+    tokens, routes, gate_values, expert_in, expert_out, queries, cached_keys, cached_values, lengths
+):
+    tok_rows = tokens.shape[0]
+    experts_here = lax.axis_size("expert")
+    far = [8 * k for k in range(1, experts_here // 8)]
+    wide, half = jnp.float32, jnp.bfloat16
+    own = label_tokens(tokens, routes, gate_values, experts_here)
+    arrived = [swap(own, d) for d in far]
+    attended, near_in, near_out = attend_and_fetch(
+        queries, cached_keys, cached_values, lengths, expert_in, expert_out
+    )
+    column = stack_rows([own] + arrived, attended)
+    size = column.shape[0]
+    mid = size // 2
+
+    def gated(parts, results):
+        return run_expert(parts, near_in, near_out, results)
+
+    by_x, by_y = swap(column, 2), swap(column, 4)
+    pair = swap(column, 1)
+    kept_own, sent_own = gated([column, pair], [(size, wide), (size, half)])
+    back_own = swap(sent_own, 1)
+    corner = [swap(by_y[:mid], 2), swap(by_x[mid:], 4)]
+    pair_x, pair_y = swap(by_x, 1), swap(by_y, 1)
+    kept_x, kept_y = gated([by_x, by_y], [(size, wide)] * 2)
+    sent_x, sent_y = gated([pair_x, pair_y], [(size, half)] * 2)
+    back_x, back_y = swap(sent_x, 1), swap(sent_y, 1)
+    pair_corner = [swap(part, 1) for part in corner]
+    kept_corner, sent_corner = gated(corner + pair_corner, [(size, wide), (size, half)])
+    back_corner = swap(sent_corner, 1)
+
+    total = kept_own + back_own.astype(wide)
+    for kept, back, d in ((kept_x, back_x, 2), (kept_y, back_y, 4), (kept_corner, back_corner, 6)):
+        total = total + swap((kept + back.astype(wide)).astype(half), d).astype(wide)
+    final = total[:tok_rows]
+    for i, d in enumerate(far):
+        block = total[(i + 1) * tok_rows : (i + 2) * tok_rows].astype(half)
+        final = final + swap(block, d).astype(wide)
+    return final.astype(half), attended.reshape(queries.shape)
+
+
 def on_device(
     tokens, routes, gate_values, expert_in, expert_out, queries, cached_keys, cached_values, lengths
 ):
@@ -95,6 +333,8 @@
 
 
 def solution(mesh):
+    sizes = dict(mesh.shape)
+    spread = sizes["cuts"] == 1 and sizes["expert"] in (8, 16, 32)
     in_specs = (
         P(("groups", "expert", "cuts"), None),
         P(("groups", "expert", "cuts"), None),
@@ -108,5 +348,9 @@
     )
     out_specs = (P(("groups", "expert", "cuts"), None), P(("groups", "expert"), None))
     return jax.shard_map(
-        on_device, mesh=mesh, in_specs=in_specs, out_specs=out_specs, check_vma=False
-    )
+        spread_step if spread else on_device,
+        mesh=mesh,
+        in_specs=in_specs,
+        out_specs=out_specs,
+        check_vma=False,
+    )

time: 74.8 us -> 59.9 us (0.80)
  blocking collectives: 33.4 us -> 0 us
  starting transfers between devices: 3.75 us -> 20.9 us
  waiting for transfers between devices: 10.4 us -> 25.1 us
  matrix products: 13.4 us -> 0 us
  Pallas kernels: 0 us -> 9.83 us
  local copies, waits for them, and re-layouts: 10.3 us -> 1.43 us
  other arithmetic: 1.75 us -> 0.98 us
    all_to_all x1 -> x0, blocking collectives: 33.4 us -> none  [route_experts(): lax.all_to_all(outgoing, 'expert', split_axis=0, concat_axis=0, tiled=True)]
    ppermute x0 -> x22, waiting for transfers between devices: none -> 25.1 us  [swap(): lax.ppermute(block, 'expert', [(i, i ^ distance) for i in range(count)])]
    ppermute x0 -> x22, starting transfers between devices: none -> 20.9 us  [swap(): lax.ppermute(block, 'expert', [(i, i ^ distance) for i in range(count)])]
    dot_general x6 -> x0, matrix products: 13.4 us -> none  [the longest x1 5.33 us: route_experts(): jnp.dot(hidden, expert_out[0], preferred_element_type=jnp.float32)]
    all_to_all x1 -> x0, waiting for transfers between devices: 10.4 us -> none  [route_experts(): lax.all_to_all(produced.reshape(arrived.shape), 'expert', split_axis=0, c...]
    pallas_call x0 -> x7, Pallas kernels: none -> 9.83 us  [the longest x4 5.06 us: run_expert(): pl.pallas_call(functools.partial(expert_kernel, len(parts)), out_shape=[j...]
    another operation x2 -> x0, local copies, waits for them, and re-layouts: 7.03 us -> none
    all_to_all x1 -> x0, starting transfers between devices: 3.75 us -> none  [route_experts(): lax.all_to_all(produced.reshape(arrived.shape), 'expert', split_axis=0, c...]
  transfers between devices with their start and end apart: 1 -> 22, of which waited for: 1 -> 9; matrix products, arithmetic and copies ran while one was open for 20% -> 1% of each run, Pallas kernels for 0% -> 15%
where the time goes in v2:
time: 59.9 us; the launch traced here: 59.6 us
  waiting for transfers between devices  25.1 us (42%)
  starting transfers between devices  20.9 us (35%)
  Pallas kernels  9.83 us (16%)
  local copies, waits for them, and re-layouts  1.43 us (2%)
  between operations  1.42 us (2%)
  other arithmetic  0.98 us (2%)
    ppermute x22, waiting for transfers between devices, swap(): lax.ppermute(block, 'expert', [(i, i ^ distance) for i in range(count)])  25.1 us
    ppermute x22, starting transfers between devices, swap(): lax.ppermute(block, 'expert', [(i, i ^ distance) for i in range(count)])  20.9 us
    pallas_call x4, Pallas kernels, run_expert(): pl.pallas_call(functools.partial(expert_kernel, len(parts)), out_shape=[j...  5.06 us
    pallas_call x1, Pallas kernels, attend_and_fetch(): pl.pallas_call(attend_kernel, out_shape=[jax.ShapeDtypeStruct((head_count...  3.79 us
    unnamed x3, local copies, waits for them, and re-layouts  1.39 us
  transfers between devices with their start and end apart: 22, of which 9 were waited for; matrix products, arithmetic and copies ran while one was open for 1% of the time, Pallas kernels for 15%

profile of v2, /device:TPU:0, one launch (start us, length us, event | category | flops | bytes accessed | tf_op | source)
XLA Modules:
  0.0 59.6 jit_solution(12808983492490769984)
XLA Ops:
  0.6 1.0 %label.1.refs_0_ = bf16[16,2176]{1,0:T(8,128)(2,1)S(1)} custom-call(bf16[16,2048]{1,0:T(8,128)(2,1)} %tokens_hbm.1, s32[8,16]{1,0:T(8,128)} %bitcast.17, bf16[8,16]{1,0:T(8,128)(2,1)} %bitcast.18), custom_call_target="tpu_custom_call" | custom-call | tf_op jit(solution)/shard_map/label/pallas_call | solution.py:136
  1.6 3.1 %collective-permute-start = (bf16[16,2176]{1,0:T(8,128)(2,1)S(1)}, bf16[16,2176]{1,0:T(8,128)(2,1)S(1)}, u32[]{:S(2)}, u32[]{:S(2)}) collective-permute-start(bf16[16,2176]{1,0:T(8,128)(2,1)S(1)} %label.1.refs_0_), channel_id=1, source_target_pairs={{0,8},{1,9},{2,10},{3,11},{4,12},{5,13},{6,14},{7,15},{8,0},{9,1},... | collective-permute-start | bytes 208904 | tf_op jit(solution)/shard_map/ppermute | solution.py:282
  4.7 2.6 %collective-permute-start.1 = (bf16[16,2176]{1,0:T(8,128)(2,1)S(1)}, bf16[16,2176]{1,0:T(8,128)(2,1)S(1)}, u32[]{:S(2)}, u32[]{:S(2)}) collective-permute-start(bf16[16,2176]{1,0:T(8,128)(2,1)S(1)} %label.1.refs_0_), channel_id=1, source_target_pairs={{0,16},{1,17},{2,18},{3,19},{4,20},{5,21},{6,22},{7,23},{8,24},{9,... | collective-permute-start | bytes 208904 | tf_op jit(solution)/shard_map/ppermute | solution.py:282
  7.3 0.0 collective-permute-start.2
  7.9 0.0 copy-start
  7.9 0.7 %copy-done = bf16[1,8192]{1,0:T(2,128)(2,1)S(1)} copy-done((bf16[1,8192]{1,0:T(2,128)(2,1)S(1)}, bf16[1,8192]{1,0:T(2,128)(2,1)}, u32[]{:S(2)}) %copy-start) | copy-done | bytes 16408
  8.7 3.8 %attention.1 = (bf16[64,128]{1,0:T(8,128)(2,1)S(1)}, bf16[2048,768]{1,0:T(8,128)(2,1)S(1)}, bf16[768,2048]{1,0:T(8,128)(2,1)S(1)}) custom-call(s32[1]{0:T(128)S(6)} %copy.14.lengths_ref, bf16[1,8192]{1,0:T(2,128)(2,1)S(1)} %copy-done, bf16[1536,512]{1,0:T(8,128)(2,1)} %bitcast.14, bf16[1536,512]{1,0:T(8,128)(2,1)} %bitcast.15, bf16[2048,768]{1,0:T(8,128)(2,1)} %bitcast.12, ...), custom_call_target="tpu_custom_call" | custom-call | flops 50331648 | bytes 15728640 | tf_op jit(solution)/shard_map/attention/pallas_call | solution.py:191
  12.5 0.0 collective-permute-done.1.refs_2_
  12.5 1.0 %collective-permute-done.2.refs_3_ = bf16[16,2176]{1,0:T(8,128)(2,1)S(1)} collective-permute-done((bf16[16,2176]{1,0:T(8,128)(2,1)S(1)}, bf16[16,2176]{1,0:T(8,128)(2,1)S(1)}, u32[]{:S(2)}, u32[]{:S(2)}) %collective-permute-start.2) | collective-permute-done | bytes 69664 | tf_op jit(solution)/shard_map/ppermute | solution.py:282
  13.5 1.6 %collective-permute-start.5 = (bf16[64,2176]{1,0:T(8,128)(2,1)S(1)}, bf16[64,2176]{1,0:T(8,128)(2,1)S(1)}, u32[]{:S(2)}, u32[]{:S(2)}) collective-permute-start(bf16[64,2176]{1,0:T(8,128)(2,1)S(1)} %stack.1.refs_0_), channel_id=1, source_target_pairs={{0,2},{1,3},{2,0},{3,1},{4,6},{5,7},{6,4},{7,5},{8,10},{9,11},{10,... | collective-permute-start | bytes 835592 | tf_op jit(solution)/shard_map/ppermute | solution.py:282
  15.1 1.5 %collective-permute-start.6 = (bf16[64,2176]{1,0:T(8,128)(2,1)S(1)}, bf16[64,2176]{1,0:T(8,128)(2,1)S(1)}, u32[]{:S(2)}, u32[]{:S(2)}) collective-permute-start(bf16[64,2176]{1,0:T(8,128)(2,1)S(1)} %stack.1.refs_0_), channel_id=1, source_target_pairs={{0,4},{1,5},{2,6},{3,7},{4,0},{5,1},{6,2},{7,3},{8,12},{9,13},{10,... | collective-permute-start | bytes 835592 | tf_op jit(solution)/shard_map/ppermute | solution.py:282
  16.6 3.9 %collective-permute-done.5.refs_0_ = bf16[64,2176]{1,0:T(8,128)(2,1)S(1)} collective-permute-done((bf16[64,2176]{1,0:T(8,128)(2,1)S(1)}, bf16[64,2176]{1,0:T(8,128)(2,1)S(1)}, u32[]{:S(2)}, u32[]{:S(2)}) %collective-permute-start.5) | collective-permute-done | bytes 278560 | tf_op jit(solution)/shard_map/ppermute | solution.py:282
  20.4 0.0 collective-permute-start.7
  20.5 1.2 %collective-permute-done.6.refs_1_ = bf16[64,2176]{1,0:T(8,128)(2,1)S(1)} collective-permute-done((bf16[64,2176]{1,0:T(8,128)(2,1)S(1)}, bf16[64,2176]{1,0:T(8,128)(2,1)S(1)}, u32[]{:S(2)}, u32[]{:S(2)}) %collective-permute-start.6) | collective-permute-done | bytes 278560 | tf_op jit(solution)/shard_map/ppermute | solution.py:282
  21.7 0.0 collective-permute-start.8
  21.7 0.5 collective-permute-start.3
  22.2 0.6 %collective-permute-start.13 = (bf16[32,2176]{1,0:T(8,128)(2,1)S(1)}, bf16[32,2176]{1,0:T(8,128)(2,1)S(1)}, u32[]{:S(2)}, u32[]{:S(2)}) collective-permute-start(bf16[32,2176]{1,0:T(8,128)(2,1)S(1)} %slice.27), channel_id=1, source_target_pairs={{0,2},{1,3},{2,0},{3,1},{4,6},{5,7},{6,4},{7,5},{8,10},{9,11},{10,... | collective-permute-start | bytes 417800 | tf_op jit(solution)/shard_map/ppermute | solution.py:282
  22.8 1.6 %collective-permute-start.14 = (bf16[32,2176]{1,0:T(8,128)(2,1)S(1)}, bf16[32,2176]{1,0:T(8,128)(2,1)S(1)}, u32[]{:S(2)}, u32[]{:S(2)}) collective-permute-start(bf16[32,2176]{1,0:T(8,128)(2,1)S(1)} %slice.28), channel_id=1, source_target_pairs={{0,4},{1,5},{2,6},{3,7},{4,0},{5,1},{6,2},{7,3},{8,12},{9,13},{10,... | collective-permute-start | bytes 417800 | tf_op jit(solution)/shard_map/ppermute | solution.py:282
  24.4 1.3 %expert.6 = (bf16[64,2048]{1,0:T(8,128)(2,1)S(1)}, bf16[64,2048]{1,0:T(8,128)(2,1)S(1)}) custom-call(bf16[64,2176]{1,0:T(8,128)(2,1)S(1)} %collective-permute-done.7.refs_0_, bf16[64,2176]{1,0:T(8,128)(2,1)S(1)} %collective-permute-done.8.refs_1_, bf16[2048,768]{1,0:T(8,128)(2,1)S(1)} %get-tuple-element.14.refs_2_.refs_4_, ...), custom_call_target="tpu_custom_call" | custom-call | flops 805306368 | bytes 1572864 | tf_op jit(solution)/shard_map/expert/pallas_call | solution.py:261
  25.7 0.1 collective-permute-start.9
  25.7 2.1 %collective-permute-done.13.refs_0_ = bf16[32,2176]{1,0:T(8,128)(2,1)S(1)} collective-permute-done((bf16[32,2176]{1,0:T(8,128)(2,1)S(1)}, bf16[32,2176]{1,0:T(8,128)(2,1)S(1)}, u32[]{:S(2)}, u32[]{:S(2)}) %collective-permute-start.13) | collective-permute-done | bytes 139296 | tf_op jit(solution)/shard_map/ppermute | solution.py:282
  27.8 0.0 collective-permute-start.15
  27.8 0.6 collective-permute-done.14.refs_1_
  28.4 0.0 collective-permute-start.16
  28.4 0.0 collective-permute-done.3.refs_1_
  28.4 1.3 %expert.4 = (f32[64,2048]{1,0:T(8,128)S(1)}, bf16[64,2048]{1,0:T(8,128)(2,1)S(1)}) custom-call(bf16[64,2176]{1,0:T(8,128)(2,1)S(1)} %stack.1.refs_0_, bf16[64,2176]{1,0:T(8,128)(2,1)S(1)} %collective-permute-done.3.refs_1_, bf16[2048,768]{1,0:T(8,128)(2,1)S(1)} %get-tuple-element.14.refs_2_.refs_4_, bf16[768,2048]{1,0:T(8,128)(2,1)S(1)} %get-tuple-element.15.refs_3_.refs_5_), custom_call_target="tpu_custom_call" | custom-call | flops 805306368 | bytes 1572864 | tf_op jit(solution)/shard_map/expert/pallas_call | solution.py:261
  29.7 0.6 collective-permute-start.4
  30.3 1.3 %expert.5 = (f32[64,2048]{1,0:T(8,128)S(1)}, f32[64,2048]{1,0:T(8,128)S(1)}) custom-call(bf16[64,2176]{1,0:T(8,128)(2,1)S(1)} %collective-permute-done.5.refs_0_, bf16[64,2176]{1,0:T(8,128)(2,1)S(1)} %collective-permute-done.6.refs_1_, bf16[2048,768]{1,0:T(8,128)(2,1)S(1)} %get-tuple-element.14.refs_2_.refs_4_, ...), custom_call_target="tpu_custom_call" | custom-call | flops 805306368 | bytes 1572864 | tf_op jit(solution)/shard_map/expert/pallas_call | solution.py:261
  31.5 0.1 collective-permute-start.11
  31.6 1.3 %expert.7 = (f32[64,2048]{1,0:T(8,128)S(1)}, bf16[64,2048]{1,0:T(8,128)(2,1)S(1)}) custom-call(bf16[32,2176]{1,0:T(8,128)(2,1)S(1)} %collective-permute-done.13.refs_0_, bf16[32,2176]{1,0:T(8,128)(2,1)S(1)} %collective-permute-done.14.refs_1_, bf16[32,2176]{1,0:T(8,128)(2,1)S(1)} %collective-permute-done.15.refs_2_, ...), custom_call_target="tpu_custom_call" | custom-call | flops 805306368 | bytes 1572864 | tf_op jit(solution)/shard_map/expert/pallas_call | solution.py:261
  32.9 0.5 collective-permute-start.17
  33.5 0.0 collective-permute-done.9
  33.5 0.1 add_convert_fusion.2
  33.5 1.3 %collective-permute-start.10 = (bf16[64,2048]{1,0:T(8,128)(2,1)S(1)}, bf16[64,2048]{1,0:T(8,128)(2,1)S(1)}, u32[]{:S(2)}, u32[]{:S(2)}) collective-permute-start(bf16[64,2048]{1,0:T(8,128)(2,1)S(1)} %add_convert_fusion.2), channel_id=1, source_target_pairs={{0,2},{1,3},{2,0},{3,1},{4,6},{5,7},{6,4},{7,5},{8,10},{9,11},{10,... | collective-permute-start | bytes 786440 | tf_op jit(solution)/shard_map/ppermute | solution.py:282
  34.8 0.0 collective-permute-done.11
  34.9 1.6 %collective-permute-start.12 = (bf16[64,2048]{1,0:T(8,128)(2,1)S(1)}, bf16[64,2048]{1,0:T(8,128)(2,1)S(1)}, u32[]{:S(2)}, u32[]{:S(2)}) collective-permute-start(bf16[64,2048]{1,0:T(8,128)(2,1)S(1)} %add_convert_fusion.1), channel_id=1, source_target_pairs={{0,4},{1,5},{2,6},{3,7},{4,0},{5,1},{6,2},{7,3},{8,12},{9,13},{10,... | collective-permute-start | bytes 786440 | tf_op jit(solution)/shard_map/ppermute | solution.py:282
  36.5 0.8 %collective-permute-start.18 = (bf16[64,2048]{1,0:T(8,128)(2,1)S(1)}, bf16[64,2048]{1,0:T(8,128)(2,1)S(1)}, u32[]{:S(2)}, u32[]{:S(2)}) collective-permute-start(bf16[64,2048]{1,0:T(8,128)(2,1)S(1)} %add_convert_fusion), channel_id=1, source_target_pairs={{0,6},{1,7},{2,4},{3,5},{4,2},{5,3},{6,0},{7,1},{8,14},{9,15},{10,... | collective-permute-start | bytes 786440 | tf_op jit(solution)/shard_map/ppermute | solution.py:282
  37.3 0.0 collective-permute-done.4
  37.3 5.4 %collective-permute-done.10 = bf16[64,2048]{1,0:T(8,128)(2,1)S(1)} collective-permute-done((bf16[64,2048]{1,0:T(8,128)(2,1)S(1)}, bf16[64,2048]{1,0:T(8,128)(2,1)S(1)}, u32[]{:S(2)}, u32[]{:S(2)}) %collective-permute-start.10) | collective-permute-done | bytes 262176 | tf_op jit(solution)/shard_map/ppermute | solution.py:282
  42.8 5.8 %collective-permute-done.12 = bf16[64,2048]{1,0:T(8,128)(2,1)S(1)} collective-permute-done((bf16[64,2048]{1,0:T(8,128)(2,1)S(1)}, bf16[64,2048]{1,0:T(8,128)(2,1)S(1)}, u32[]{:S(2)}, u32[]{:S(2)}) %collective-permute-start.12) | collective-permute-done | bytes 262176 | tf_op jit(solution)/shard_map/ppermute | solution.py:282
  48.5 0.2 fusion.3
  48.7 0.8 %collective-permute-start.19 = (bf16[16,2048]{1,0:T(8,128)(2,1)S(1)}, bf16[16,2048]{1,0:T(8,128)(2,1)S(1)}, u32[]{:S(2)}, u32[]{:S(2)}) collective-permute-start(bf16[16,2048]{1,0:T(8,128)(2,1)S(1)} %get-tuple-element.26), channel_id=1, source_target_pairs={{0,8},{1,9},{2,10},{3,11},{4,12},{5,13},{6,14},{7,15},{8,0},{9,1},... | collective-permute-start | bytes 196616 | tf_op jit(solution)/shard_map/ppermute | solution.py:282
  49.5 3.4 %collective-permute-start.20 = (bf16[16,2048]{1,0:T(8,128)(2,1)S(1)}, bf16[16,2048]{1,0:T(8,128)(2,1)S(1)}, u32[]{:S(2)}, u32[]{:S(2)}) collective-permute-start(bf16[16,2048]{1,0:T(8,128)(2,1)S(1)} %get-tuple-element.28), channel_id=1, source_target_pairs={{0,16},{1,17},{2,18},{3,19},{4,20},{5,21},{6,22},{7,23},{8,24},{9,... | collective-permute-start | bytes 196616 | tf_op jit(solution)/shard_map/ppermute | solution.py:282
  52.9 0.3 collective-permute-start.21
  53.2 0.6 %copy.13 = bf16[1,1,64,128]{3,1,2,0:T(2,128)(2,1)} copy(bf16[1,1,64,128]{3,2,1,0:T(8,128)(2,1)S(1)} %bitcast.11) | data formatting | bytes 32768
  53.8 3.0 %collective-permute-done.20 = bf16[16,2048]{1,0:T(8,128)(2,1)S(1)} collective-permute-done((bf16[16,2048]{1,0:T(8,128)(2,1)S(1)}, bf16[16,2048]{1,0:T(8,128)(2,1)S(1)}, u32[]{:S(2)}, u32[]{:S(2)}) %collective-permute-start.20) | collective-permute-done | bytes 65568 | tf_op jit(solution)/shard_map/ppermute | solution.py:282
  56.8 2.2 %collective-permute-done.21 = bf16[16,2048]{1,0:T(8,128)(2,1)S(1)} collective-permute-done((bf16[16,2048]{1,0:T(8,128)(2,1)S(1)}, bf16[16,2048]{1,0:T(8,128)(2,1)S(1)}, u32[]{:S(2)}, u32[]{:S(2)}) %collective-permute-start.21) | collective-permute-done | bytes 65568 | tf_op jit(solution)/shard_map/ppermute | solution.py:282
  59.0 0.7 %fusion.2 = bf16[16,2048]{1,0:T(8,128)(2,1)} fusion(f32[64,2048]{1,0:T(8,128)S(1)} %get-tuple-element.25, bf16[16,2048]{1,0:T(8,128)(2,1)S(1)} %collective-permute-done.21, bf16[16,2048]{1,0:T(8,128)(2,1)S(1)} %collective-permute-done.20, bf16[16,2048]{1,0:T(8,128)(2,1)S(1)} %collective-permute-done.19), kind=kLoop, calls=%fused_computation.7 | loop fusion | flops 229376 | bytes 393216 | tf_op jit(solution)/shard_map/convert_element_type | solution.py:324
  (14 shorter events, 0.2 us)
Async XLA Ops:
  1.6 10.9 %collective-permute-start = (bf16[16,2176]{1,0:T(8,128)(2,1)S(1)}, bf16[16,2176]{1,0:T(8,128)(2,1)S(1)}, u32[]{:S(2)}, u32[]{:S(2)}) collective-permute-start(bf16[16,2176]{1,0:T(8,128)(2,1)S(1)} %label.1.refs_0_), channel_id=1, source_target_pairs={{0,8},{1,9},{2,10},{3,11},{4,12},{5,13},{6,14},{7,15},{8,0},{9,1},... | collective-permute-start | bytes 208904 | tf_op jit(solution)/shard_map/ppermute | solution.py:282
  4.7 7.8 %collective-permute-start.1 = (bf16[16,2176]{1,0:T(8,128)(2,1)S(1)}, bf16[16,2176]{1,0:T(8,128)(2,1)S(1)}, u32[]{:S(2)}, u32[]{:S(2)}) collective-permute-start(bf16[16,2176]{1,0:T(8,128)(2,1)S(1)} %label.1.refs_0_), channel_id=1, source_target_pairs={{0,16},{1,17},{2,18},{3,19},{4,20},{5,21},{6,22},{7,23},{8,24},{9,... | collective-permute-start | bytes 208904 | tf_op jit(solution)/shard_map/ppermute | solution.py:282
  7.3 6.2 %collective-permute-start.2 = (bf16[16,2176]{1,0:T(8,128)(2,1)S(1)}, bf16[16,2176]{1,0:T(8,128)(2,1)S(1)}, u32[]{:S(2)}, u32[]{:S(2)}) collective-permute-start(bf16[16,2176]{1,0:T(8,128)(2,1)S(1)} %label.1.refs_0_), channel_id=1, source_target_pairs={{0,24},{1,25},{2,26},{3,27},{4,28},{5,29},{6,30},{7,31},{8,16},{9,... | collective-permute-start | bytes 208904 | tf_op jit(solution)/shard_map/ppermute | solution.py:282
  7.9 0.8 %copy-start = (bf16[1,8192]{1,0:T(2,128)(2,1)S(1)}, bf16[1,8192]{1,0:T(2,128)(2,1)}, u32[]{:S(2)}) copy-start(bf16[1,8192]{1,0:T(2,128)(2,1)} %query_ref.1) | copy-start | bytes 49156
  13.5 6.9 %collective-permute-start.5 = (bf16[64,2176]{1,0:T(8,128)(2,1)S(1)}, bf16[64,2176]{1,0:T(8,128)(2,1)S(1)}, u32[]{:S(2)}, u32[]{:S(2)}) collective-permute-start(bf16[64,2176]{1,0:T(8,128)(2,1)S(1)} %stack.1.refs_0_), channel_id=1, source_target_pairs={{0,2},{1,3},{2,0},{3,1},{4,6},{5,7},{6,4},{7,5},{8,10},{9,11},{10,... | collective-permute-start | bytes 835592 | tf_op jit(solution)/shard_map/ppermute | solution.py:282
  15.1 6.6 %collective-permute-start.6 = (bf16[64,2176]{1,0:T(8,128)(2,1)S(1)}, bf16[64,2176]{1,0:T(8,128)(2,1)S(1)}, u32[]{:S(2)}, u32[]{:S(2)}) collective-permute-start(bf16[64,2176]{1,0:T(8,128)(2,1)S(1)} %stack.1.refs_0_), channel_id=1, source_target_pairs={{0,4},{1,5},{2,6},{3,7},{4,0},{5,1},{6,2},{7,3},{8,12},{9,13},{10,... | collective-permute-start | bytes 835592 | tf_op jit(solution)/shard_map/ppermute | solution.py:282
  20.4 3.9 %collective-permute-start.7 = (bf16[64,2176]{1,0:T(8,128)(2,1)S(1)}, bf16[64,2176]{1,0:T(8,128)(2,1)S(1)}, u32[]{:S(2)}, u32[]{:S(2)}) collective-permute-start(bf16[64,2176]{1,0:T(8,128)(2,1)S(1)} %collective-permute-done.5.refs_0_), channel_id=1, source_target_pairs={{0,1},{1,0},{2,3},{3,2},{4,5},{5,4},{6,7},{7,6},{8,9},{9,8},{10,11... | collective-permute-start | bytes 835592 | tf_op jit(solution)/shard_map/ppermute | solution.py:282
  21.7 2.7 %collective-permute-start.8 = (bf16[64,2176]{1,0:T(8,128)(2,1)S(1)}, bf16[64,2176]{1,0:T(8,128)(2,1)S(1)}, u32[]{:S(2)}, u32[]{:S(2)}) collective-permute-start(bf16[64,2176]{1,0:T(8,128)(2,1)S(1)} %collective-permute-done.6.refs_1_), channel_id=1, source_target_pairs={{0,1},{1,0},{2,3},{3,2},{4,5},{5,4},{6,7},{7,6},{8,9},{9,8},{10,11... | collective-permute-start | bytes 835592 | tf_op jit(solution)/shard_map/ppermute | solution.py:282
  21.7 6.8 %collective-permute-start.3 = (bf16[64,2176]{1,0:T(8,128)(2,1)S(1)}, bf16[64,2176]{1,0:T(8,128)(2,1)S(1)}, u32[]{:S(2)}, u32[]{:S(2)}) collective-permute-start(bf16[64,2176]{1,0:T(8,128)(2,1)S(1)} %stack.1.refs_0_), channel_id=1, source_target_pairs={{0,1},{1,0},{2,3},{3,2},{4,5},{5,4},{6,7},{7,6},{8,9},{9,8},{10,11... | collective-permute-start | bytes 835592 | tf_op jit(solution)/shard_map/ppermute | solution.py:282
  22.2 5.6 %collective-permute-start.13 = (bf16[32,2176]{1,0:T(8,128)(2,1)S(1)}, bf16[32,2176]{1,0:T(8,128)(2,1)S(1)}, u32[]{:S(2)}, u32[]{:S(2)}) collective-permute-start(bf16[32,2176]{1,0:T(8,128)(2,1)S(1)} %slice.27), channel_id=1, source_target_pairs={{0,2},{1,3},{2,0},{3,1},{4,6},{5,7},{6,4},{7,5},{8,10},{9,11},{10,... | collective-permute-start | bytes 417800 | tf_op jit(solution)/shard_map/ppermute | solution.py:282
  22.8 5.6 %collective-permute-start.14 = (bf16[32,2176]{1,0:T(8,128)(2,1)S(1)}, bf16[32,2176]{1,0:T(8,128)(2,1)S(1)}, u32[]{:S(2)}, u32[]{:S(2)}) collective-permute-start(bf16[32,2176]{1,0:T(8,128)(2,1)S(1)} %slice.28), channel_id=1, source_target_pairs={{0,4},{1,5},{2,6},{3,7},{4,0},{5,1},{6,2},{7,3},{8,12},{9,13},{10,... | collective-permute-start | bytes 417800 | tf_op jit(solution)/shard_map/ppermute | solution.py:282
  25.7 7.8 %collective-permute-start.9 = (bf16[64,2048]{1,0:T(8,128)(2,1)S(1)}, bf16[64,2048]{1,0:T(8,128)(2,1)S(1)}, u32[]{:S(2)}, u32[]{:S(2)}) collective-permute-start(bf16[64,2048]{1,0:T(8,128)(2,1)S(1)} %get-tuple-element.19), channel_id=1, source_target_pairs={{0,1},{1,0},{2,3},{3,2},{4,5},{5,4},{6,7},{7,6},{8,9},{9,8},{10,11... | collective-permute-start | bytes 786440 | tf_op jit(solution)/shard_map/ppermute | solution.py:282
  27.8 3.8 %collective-permute-start.15 = (bf16[32,2176]{1,0:T(8,128)(2,1)S(1)}, bf16[32,2176]{1,0:T(8,128)(2,1)S(1)}, u32[]{:S(2)}, u32[]{:S(2)}) collective-permute-start(bf16[32,2176]{1,0:T(8,128)(2,1)S(1)} %collective-permute-done.13.refs_0_), channel_id=1, source_target_pairs={{0,1},{1,0},{2,3},{3,2},{4,5},{5,4},{6,7},{7,6},{8,9},{9,8},{10,11... | collective-permute-start | bytes 417800 | tf_op jit(solution)/shard_map/ppermute | solution.py:282
  28.4 3.2 %collective-permute-start.16 = (bf16[32,2176]{1,0:T(8,128)(2,1)S(1)}, bf16[32,2176]{1,0:T(8,128)(2,1)S(1)}, u32[]{:S(2)}, u32[]{:S(2)}) collective-permute-start(bf16[32,2176]{1,0:T(8,128)(2,1)S(1)} %collective-permute-done.14.refs_1_), channel_id=1, source_target_pairs={{0,1},{1,0},{2,3},{3,2},{4,5},{5,4},{6,7},{7,6},{8,9},{9,8},{10,11... | collective-permute-start | bytes 417800 | tf_op jit(solution)/shard_map/ppermute | solution.py:282
  29.7 7.6 %collective-permute-start.4 = (bf16[64,2048]{1,0:T(8,128)(2,1)S(1)}, bf16[64,2048]{1,0:T(8,128)(2,1)S(1)}, u32[]{:S(2)}, u32[]{:S(2)}) collective-permute-start(bf16[64,2048]{1,0:T(8,128)(2,1)S(1)} %get-tuple-element.17), channel_id=1, source_target_pairs={{0,1},{1,0},{2,3},{3,2},{4,5},{5,4},{6,7},{7,6},{8,9},{9,8},{10,11... | collective-permute-start | bytes 786440 | tf_op jit(solution)/shard_map/ppermute | solution.py:282
  31.5 3.3 %collective-permute-start.11 = (bf16[64,2048]{1,0:T(8,128)(2,1)S(1)}, bf16[64,2048]{1,0:T(8,128)(2,1)S(1)}, u32[]{:S(2)}, u32[]{:S(2)}) collective-permute-start(bf16[64,2048]{1,0:T(8,128)(2,1)S(1)} %get-tuple-element.21), channel_id=1, source_target_pairs={{0,1},{1,0},{2,3},{3,2},{4,5},{5,4},{6,7},{7,6},{8,9},{9,8},{10,11... | collective-permute-start | bytes 786440 | tf_op jit(solution)/shard_map/ppermute | solution.py:282
  32.9 3.6 %collective-permute-start.17 = (bf16[64,2048]{1,0:T(8,128)(2,1)S(1)}, bf16[64,2048]{1,0:T(8,128)(2,1)S(1)}, u32[]{:S(2)}, u32[]{:S(2)}) collective-permute-start(bf16[64,2048]{1,0:T(8,128)(2,1)S(1)} %get-tuple-element.23), channel_id=1, source_target_pairs={{0,1},{1,0},{2,3},{3,2},{4,5},{5,4},{6,7},{7,6},{8,9},{9,8},{10,11... | collective-permute-start | bytes 786440 | tf_op jit(solution)/shard_map/ppermute | solution.py:282
  33.5 9.2 %collective-permute-start.10 = (bf16[64,2048]{1,0:T(8,128)(2,1)S(1)}, bf16[64,2048]{1,0:T(8,128)(2,1)S(1)}, u32[]{:S(2)}, u32[]{:S(2)}) collective-permute-start(bf16[64,2048]{1,0:T(8,128)(2,1)S(1)} %add_convert_fusion.2), channel_id=1, source_target_pairs={{0,2},{1,3},{2,0},{3,1},{4,6},{5,7},{6,4},{7,5},{8,10},{9,11},{10,... | collective-permute-start | bytes 786440 | tf_op jit(solution)/shard_map/ppermute | solution.py:282
  34.9 13.6 %collective-permute-start.12 = (bf16[64,2048]{1,0:T(8,128)(2,1)S(1)}, bf16[64,2048]{1,0:T(8,128)(2,1)S(1)}, u32[]{:S(2)}, u32[]{:S(2)}) collective-permute-start(bf16[64,2048]{1,0:T(8,128)(2,1)S(1)} %add_convert_fusion.1), channel_id=1, source_target_pairs={{0,4},{1,5},{2,6},{3,7},{4,0},{5,1},{6,2},{7,3},{8,12},{9,13},{10,... | collective-permute-start | bytes 786440 | tf_op jit(solution)/shard_map/ppermute | solution.py:282
  36.5 12.0 %collective-permute-start.18 = (bf16[64,2048]{1,0:T(8,128)(2,1)S(1)}, bf16[64,2048]{1,0:T(8,128)(2,1)S(1)}, u32[]{:S(2)}, u32[]{:S(2)}) collective-permute-start(bf16[64,2048]{1,0:T(8,128)(2,1)S(1)} %add_convert_fusion), channel_id=1, source_target_pairs={{0,6},{1,7},{2,4},{3,5},{4,2},{5,3},{6,0},{7,1},{8,14},{9,15},{10,... | collective-permute-start | bytes 786440 | tf_op jit(solution)/shard_map/ppermute | solution.py:282
  48.7 5.1 %collective-permute-start.19 = (bf16[16,2048]{1,0:T(8,128)(2,1)S(1)}, bf16[16,2048]{1,0:T(8,128)(2,1)S(1)}, u32[]{:S(2)}, u32[]{:S(2)}) collective-permute-start(bf16[16,2048]{1,0:T(8,128)(2,1)S(1)} %get-tuple-element.26), channel_id=1, source_target_pairs={{0,8},{1,9},{2,10},{3,11},{4,12},{5,13},{6,14},{7,15},{8,0},{9,1},... | collective-permute-start | bytes 196616 | tf_op jit(solution)/shard_map/ppermute | solution.py:282
  49.5 7.3 %collective-permute-start.20 = (bf16[16,2048]{1,0:T(8,128)(2,1)S(1)}, bf16[16,2048]{1,0:T(8,128)(2,1)S(1)}, u32[]{:S(2)}, u32[]{:S(2)}) collective-permute-start(bf16[16,2048]{1,0:T(8,128)(2,1)S(1)} %get-tuple-element.28), channel_id=1, source_target_pairs={{0,16},{1,17},{2,18},{3,19},{4,20},{5,21},{6,22},{7,23},{8,24},{9,... | collective-permute-start | bytes 196616 | tf_op jit(solution)/shard_map/ppermute | solution.py:282
  52.9 6.1 %collective-permute-start.21 = (bf16[16,2048]{1,0:T(8,128)(2,1)S(1)}, bf16[16,2048]{1,0:T(8,128)(2,1)S(1)}, u32[]{:S(2)}, u32[]{:S(2)}) collective-permute-start(bf16[16,2048]{1,0:T(8,128)(2,1)S(1)} %get-tuple-element.27), channel_id=1, source_target_pairs={{0,24},{1,25},{2,26},{3,27},{4,28},{5,29},{6,30},{7,31},{8,16},{9,... | collective-permute-start | bytes 196616 | tf_op jit(solution)/shard_map/ppermute | solution.py:282

commit v3 on v2

--- a/solution.py
+++ b/solution.py
@@ -217,28 +217,28 @@
     return attended, near_in, near_out
 
 
-def stack_kernel(*refs):
-    parts, out_ref = refs[:-2], refs[-1]
+def stack_kernel(part_count, *refs):
+    parts, out_ref = refs[:part_count], refs[-1]
     size = parts[0].shape[0]
     for i, part in enumerate(parts):
         out_ref[i * size : (i + 1) * size, :] = part[...]
 
 
-def stack_rows(parts, after):
+def stack_rows(parts, after=()):
     size, width = parts[0].shape
     return pl.pallas_call(
-        stack_kernel,
+        functools.partial(stack_kernel, len(parts)),
         out_shape=jax.ShapeDtypeStruct((size * len(parts), width), parts[0].dtype),
-        in_specs=[VMEM] * len(parts) + [ANYWHERE],
+        in_specs=[VMEM] * len(parts) + [ANYWHERE] * len(after),
         out_specs=VMEM,
         compiler_params=pltpu.CompilerParams(vmem_limit_bytes=4 << 20),
         name="stack",
-    )(*parts, after)
-
-
-def expert_kernel(part_count, *refs):
+    )(*parts, *after)
+
+
+def expert_kernel(part_count, after_count, *refs):
     parts, (in_ref, proj_ref), results = (
-        refs[:part_count], refs[part_count : part_count + 2], refs[part_count + 2 :]
+        refs[:part_count], refs[part_count : part_count + 2], refs[part_count + 2 + after_count :]
     )
     width = in_ref.shape[0]
     rows = jnp.concatenate([part[:, :width] for part in parts], axis=0)
@@ -255,13 +255,13 @@
         first += size
 
 
-def run_expert(parts, near_in, near_out, results):
+def run_expert(parts, near_in, near_out, results, after):
     count = sum(part.shape[0] for part in parts)
     width, units = near_in.shape
     return pl.pallas_call(
-        functools.partial(expert_kernel, len(parts)),
+        functools.partial(expert_kernel, len(parts), len(after)),
         out_shape=[jax.ShapeDtypeStruct((size, width), kind) for size, kind in results],
-        in_specs=[VMEM] * (len(parts) + 2),
+        in_specs=[VMEM] * (len(parts) + 2) + [ANYWHERE] * len(after),
         out_specs=[VMEM] * len(results),
         compiler_params=pltpu.CompilerParams(vmem_limit_bytes=14 << 20),
         cost_estimate=pl.CostEstimate(
@@ -270,11 +270,39 @@
             transcendentals=count * units,
         ),
         name="expert",
-    )(*parts, hold(near_in), hold(near_out))
+    )(*parts, hold(near_in), hold(near_out), *after)
 
 
 def hold(x):
     return pltpu.with_memory_space_constraint(x, pltpu.VMEM)
+
+
+def add_kernel(part_count, *refs):
+    kept_ref, parts, result_ref = refs[0], refs[1 : part_count + 1], refs[-1]
+    back = jnp.concatenate([part[...] for part in parts], axis=0).astype(jnp.float32)
+    result_ref[...] = (kept_ref[...] + back).astype(result_ref.dtype)
+
+
+def add_parts(kept, parts, after=()):
+    return pl.pallas_call(
+        functools.partial(add_kernel, len(parts)),
+        out_shape=jax.ShapeDtypeStruct(kept.shape, parts[0].dtype),
+        in_specs=[VMEM] * (len(parts) + 1) + [ANYWHERE] * len(after),
+        out_specs=VMEM,
+        compiler_params=pltpu.CompilerParams(vmem_limit_bytes=6 << 20),
+        name="add",
+    )(kept, *parts, *after)
+
+
+def cut(block, count):
+    rows = block.shape[0] // count
+    return [block[i * rows : (i + 1) * rows] for i in range(count)]
+
+
+def cross(block, even, odd):
+    count = lax.axis_size("expert")
+    pairs = [(i, i ^ (odd if i % 2 else even)) for i in range(count)]
+    return lax.ppermute(block, "expert", pairs)
 
 
 def swap(block, distance):
@@ -294,29 +322,35 @@
     attended, near_in, near_out = attend_and_fetch(
         queries, cached_keys, cached_values, lengths, expert_in, expert_out
     )
-    column = stack_rows([own] + arrived, attended)
+
+    def gated(parts, results, after=()):
+        return run_expert(parts, near_in, near_out, results, after)
+
+    column = stack_rows([own] + arrived, [attended])
     size = column.shape[0]
     mid = size // 2
-
-    def gated(parts, results):
-        return run_expert(parts, near_in, near_out, results)
-
-    by_x, by_y = swap(column, 2), swap(column, 4)
+    cuts_in, cuts_out = 2, 2
+    split = [(size, wide)] + [(size // cuts_out, half)] * cuts_out
+
+    def halves(block):
+        return [swap(part, 1) for part in cut(block, cuts_in)]
+
     pair = swap(column, 1)
-    kept_own, sent_own = gated([column, pair], [(size, wide), (size, half)])
-    back_own = swap(sent_own, 1)
-    corner = [swap(by_y[:mid], 2), swap(by_x[mid:], 4)]
-    pair_x, pair_y = swap(by_x, 1), swap(by_y, 1)
-    kept_x, kept_y = gated([by_x, by_y], [(size, wide)] * 2)
-    sent_x, sent_y = gated([pair_x, pair_y], [(size, half)] * 2)
-    back_x, back_y = swap(sent_x, 1), swap(sent_y, 1)
-    pair_corner = [swap(part, 1) for part in corner]
-    kept_corner, sent_corner = gated(corner + pair_corner, [(size, wide), (size, half)])
-    back_corner = swap(sent_corner, 1)
-
-    total = kept_own + back_own.astype(wide)
-    for kept, back, d in ((kept_x, back_x, 2), (kept_y, back_y, 4), (kept_corner, back_corner, 6)):
-        total = total + swap((kept + back.astype(wide)).astype(half), d).astype(wide)
+    side_a = cross(column, 2, 4)
+    side_b = cross(pair, 2, 4)
+    corner = cross(side_a, 5, 3)
+    kept_a, *sent_a = gated([side_a] + halves(side_a), split)
+    sum_a = add_parts(kept_a, [swap(part, 1) for part in sent_a])
+    got_a = cross(sum_a, 2, 4)
+    kept_b, *sent_b = gated([side_b] + halves(side_b), split, [sum_a])
+    sum_b = add_parts(kept_b, [swap(part, 1) for part in sent_b])
+    got_b = cross(sum_b, 2, 4)
+    (kept_own, kept_pair) = gated([column, pair], [(size, wide)] * 2, [sum_b])
+    kept_c, *sent_c = gated([corner] + halves(corner), split, [sum_b])
+    sum_c = add_parts(kept_c, [swap(part, 1) for part in sent_c])
+    got_c = swap(sum_c, 7)
+    total = kept_own + got_a.astype(wide) + swap((kept_pair + got_b.astype(wide)).astype(half), 1).astype(wide)
+    total = total + got_c.astype(wide)
     final = total[:tok_rows]
     for i, d in enumerate(far):
         block = total[(i + 1) * tok_rows : (i + 2) * tok_rows].astype(half)

time: 59.9 us -> 55.9 us (0.933)
  waiting for transfers between devices: 25.1 us -> 19.2 us
  starting transfers between devices: 20.9 us -> 22.7 us
    ppermute x22 -> x21, waiting for transfers between devices: 25.1 us -> 12.3 us  [swap(): lax.ppermute(block, 'expert', [(i, i ^ distance) for i in range(count)])]
    ppermute x0 -> x5, waiting for transfers between devices: none -> 6.87 us  [cross(): return lax.ppermute(block, 'expert', pairs)]
    ppermute x0 -> x5, starting transfers between devices: none -> 6.79 us  [cross(): return lax.ppermute(block, 'expert', pairs)]
    ppermute x22 -> x21, starting transfers between devices: 20.9 us -> 15.9 us  [swap(): lax.ppermute(block, 'expert', [(i, i ^ distance) for i in range(count)])]
    pallas_call x5 -> x8, Pallas kernels: 5.08 us -> 5.24 us  [the longest x4 5.05 us: run_expert(): pl.pallas_call(functools.partial(expert_kernel, len(parts), len(after)),...]
  transfers between devices with their start and end apart: 22 -> 26, of which waited for: 9 -> 11; matrix products, arithmetic and copies ran while one was open for 1% -> 1% of each run, Pallas kernels for 15% -> 16%
where the time goes in v3:
time: 55.9 us; the launch traced here: 55.6 us
  starting transfers between devices  22.7 us (41%)
  waiting for transfers between devices  19.2 us (34%)
  Pallas kernels  9.99 us (18%)
  between operations  1.48 us (3%)
  local copies, waits for them, and re-layouts  1.47 us (3%)
  other arithmetic  0.85 us (2%)
    ppermute x21, starting transfers between devices, swap(): lax.ppermute(block, 'expert', [(i, i ^ distance) for i in range(count)])  15.9 us
    ppermute x21, waiting for transfers between devices, swap(): lax.ppermute(block, 'expert', [(i, i ^ distance) for i in range(count)])  12.3 us
    ppermute x5, waiting for transfers between devices, cross(): return lax.ppermute(block, 'expert', pairs)  6.87 us
    ppermute x5, starting transfers between devices, cross(): return lax.ppermute(block, 'expert', pairs)  6.79 us
    pallas_call x4, Pallas kernels, run_expert(): pl.pallas_call(functools.partial(expert_kernel, len(parts), len(after)),...  5.05 us
    pallas_call x1, Pallas kernels, attend_and_fetch(): pl.pallas_call(attend_kernel, out_shape=[jax.ShapeDtypeStruct((head_count...  3.79 us
    unnamed x3, local copies, waits for them, and re-layouts  1.39 us
  transfers between devices with their start and end apart: 26, of which 11 were waited for; matrix products, arithmetic and copies ran while one was open for 1% of the time, Pallas kernels for 16%

profile of v3, /device:TPU:0, one launch (start us, length us, event | category | flops | bytes accessed | tf_op | source)
XLA Modules:
  0.0 55.6 jit_solution(13587662710256376418)
XLA Ops:
  0.6 1.0 %label.1.refs_0_ = bf16[16,2176]{1,0:T(8,128)(2,1)S(1)} custom-call(bf16[16,2048]{1,0:T(8,128)(2,1)} %tokens_hbm.1, s32[8,16]{1,0:T(8,128)} %bitcast.17, bf16[8,16]{1,0:T(8,128)(2,1)} %bitcast.18), custom_call_target="tpu_custom_call" | custom-call | tf_op jit(solution)/shard_map/label/pallas_call | solution.py:136
  1.6 3.1 %collective-permute-start = (bf16[16,2176]{1,0:T(8,128)(2,1)S(1)}, bf16[16,2176]{1,0:T(8,128)(2,1)S(1)}, u32[]{:S(2)}, u32[]{:S(2)}) collective-permute-start(bf16[16,2176]{1,0:T(8,128)(2,1)S(1)} %label.1.refs_0_), channel_id=1, source_target_pairs={{0,8},{1,9},{2,10},{3,11},{4,12},{5,13},{6,14},{7,15},{8,0},{9,1},... | collective-permute-start | bytes 208904 | tf_op jit(solution)/shard_map/ppermute | solution.py:310
  4.7 2.6 %collective-permute-start.1 = (bf16[16,2176]{1,0:T(8,128)(2,1)S(1)}, bf16[16,2176]{1,0:T(8,128)(2,1)S(1)}, u32[]{:S(2)}, u32[]{:S(2)}) collective-permute-start(bf16[16,2176]{1,0:T(8,128)(2,1)S(1)} %label.1.refs_0_), channel_id=1, source_target_pairs={{0,16},{1,17},{2,18},{3,19},{4,20},{5,21},{6,22},{7,23},{8,24},{9,... | collective-permute-start | bytes 208904 | tf_op jit(solution)/shard_map/ppermute | solution.py:310
  7.9 0.7 %copy-done = bf16[1,8192]{1,0:T(2,128)(2,1)S(1)} copy-done((bf16[1,8192]{1,0:T(2,128)(2,1)S(1)}, bf16[1,8192]{1,0:T(2,128)(2,1)}, u32[]{:S(2)}) %copy-start) | copy-done | bytes 16408
  8.7 3.8 %attention.1 = (bf16[64,128]{1,0:T(8,128)(2,1)S(1)}, bf16[2048,768]{1,0:T(8,128)(2,1)S(1)}, bf16[768,2048]{1,0:T(8,128)(2,1)S(1)}) custom-call(s32[1]{0:T(128)S(6)} %copy.14.lengths_ref, bf16[1,8192]{1,0:T(2,128)(2,1)S(1)} %copy-done, bf16[1536,512]{1,0:T(8,128)(2,1)} %bitcast.14, bf16[1536,512]{1,0:T(8,128)(2,1)} %bitcast.15, bf16[2048,768]{1,0:T(8,128)(2,1)} %bitcast.12, ...), custom_call_target="tpu_custom_call" | custom-call | flops 50331648 | bytes 15728640 | tf_op jit(solution)/shard_map/attention/pallas_call | solution.py:191
  12.5 1.0 %collective-permute-done.2.refs_3_ = bf16[16,2176]{1,0:T(8,128)(2,1)S(1)} collective-permute-done((bf16[16,2176]{1,0:T(8,128)(2,1)S(1)}, bf16[16,2176]{1,0:T(8,128)(2,1)S(1)}, u32[]{:S(2)}, u32[]{:S(2)}) %collective-permute-start.2) | collective-permute-done | bytes 69664 | tf_op jit(solution)/shard_map/ppermute | solution.py:310
  13.5 0.1 collective-permute-start.3
  13.6 1.6 %collective-permute-start.7 = (bf16[64,2176]{1,0:T(8,128)(2,1)S(1)}, bf16[64,2176]{1,0:T(8,128)(2,1)S(1)}, u32[]{:S(2)}, u32[]{:S(2)}) collective-permute-start(bf16[64,2176]{1,0:T(8,128)(2,1)S(1)} %stack.1.refs_0_), channel_id=1, source_target_pairs={{0,2},{1,5},{2,0},{3,7},{4,6},{5,1},{6,4},{7,3},{8,10},{9,13},{10,... | collective-permute-start | bytes 835592 | tf_op jit(solution)/shard_map/ppermute | solution.py:305
  15.1 1.5 %collective-permute-start.4 = (bf16[64,2176]{1,0:T(8,128)(2,1)S(1)}, bf16[64,2176]{1,0:T(8,128)(2,1)S(1)}, u32[]{:S(2)}, u32[]{:S(2)}) collective-permute-start(bf16[64,2176]{1,0:T(8,128)(2,1)S(1)} %collective-permute-done.3.refs_1_), channel_id=1, source_target_pairs={{0,2},{1,5},{2,0},{3,7},{4,6},{5,1},{6,4},{7,3},{8,10},{9,13},{10,... | collective-permute-start | bytes 835592 | tf_op jit(solution)/shard_map/ppermute | solution.py:305
  16.6 3.6 %collective-permute-done.7.refs_0_ = bf16[64,2176]{1,0:T(8,128)(2,1)S(1)} collective-permute-done((bf16[64,2176]{1,0:T(8,128)(2,1)S(1)}, bf16[64,2176]{1,0:T(8,128)(2,1)S(1)}, u32[]{:S(2)}, u32[]{:S(2)}) %collective-permute-start.7) | collective-permute-done | bytes 278560 | tf_op jit(solution)/shard_map/ppermute | solution.py:305
  20.2 0.1 collective-permute-start.8
  20.3 0.5 collective-permute-start.9
  20.8 1.2 %collective-permute-start.17 = (bf16[64,2176]{1,0:T(8,128)(2,1)S(1)}, bf16[64,2176]{1,0:T(8,128)(2,1)S(1)}, u32[]{:S(2)}, u32[]{:S(2)}) collective-permute-start(bf16[64,2176]{1,0:T(8,128)(2,1)S(1)} %collective-permute-done.7.refs_0_), channel_id=1, source_target_pairs={{0,5},{1,2},{2,7},{3,0},{4,1},{5,6},{6,3},{7,4},{8,13},{9,10},{10,... | collective-permute-start | bytes 835592 | tf_op jit(solution)/shard_map/ppermute | solution.py:305
  22.0 1.2 %collective-permute-done.4.refs_0_ = bf16[64,2176]{1,0:T(8,128)(2,1)S(1)} collective-permute-done((bf16[64,2176]{1,0:T(8,128)(2,1)S(1)}, bf16[64,2176]{1,0:T(8,128)(2,1)S(1)}, u32[]{:S(2)}, u32[]{:S(2)}) %collective-permute-start.4) | collective-permute-done | bytes 278560 | tf_op jit(solution)/shard_map/ppermute | solution.py:305
  23.2 0.1 collective-permute-start.5
  23.3 0.5 collective-permute-start.6
  23.8 1.3 %expert.4 = (f32[64,2048]{1,0:T(8,128)S(1)}, bf16[32,2048]{1,0:T(8,128)(2,1)S(1)}, bf16[32,2048]{1,0:T(8,128)(2,1)S(1)}) custom-call(bf16[64,2176]{1,0:T(8,128)(2,1)S(1)} %collective-permute-done.7.refs_0_, bf16[32,2176]{1,0:T(8,128)(2,1)S(1)} %collective-permute-done.8.refs_1_, bf16[32,2176]{1,0:T(8,128)(2,1)S(1)} %collective-permute-done.9.refs_2_, ...), custom_call_target="tpu_custom_call" | custom-call | flops 805306368 | bytes 1572864 | tf_op jit(solution)/shard_map/expert/pallas_call | solution.py:261
  25.1 0.1 collective-permute-start.10
  25.2 0.4 collective-permute-start.11
  25.6 0.8 %collective-permute-done.10.refs_1_ = bf16[32,2048]{1,0:T(8,128)(2,1)S(1)} collective-permute-done((bf16[32,2048]{1,0:T(8,128)(2,1)S(1)}, bf16[32,2048]{1,0:T(8,128)(2,1)S(1)}, u32[]{:S(2)}, u32[]{:S(2)}) %collective-permute-start.10) | collective-permute-done | bytes 131104 | tf_op jit(solution)/shard_map/ppermute | solution.py:310
  26.5 0.2 collective-permute-done.11.refs_2_
  26.7 1.3 %expert.5 = (f32[64,2048]{1,0:T(8,128)S(1)}, bf16[32,2048]{1,0:T(8,128)(2,1)S(1)}, bf16[32,2048]{1,0:T(8,128)(2,1)S(1)}) custom-call(bf16[64,2176]{1,0:T(8,128)(2,1)S(1)} %collective-permute-done.4.refs_0_, bf16[32,2176]{1,0:T(8,128)(2,1)S(1)} %collective-permute-done.5.refs_1_, bf16[32,2176]{1,0:T(8,128)(2,1)S(1)} %collective-permute-done.6.refs_2_, ...), custom_call_target="tpu_custom_call" | custom-call | flops 805306368 | bytes 1572864 | tf_op jit(solution)/shard_map/expert/pallas_call | solution.py:261
  28.0 0.4 collective-permute-start.12
  28.4 0.2 collective-permute-start.13
  28.6 0.4 collective-permute-start.18
  29.0 0.2 collective-permute-start.19
  29.2 0.2 collective-permute-done.12.refs_1_
  29.4 0.3 collective-permute-done.13.refs_2_
  29.8 1.6 %collective-permute-start.15 = (bf16[64,2048]{1,0:T(8,128)(2,1)S(1)}, bf16[64,2048]{1,0:T(8,128)(2,1)S(1)}, u32[]{:S(2)}, u32[]{:S(2)}) collective-permute-start(bf16[64,2048]{1,0:T(8,128)(2,1)S(1)} %add.54.refs_4_.refs_5_), channel_id=1, source_target_pairs={{0,2},{1,5},{2,0},{3,7},{4,6},{5,1},{6,4},{7,3},{8,10},{9,13},{10,... | collective-permute-start | bytes 786440 | tf_op jit(solution)/shard_map/ppermute | solution.py:305
  31.4 1.3 %expert.7 = (f32[64,2048]{1,0:T(8,128)S(1)}, bf16[32,2048]{1,0:T(8,128)(2,1)S(1)}, bf16[32,2048]{1,0:T(8,128)(2,1)S(1)}) custom-call(bf16[64,2176]{1,0:T(8,128)(2,1)S(1)} %collective-permute-done.17.refs_0_, bf16[32,2176]{1,0:T(8,128)(2,1)S(1)} %collective-permute-done.18.refs_1_, bf16[32,2176]{1,0:T(8,128)(2,1)S(1)} %collective-permute-done.19.refs_2_, ...), custom_call_target="tpu_custom_call" | custom-call | flops 805306368 | bytes 1572864 | tf_op jit(solution)/shard_map/expert/pallas_call | solution.py:261
  32.6 0.1 collective-permute-start.20
  32.7 0.5 collective-permute-start.21
  33.2 1.0 %collective-permute-start.14 = (bf16[64,2048]{1,0:T(8,128)(2,1)S(1)}, bf16[64,2048]{1,0:T(8,128)(2,1)S(1)}, u32[]{:S(2)}, u32[]{:S(2)}) collective-permute-start(bf16[64,2048]{1,0:T(8,128)(2,1)S(1)} %add.53.refs_5_), channel_id=1, source_target_pairs={{0,2},{1,5},{2,0},{3,7},{4,6},{5,1},{6,4},{7,3},{8,10},{9,13},{10,... | collective-permute-start | bytes 786440 | tf_op jit(solution)/shard_map/ppermute | solution.py:305
  34.2 1.3 %expert.6 = (f32[64,2048]{1,0:T(8,128)S(1)}, f32[64,2048]{1,0:T(8,128)S(1)}) custom-call(bf16[64,2176]{1,0:T(8,128)(2,1)S(1)} %stack.1.refs_0_, bf16[64,2176]{1,0:T(8,128)(2,1)S(1)} %collective-permute-done.3.refs_1_, bf16[2048,768]{1,0:T(8,128)(2,1)S(1)} %get-tuple-element.17.refs_3_.refs_2_, bf16[768,2048]{1,0:T(8,128)(2,1)S(1)} %get-tuple-element.18.refs_4_.refs_3_, ...), custom_call_target="tpu_custom_call" | custom-call | flops 805306368 | bytes 1572864 | tf_op jit(solution)/shard_map/expert/pallas_call | solution.py:261
  35.5 0.1 add.55
  35.6 1.3 %collective-permute-start.22 = (bf16[64,2048]{1,0:T(8,128)(2,1)S(1)}, bf16[64,2048]{1,0:T(8,128)(2,1)S(1)}, u32[]{:S(2)}, u32[]{:S(2)}) collective-permute-start(bf16[64,2048]{1,0:T(8,128)(2,1)S(1)} %add.55), channel_id=1, source_target_pairs={{0,7},{1,6},{2,5},{3,4},{4,3},{5,2},{6,1},{7,0},{8,15},{9,14},{10,... | collective-permute-start | bytes 786440 | tf_op jit(solution)/shard_map/ppermute | solution.py:310
  36.8 0.1 add_convert_fusion
  36.9 1.0 %collective-permute-start.16 = (bf16[64,2048]{1,0:T(8,128)(2,1)S(1)}, bf16[64,2048]{1,0:T(8,128)(2,1)S(1)}, u32[]{:S(2)}, u32[]{:S(2)}) collective-permute-start(bf16[64,2048]{1,0:T(8,128)(2,1)S(1)} %add_convert_fusion), channel_id=1, source_target_pairs={{0,1},{1,0},{2,3},{3,2},{4,5},{5,4},{6,7},{7,6},{8,9},{9,8},{10,11... | collective-permute-start | bytes 786440 | tf_op jit(solution)/shard_map/ppermute | solution.py:310
  37.9 2.1 %collective-permute-done.14 = bf16[64,2048]{1,0:T(8,128)(2,1)S(1)} collective-permute-done((bf16[64,2048]{1,0:T(8,128)(2,1)S(1)}, bf16[64,2048]{1,0:T(8,128)(2,1)S(1)}, u32[]{:S(2)}, u32[]{:S(2)}) %collective-permute-start.14) | collective-permute-done | bytes 262176 | tf_op jit(solution)/shard_map/ppermute | solution.py:305
  40.0 5.2 %collective-permute-done.22 = bf16[64,2048]{1,0:T(8,128)(2,1)S(1)} collective-permute-done((bf16[64,2048]{1,0:T(8,128)(2,1)S(1)}, bf16[64,2048]{1,0:T(8,128)(2,1)S(1)}, u32[]{:S(2)}, u32[]{:S(2)}) %collective-permute-start.22) | collective-permute-done | bytes 262176 | tf_op jit(solution)/shard_map/ppermute | solution.py:310
  45.2 0.1 fusion.3
  45.4 0.8 %collective-permute-start.23 = (bf16[16,2048]{1,0:T(8,128)(2,1)S(1)}, bf16[16,2048]{1,0:T(8,128)(2,1)S(1)}, u32[]{:S(2)}, u32[]{:S(2)}) collective-permute-start(bf16[16,2048]{1,0:T(8,128)(2,1)S(1)} %get-tuple-element.38), channel_id=1, source_target_pairs={{0,8},{1,9},{2,10},{3,11},{4,12},{5,13},{6,14},{7,15},{8,0},{9,1},... | collective-permute-start | bytes 196616 | tf_op jit(solution)/shard_map/ppermute | solution.py:310
  46.2 2.6 %collective-permute-start.24 = (bf16[16,2048]{1,0:T(8,128)(2,1)S(1)}, bf16[16,2048]{1,0:T(8,128)(2,1)S(1)}, u32[]{:S(2)}, u32[]{:S(2)}) collective-permute-start(bf16[16,2048]{1,0:T(8,128)(2,1)S(1)} %get-tuple-element.40), channel_id=1, source_target_pairs={{0,16},{1,17},{2,18},{3,19},{4,20},{5,21},{6,22},{7,23},{8,24},{9,... | collective-permute-start | bytes 196616 | tf_op jit(solution)/shard_map/ppermute | solution.py:310
  48.8 1.0 %collective-permute-start.25 = (bf16[16,2048]{1,0:T(8,128)(2,1)S(1)}, bf16[16,2048]{1,0:T(8,128)(2,1)S(1)}, u32[]{:S(2)}, u32[]{:S(2)}) collective-permute-start(bf16[16,2048]{1,0:T(8,128)(2,1)S(1)} %get-tuple-element.39), channel_id=1, source_target_pairs={{0,24},{1,25},{2,26},{3,27},{4,28},{5,29},{6,30},{7,31},{8,16},{9,... | collective-permute-start | bytes 196616 | tf_op jit(solution)/shard_map/ppermute | solution.py:310
  49.8 0.6 %copy.13 = bf16[1,1,64,128]{3,1,2,0:T(2,128)(2,1)} copy(bf16[1,1,64,128]{3,2,1,0:T(8,128)(2,1)S(1)} %bitcast.11) | data formatting | bytes 32768
  50.5 2.8 %collective-permute-done.24 = bf16[16,2048]{1,0:T(8,128)(2,1)S(1)} collective-permute-done((bf16[16,2048]{1,0:T(8,128)(2,1)S(1)}, bf16[16,2048]{1,0:T(8,128)(2,1)S(1)}, u32[]{:S(2)}, u32[]{:S(2)}) %collective-permute-start.24) | collective-permute-done | bytes 65568 | tf_op jit(solution)/shard_map/ppermute | solution.py:310
  53.3 1.7 %collective-permute-done.25 = bf16[16,2048]{1,0:T(8,128)(2,1)S(1)} collective-permute-done((bf16[16,2048]{1,0:T(8,128)(2,1)S(1)}, bf16[16,2048]{1,0:T(8,128)(2,1)S(1)}, u32[]{:S(2)}, u32[]{:S(2)}) %collective-permute-start.25) | collective-permute-done | bytes 65568 | tf_op jit(solution)/shard_map/ppermute | solution.py:310
  55.0 0.7 %fusion.2 = bf16[16,2048]{1,0:T(8,128)(2,1)} fusion(f32[64,2048]{1,0:T(8,128)S(1)} %get-tuple-element.31, bf16[16,2048]{1,0:T(8,128)(2,1)S(1)} %collective-permute-done.25, bf16[16,2048]{1,0:T(8,128)(2,1)S(1)} %collective-permute-done.24, bf16[16,2048]{1,0:T(8,128)(2,1)S(1)} %collective-permute-done.23), kind=kLoop, calls=%fused_computation.5 | loop fusion | flops 229376 | bytes 393216 | tf_op jit(solution)/shard_map/convert_element_type | solution.py:358
  (24 shorter events, 0.3 us)
Async XLA Ops:
  1.6 10.9 %collective-permute-start = (bf16[16,2176]{1,0:T(8,128)(2,1)S(1)}, bf16[16,2176]{1,0:T(8,128)(2,1)S(1)}, u32[]{:S(2)}, u32[]{:S(2)}) collective-permute-start(bf16[16,2176]{1,0:T(8,128)(2,1)S(1)} %label.1.refs_0_), channel_id=1, source_target_pairs={{0,8},{1,9},{2,10},{3,11},{4,12},{5,13},{6,14},{7,15},{8,0},{9,1},... | collective-permute-start | bytes 208904 | tf_op jit(solution)/shard_map/ppermute | solution.py:310
  4.7 7.8 %collective-permute-start.1 = (bf16[16,2176]{1,0:T(8,128)(2,1)S(1)}, bf16[16,2176]{1,0:T(8,128)(2,1)S(1)}, u32[]{:S(2)}, u32[]{:S(2)}) collective-permute-start(bf16[16,2176]{1,0:T(8,128)(2,1)S(1)} %label.1.refs_0_), channel_id=1, source_target_pairs={{0,16},{1,17},{2,18},{3,19},{4,20},{5,21},{6,22},{7,23},{8,24},{9,... | collective-permute-start | bytes 208904 | tf_op jit(solution)/shard_map/ppermute | solution.py:310
  7.3 6.2 %collective-permute-start.2 = (bf16[16,2176]{1,0:T(8,128)(2,1)S(1)}, bf16[16,2176]{1,0:T(8,128)(2,1)S(1)}, u32[]{:S(2)}, u32[]{:S(2)}) collective-permute-start(bf16[16,2176]{1,0:T(8,128)(2,1)S(1)} %label.1.refs_0_), channel_id=1, source_target_pairs={{0,24},{1,25},{2,26},{3,27},{4,28},{5,29},{6,30},{7,31},{8,16},{9,... | collective-permute-start | bytes 208904 | tf_op jit(solution)/shard_map/ppermute | solution.py:310
  7.9 0.8 %copy-start = (bf16[1,8192]{1,0:T(2,128)(2,1)S(1)}, bf16[1,8192]{1,0:T(2,128)(2,1)}, u32[]{:S(2)}) copy-start(bf16[1,8192]{1,0:T(2,128)(2,1)} %query_ref.1) | copy-start | bytes 49156
  13.5 1.6 %collective-permute-start.3 = (bf16[64,2176]{1,0:T(8,128)(2,1)S(1)}, bf16[64,2176]{1,0:T(8,128)(2,1)S(1)}, u32[]{:S(2)}, u32[]{:S(2)}) collective-permute-start(bf16[64,2176]{1,0:T(8,128)(2,1)S(1)} %stack.1.refs_0_), channel_id=1, source_target_pairs={{0,1},{1,0},{2,3},{3,2},{4,5},{5,4},{6,7},{7,6},{8,9},{9,8},{10,11... | collective-permute-start | bytes 835592 | tf_op jit(solution)/shard_map/ppermute | solution.py:310
  13.6 6.6 %collective-permute-start.7 = (bf16[64,2176]{1,0:T(8,128)(2,1)S(1)}, bf16[64,2176]{1,0:T(8,128)(2,1)S(1)}, u32[]{:S(2)}, u32[]{:S(2)}) collective-permute-start(bf16[64,2176]{1,0:T(8,128)(2,1)S(1)} %stack.1.refs_0_), channel_id=1, source_target_pairs={{0,2},{1,5},{2,0},{3,7},{4,6},{5,1},{6,4},{7,3},{8,10},{9,13},{10,... | collective-permute-start | bytes 835592 | tf_op jit(solution)/shard_map/ppermute | solution.py:305
  15.1 8.0 %collective-permute-start.4 = (bf16[64,2176]{1,0:T(8,128)(2,1)S(1)}, bf16[64,2176]{1,0:T(8,128)(2,1)S(1)}, u32[]{:S(2)}, u32[]{:S(2)}) collective-permute-start(bf16[64,2176]{1,0:T(8,128)(2,1)S(1)} %collective-permute-done.3.refs_1_), channel_id=1, source_target_pairs={{0,2},{1,5},{2,0},{3,7},{4,6},{5,1},{6,4},{7,3},{8,10},{9,13},{10,... | collective-permute-start | bytes 835592 | tf_op jit(solution)/shard_map/ppermute | solution.py:305
  20.2 3.6 %collective-permute-start.8 = (bf16[32,2176]{1,0:T(8,128)(2,1)S(1)}, bf16[32,2176]{1,0:T(8,128)(2,1)S(1)}, u32[]{:S(2)}, u32[]{:S(2)}) collective-permute-start(bf16[32,2176]{1,0:T(8,128)(2,1)S(1)} %get-tuple-element.33), channel_id=1, source_target_pairs={{0,1},{1,0},{2,3},{3,2},{4,5},{5,4},{6,7},{7,6},{8,9},{9,8},{10,11... | collective-permute-start | bytes 417800 | tf_op jit(solution)/shard_map/ppermute | solution.py:310
  20.3 3.5 %collective-permute-start.9 = (bf16[32,2176]{1,0:T(8,128)(2,1)S(1)}, bf16[32,2176]{1,0:T(8,128)(2,1)S(1)}, u32[]{:S(2)}, u32[]{:S(2)}) collective-permute-start(bf16[32,2176]{1,0:T(8,128)(2,1)S(1)} %get-tuple-element.32), channel_id=1, source_target_pairs={{0,1},{1,0},{2,3},{3,2},{4,5},{5,4},{6,7},{7,6},{8,9},{9,8},{10,11... | collective-permute-start | bytes 417800 | tf_op jit(solution)/shard_map/ppermute | solution.py:310
  20.8 7.8 %collective-permute-start.17 = (bf16[64,2176]{1,0:T(8,128)(2,1)S(1)}, bf16[64,2176]{1,0:T(8,128)(2,1)S(1)}, u32[]{:S(2)}, u32[]{:S(2)}) collective-permute-start(bf16[64,2176]{1,0:T(8,128)(2,1)S(1)} %collective-permute-done.7.refs_0_), channel_id=1, source_target_pairs={{0,5},{1,2},{2,7},{3,0},{4,1},{5,6},{6,3},{7,4},{8,13},{9,10},{10,... | collective-permute-start | bytes 835592 | tf_op jit(solution)/shard_map/ppermute | solution.py:305
  23.2 3.5 %collective-permute-start.5 = (bf16[32,2176]{1,0:T(8,128)(2,1)S(1)}, bf16[32,2176]{1,0:T(8,128)(2,1)S(1)}, u32[]{:S(2)}, u32[]{:S(2)}) collective-permute-start(bf16[32,2176]{1,0:T(8,128)(2,1)S(1)} %get-tuple-element.35), channel_id=1, source_target_pairs={{0,1},{1,0},{2,3},{3,2},{4,5},{5,4},{6,7},{7,6},{8,9},{9,8},{10,11... | collective-permute-start | bytes 417800 | tf_op jit(solution)/shard_map/ppermute | solution.py:310
  23.3 3.4 %collective-permute-start.6 = (bf16[32,2176]{1,0:T(8,128)(2,1)S(1)}, bf16[32,2176]{1,0:T(8,128)(2,1)S(1)}, u32[]{:S(2)}, u32[]{:S(2)}) collective-permute-start(bf16[32,2176]{1,0:T(8,128)(2,1)S(1)} %get-tuple-element.34), channel_id=1, source_target_pairs={{0,1},{1,0},{2,3},{3,2},{4,5},{5,4},{6,7},{7,6},{8,9},{9,8},{10,11... | collective-permute-start | bytes 417800 | tf_op jit(solution)/shard_map/ppermute | solution.py:310
  25.1 1.4 %collective-permute-start.10 = (bf16[32,2048]{1,0:T(8,128)(2,1)S(1)}, bf16[32,2048]{1,0:T(8,128)(2,1)S(1)}, u32[]{:S(2)}, u32[]{:S(2)}) collective-permute-start(bf16[32,2048]{1,0:T(8,128)(2,1)S(1)} %get-tuple-element.20), channel_id=1, source_target_pairs={{0,1},{1,0},{2,3},{3,2},{4,5},{5,4},{6,7},{7,6},{8,9},{9,8},{10,11... | collective-permute-start | bytes 393224 | tf_op jit(solution)/shard_map/ppermute | solution.py:310
  25.2 1.5 %collective-permute-start.11 = (bf16[32,2048]{1,0:T(8,128)(2,1)S(1)}, bf16[32,2048]{1,0:T(8,128)(2,1)S(1)}, u32[]{:S(2)}, u32[]{:S(2)}) collective-permute-start(bf16[32,2048]{1,0:T(8,128)(2,1)S(1)} %get-tuple-element.21), channel_id=1, source_target_pairs={{0,1},{1,0},{2,3},{3,2},{4,5},{5,4},{6,7},{7,6},{8,9},{9,8},{10,11... | collective-permute-start | bytes 393224 | tf_op jit(solution)/shard_map/ppermute | solution.py:310
  28.0 1.4 %collective-permute-start.12 = (bf16[32,2048]{1,0:T(8,128)(2,1)S(1)}, bf16[32,2048]{1,0:T(8,128)(2,1)S(1)}, u32[]{:S(2)}, u32[]{:S(2)}) collective-permute-start(bf16[32,2048]{1,0:T(8,128)(2,1)S(1)} %get-tuple-element.23), channel_id=1, source_target_pairs={{0,1},{1,0},{2,3},{3,2},{4,5},{5,4},{6,7},{7,6},{8,9},{9,8},{10,11... | collective-permute-start | bytes 393224 | tf_op jit(solution)/shard_map/ppermute | solution.py:310
  28.4 1.3 %collective-permute-start.13 = (bf16[32,2048]{1,0:T(8,128)(2,1)S(1)}, bf16[32,2048]{1,0:T(8,128)(2,1)S(1)}, u32[]{:S(2)}, u32[]{:S(2)}) collective-permute-start(bf16[32,2048]{1,0:T(8,128)(2,1)S(1)} %get-tuple-element.24), channel_id=1, source_target_pairs={{0,1},{1,0},{2,3},{3,2},{4,5},{5,4},{6,7},{7,6},{8,9},{9,8},{10,11... | collective-permute-start | bytes 393224 | tf_op jit(solution)/shard_map/ppermute | solution.py:310
  28.6 2.7 %collective-permute-start.18 = (bf16[32,2176]{1,0:T(8,128)(2,1)S(1)}, bf16[32,2176]{1,0:T(8,128)(2,1)S(1)}, u32[]{:S(2)}, u32[]{:S(2)}) collective-permute-start(bf16[32,2176]{1,0:T(8,128)(2,1)S(1)} %get-tuple-element.37), channel_id=1, source_target_pairs={{0,1},{1,0},{2,3},{3,2},{4,5},{5,4},{6,7},{7,6},{8,9},{9,8},{10,11... | collective-permute-start | bytes 417800 | tf_op jit(solution)/shard_map/ppermute | solution.py:310
  29.0 2.4 %collective-permute-start.19 = (bf16[32,2176]{1,0:T(8,128)(2,1)S(1)}, bf16[32,2176]{1,0:T(8,128)(2,1)S(1)}, u32[]{:S(2)}, u32[]{:S(2)}) collective-permute-start(bf16[32,2176]{1,0:T(8,128)(2,1)S(1)} %get-tuple-element.36), channel_id=1, source_target_pairs={{0,1},{1,0},{2,3},{3,2},{4,5},{5,4},{6,7},{7,6},{8,9},{9,8},{10,11... | collective-permute-start | bytes 417800 | tf_op jit(solution)/shard_map/ppermute | solution.py:310
  29.8 7.0 %collective-permute-start.15 = (bf16[64,2048]{1,0:T(8,128)(2,1)S(1)}, bf16[64,2048]{1,0:T(8,128)(2,1)S(1)}, u32[]{:S(2)}, u32[]{:S(2)}) collective-permute-start(bf16[64,2048]{1,0:T(8,128)(2,1)S(1)} %add.54.refs_4_.refs_5_), channel_id=1, source_target_pairs={{0,2},{1,5},{2,0},{3,7},{4,6},{5,1},{6,4},{7,3},{8,10},{9,13},{10,... | collective-permute-start | bytes 786440 | tf_op jit(solution)/shard_map/ppermute | solution.py:305
  32.6 2.9 %collective-permute-start.20 = (bf16[32,2048]{1,0:T(8,128)(2,1)S(1)}, bf16[32,2048]{1,0:T(8,128)(2,1)S(1)}, u32[]{:S(2)}, u32[]{:S(2)}) collective-permute-start(bf16[32,2048]{1,0:T(8,128)(2,1)S(1)} %get-tuple-element.28), channel_id=1, source_target_pairs={{0,1},{1,0},{2,3},{3,2},{4,5},{5,4},{6,7},{7,6},{8,9},{9,8},{10,11... | collective-permute-start | bytes 393224 | tf_op jit(solution)/shard_map/ppermute | solution.py:310
  32.7 2.8 %collective-permute-start.21 = (bf16[32,2048]{1,0:T(8,128)(2,1)S(1)}, bf16[32,2048]{1,0:T(8,128)(2,1)S(1)}, u32[]{:S(2)}, u32[]{:S(2)}) collective-permute-start(bf16[32,2048]{1,0:T(8,128)(2,1)S(1)} %get-tuple-element.29), channel_id=1, source_target_pairs={{0,1},{1,0},{2,3},{3,2},{4,5},{5,4},{6,7},{7,6},{8,9},{9,8},{10,11... | collective-permute-start | bytes 393224 | tf_op jit(solution)/shard_map/ppermute | solution.py:310
  33.2 6.8 %collective-permute-start.14 = (bf16[64,2048]{1,0:T(8,128)(2,1)S(1)}, bf16[64,2048]{1,0:T(8,128)(2,1)S(1)}, u32[]{:S(2)}, u32[]{:S(2)}) collective-permute-start(bf16[64,2048]{1,0:T(8,128)(2,1)S(1)} %add.53.refs_5_), channel_id=1, source_target_pairs={{0,2},{1,5},{2,0},{3,7},{4,6},{5,1},{6,4},{7,3},{8,10},{9,13},{10,... | collective-permute-start | bytes 786440 | tf_op jit(solution)/shard_map/ppermute | solution.py:305
  35.6 9.6 %collective-permute-start.22 = (bf16[64,2048]{1,0:T(8,128)(2,1)S(1)}, bf16[64,2048]{1,0:T(8,128)(2,1)S(1)}, u32[]{:S(2)}, u32[]{:S(2)}) collective-permute-start(bf16[64,2048]{1,0:T(8,128)(2,1)S(1)} %add.55), channel_id=1, source_target_pairs={{0,7},{1,6},{2,5},{3,4},{4,3},{5,2},{6,1},{7,0},{8,15},{9,14},{10,... | collective-permute-start | bytes 786440 | tf_op jit(solution)/shard_map/ppermute | solution.py:310
  36.9 8.3 %collective-permute-start.16 = (bf16[64,2048]{1,0:T(8,128)(2,1)S(1)}, bf16[64,2048]{1,0:T(8,128)(2,1)S(1)}, u32[]{:S(2)}, u32[]{:S(2)}) collective-permute-start(bf16[64,2048]{1,0:T(8,128)(2,1)S(1)} %add_convert_fusion), channel_id=1, source_target_pairs={{0,1},{1,0},{2,3},{3,2},{4,5},{5,4},{6,7},{7,6},{8,9},{9,8},{10,11... | collective-permute-start | bytes 786440 | tf_op jit(solution)/shard_map/ppermute | solution.py:310
  45.4 5.1 %collective-permute-start.23 = (bf16[16,2048]{1,0:T(8,128)(2,1)S(1)}, bf16[16,2048]{1,0:T(8,128)(2,1)S(1)}, u32[]{:S(2)}, u32[]{:S(2)}) collective-permute-start(bf16[16,2048]{1,0:T(8,128)(2,1)S(1)} %get-tuple-element.38), channel_id=1, source_target_pairs={{0,8},{1,9},{2,10},{3,11},{4,12},{5,13},{6,14},{7,15},{8,0},{9,1},... | collective-permute-start | bytes 196616 | tf_op jit(solution)/shard_map/ppermute | solution.py:310
  46.2 7.1 %collective-permute-start.24 = (bf16[16,2048]{1,0:T(8,128)(2,1)S(1)}, bf16[16,2048]{1,0:T(8,128)(2,1)S(1)}, u32[]{:S(2)}, u32[]{:S(2)}) collective-permute-start(bf16[16,2048]{1,0:T(8,128)(2,1)S(1)} %get-tuple-element.40), channel_id=1, source_target_pairs={{0,16},{1,17},{2,18},{3,19},{4,20},{5,21},{6,22},{7,23},{8,24},{9,... | collective-permute-start | bytes 196616 | tf_op jit(solution)/shard_map/ppermute | solution.py:310
  48.8 6.1 %collective-permute-start.25 = (bf16[16,2048]{1,0:T(8,128)(2,1)S(1)}, bf16[16,2048]{1,0:T(8,128)(2,1)S(1)}, u32[]{:S(2)}, u32[]{:S(2)}) collective-permute-start(bf16[16,2048]{1,0:T(8,128)(2,1)S(1)} %get-tuple-element.39), channel_id=1, source_target_pairs={{0,24},{1,25},{2,26},{3,27},{4,28},{5,29},{6,30},{7,31},{8,16},{9,... | collective-permute-start | bytes 196616 | tf_op jit(solution)/shard_map/ppermute | solution.py:310

commit v4 on v3

--- a/solution.py
+++ b/solution.py
@@ -294,6 +294,44 @@
     )(kept, *parts, *after)
 
 
+def finish_kernel(first, total_ref, block_ref, *part_refs):
+    rows = part_refs[0].shape[0]
+    for i, part_ref in enumerate(part_refs):
+        at = slice(first + i * rows, first + (i + 1) * rows)
+        block = block_ref[i * rows : (i + 1) * rows, :].astype(jnp.float32)
+        part_ref[...] = (total_ref[at, :] + block).astype(part_ref.dtype)
+
+
+def finish_rows(total, block, first, count):
+    part = jax.ShapeDtypeStruct((block.shape[0] // count, block.shape[1]), block.dtype)
+    return pl.pallas_call(
+        functools.partial(finish_kernel, first),
+        out_shape=[part] * count,
+        in_specs=[VMEM] * 2,
+        out_specs=[VMEM] * count,
+        compiler_params=pltpu.CompilerParams(vmem_limit_bytes=4 << 20),
+        name="finish",
+    )(total, block)
+
+
+def cut_kernel(count, block_ref, *refs):
+    rows = block_ref.shape[0] // count
+    for i, part_ref in enumerate(refs[-count:]):
+        part_ref[...] = block_ref[i * rows : (i + 1) * rows, :]
+
+
+def cut_rows(block, count, after=()):
+    part = jax.ShapeDtypeStruct((block.shape[0] // count, block.shape[1]), block.dtype)
+    return pl.pallas_call(
+        functools.partial(cut_kernel, count),
+        out_shape=[part] * count,
+        in_specs=[VMEM] + [ANYWHERE] * len(after),
+        out_specs=[VMEM] * count,
+        compiler_params=pltpu.CompilerParams(vmem_limit_bytes=4 << 20),
+        name="cut",
+    )(block, *after)
+
+
 def cut(block, count):
     rows = block.shape[0] // count
     return [block[i * rows : (i + 1) * rows] for i in range(count)]
@@ -328,33 +366,41 @@
 
     column = stack_rows([own] + arrived, [attended])
     size = column.shape[0]
-    mid = size // 2
-    cuts_in, cuts_out = 2, 2
-    split = [(size, wide)] + [(size // cuts_out, half)] * cuts_out
-
-    def halves(block):
-        return [swap(part, 1) for part in cut(block, cuts_in)]
+    pieces = 2
+    split = [(size, wide)] + [(size // pieces, half)] * pieces
+
+    def to_pair(block, after=()):
+        return [swap(part, 1) for part in cut_rows(block, pieces, after)]
 
     pair = swap(column, 1)
     side_a = cross(column, 2, 4)
     side_b = cross(pair, 2, 4)
     corner = cross(side_a, 5, 3)
-    kept_a, *sent_a = gated([side_a] + halves(side_a), split)
+    kept_own, kept_pair = gated([column, pair], [(size, wide)] * 2, [])
+    kept_a, *sent_a = gated([side_a] + to_pair(side_a, []), split)
     sum_a = add_parts(kept_a, [swap(part, 1) for part in sent_a])
     got_a = cross(sum_a, 2, 4)
-    kept_b, *sent_b = gated([side_b] + halves(side_b), split, [sum_a])
+    kept_b, *sent_b = gated([side_b] + to_pair(side_b, []), split, [sum_a])
     sum_b = add_parts(kept_b, [swap(part, 1) for part in sent_b])
     got_b = cross(sum_b, 2, 4)
-    (kept_own, kept_pair) = gated([column, pair], [(size, wide)] * 2, [sum_b])
-    kept_c, *sent_c = gated([corner] + halves(corner), split, [sum_b])
-    sum_c = add_parts(kept_c, [swap(part, 1) for part in sent_c])
-    got_c = swap(sum_c, 7)
-    total = kept_own + got_a.astype(wide) + swap((kept_pair + got_b.astype(wide)).astype(half), 1).astype(wide)
-    total = total + got_c.astype(wide)
-    final = total[:tok_rows]
-    for i, d in enumerate(far):
-        block = total[(i + 1) * tok_rows : (i + 2) * tok_rows].astype(half)
-        final = final + swap(block, d).astype(wide)
+    kept_c, *sent_c = gated([corner] + to_pair(corner), split, [sum_b])
+    sum_c = add_parts(kept_c, [swap(part, 1) for part in sent_c], [])
+    shared = add_parts(kept_pair, [got_b], [got_a, sum_c])
+    total = kept_own + got_a.astype(wide) + swap(shared, 1).astype(wide)
+    bounds = (0, tok_rows, 2 * tok_rows, size)
+    returned = []
+    for first, last in reversed(list(zip(bounds[:-1], bounds[1:]))):
+        returned.append((first, last, swap(sum_c[first:last], 7)))
+    sums = {}
+    for first, last, block in returned:
+        block = total[first:last] + block.astype(wide)
+        for k in range(first // tok_rows, last // tok_rows):
+            sums[k] = block[k * tok_rows - first : (k + 1) * tok_rows - first]
+    final = sums[0]
+    for k in (3, 2, 1):
+        block = sums[k].astype(half)
+        got = [swap(part, far[k - 1]) for part in cut(block, 2 if k == 0 else 1)]
+        final = final + (got[0] if len(got) == 1 else jnp.concatenate(got)).astype(wide)
     return final.astype(half), attended.reshape(queries.shape)
 
 

time: 55.9 us -> 51.9 us (0.928)
  waiting for transfers between devices: 19.2 us -> 12.1 us
  starting transfers between devices: 22.7 us -> 25.7 us
    ppermute x21 -> x23, waiting for transfers between devices: 12.3 us -> 5.75 us  [swap(): lax.ppermute(block, 'expert', [(i, i ^ distance) for i in range(count)])]
    ppermute x21 -> x23, starting transfers between devices: 15.9 us -> 19.3 us  [swap(): lax.ppermute(block, 'expert', [(i, i ^ distance) for i in range(count)])]
  transfers between devices with their start and end apart: 26 -> 28, of which waited for: 11 -> 8; matrix products, arithmetic and copies ran while one was open for 1% -> 2% of each run, Pallas kernels for 16% -> 18%
where the time goes in v4:
time: 51.9 us; the launch traced here: 51.6 us
  starting transfers between devices  25.7 us (50%)
  waiting for transfers between devices  12.1 us (23%)
  Pallas kernels  10.1 us (19%)
  between operations  1.52 us (3%)
  local copies, waits for them, and re-layouts  1.43 us (3%)
  other arithmetic  0.79 us (2%)
    ppermute x23, starting transfers between devices, swap(): lax.ppermute(block, 'expert', [(i, i ^ distance) for i in range(count)])  19.3 us
    ppermute x5, waiting for transfers between devices, cross(): return lax.ppermute(block, 'expert', pairs)  6.35 us
    ppermute x5, starting transfers between devices, cross(): return lax.ppermute(block, 'expert', pairs)  6.34 us
    ppermute x23, waiting for transfers between devices, swap(): lax.ppermute(block, 'expert', [(i, i ^ distance) for i in range(count)])  5.75 us
    pallas_call x4, Pallas kernels, run_expert(): pl.pallas_call(functools.partial(expert_kernel, len(parts), len(after)),...  5.08 us
    pallas_call x1, Pallas kernels, attend_and_fetch(): pl.pallas_call(attend_kernel, out_shape=[jax.ShapeDtypeStruct((head_count...  3.79 us
    unnamed x3, local copies, waits for them, and re-layouts  1.39 us
  transfers between devices with their start and end apart: 28, of which 8 were waited for; matrix products, arithmetic and copies ran while one was open for 2% of the time, Pallas kernels for 18%

profile of v4, /device:TPU:0, one launch (start us, length us, event | category | flops | bytes accessed | tf_op | source)
XLA Modules:
  0.0 51.6 jit_solution(8548201549824597454)
XLA Ops:
  0.6 1.0 %label.1.refs_0_ = bf16[16,2176]{1,0:T(8,128)(2,1)S(1)} custom-call(bf16[16,2048]{1,0:T(8,128)(2,1)} %tokens_hbm.1, s32[8,16]{1,0:T(8,128)} %bitcast.17, bf16[8,16]{1,0:T(8,128)(2,1)} %bitcast.18), custom_call_target="tpu_custom_call" | custom-call | tf_op jit(solution)/shard_map/label/pallas_call | solution.py:136
  1.6 3.1 %collective-permute-start = (bf16[16,2176]{1,0:T(8,128)(2,1)S(1)}, bf16[16,2176]{1,0:T(8,128)(2,1)S(1)}, u32[]{:S(2)}, u32[]{:S(2)}) collective-permute-start(bf16[16,2176]{1,0:T(8,128)(2,1)S(1)} %label.1.refs_0_), channel_id=1, source_target_pairs={{0,8},{1,9},{2,10},{3,11},{4,12},{5,13},{6,14},{7,15},{8,0},{9,1},... | collective-permute-start | bytes 208904 | tf_op jit(solution)/shard_map/ppermute | solution.py:348
  4.7 2.6 %collective-permute-start.1 = (bf16[16,2176]{1,0:T(8,128)(2,1)S(1)}, bf16[16,2176]{1,0:T(8,128)(2,1)S(1)}, u32[]{:S(2)}, u32[]{:S(2)}) collective-permute-start(bf16[16,2176]{1,0:T(8,128)(2,1)S(1)} %label.1.refs_0_), channel_id=1, source_target_pairs={{0,16},{1,17},{2,18},{3,19},{4,20},{5,21},{6,22},{7,23},{8,24},{9,... | collective-permute-start | bytes 208904 | tf_op jit(solution)/shard_map/ppermute | solution.py:348
  7.9 0.7 %copy-done = bf16[1,8192]{1,0:T(2,128)(2,1)S(1)} copy-done((bf16[1,8192]{1,0:T(2,128)(2,1)S(1)}, bf16[1,8192]{1,0:T(2,128)(2,1)}, u32[]{:S(2)}) %copy-start) | copy-done | bytes 16408
  8.7 3.8 %attention.1 = (bf16[64,128]{1,0:T(8,128)(2,1)S(1)}, bf16[2048,768]{1,0:T(8,128)(2,1)S(1)}, bf16[768,2048]{1,0:T(8,128)(2,1)S(1)}) custom-call(s32[1]{0:T(128)S(6)} %copy.14.lengths_ref, bf16[1,8192]{1,0:T(2,128)(2,1)S(1)} %copy-done, bf16[1536,512]{1,0:T(8,128)(2,1)} %bitcast.14, bf16[1536,512]{1,0:T(8,128)(2,1)} %bitcast.15, bf16[2048,768]{1,0:T(8,128)(2,1)} %bitcast.12, ...), custom_call_target="tpu_custom_call" | custom-call | flops 50331648 | bytes 15728640 | tf_op jit(solution)/shard_map/attention/pallas_call | solution.py:191
  12.5 1.0 %collective-permute-done.2.refs_3_ = bf16[16,2176]{1,0:T(8,128)(2,1)S(1)} collective-permute-done((bf16[16,2176]{1,0:T(8,128)(2,1)S(1)}, bf16[16,2176]{1,0:T(8,128)(2,1)S(1)}, u32[]{:S(2)}, u32[]{:S(2)}) %collective-permute-start.2) | collective-permute-done | bytes 69664 | tf_op jit(solution)/shard_map/ppermute | solution.py:348
  13.5 0.1 collective-permute-start.3
  13.6 1.6 %collective-permute-start.4 = (bf16[64,2176]{1,0:T(8,128)(2,1)S(1)}, bf16[64,2176]{1,0:T(8,128)(2,1)S(1)}, u32[]{:S(2)}, u32[]{:S(2)}) collective-permute-start(bf16[64,2176]{1,0:T(8,128)(2,1)S(1)} %stack.1.refs_0_), channel_id=1, source_target_pairs={{0,2},{1,5},{2,0},{3,7},{4,6},{5,1},{6,4},{7,3},{8,10},{9,13},{10,... | collective-permute-start | bytes 835592 | tf_op jit(solution)/shard_map/ppermute | solution.py:343
  15.1 1.5 %collective-permute-start.10 = (bf16[64,2176]{1,0:T(8,128)(2,1)S(1)}, bf16[64,2176]{1,0:T(8,128)(2,1)S(1)}, u32[]{:S(2)}, u32[]{:S(2)}) collective-permute-start(bf16[64,2176]{1,0:T(8,128)(2,1)S(1)} %collective-permute-done.3.refs_1_), channel_id=1, source_target_pairs={{0,2},{1,5},{2,0},{3,7},{4,6},{5,1},{6,4},{7,3},{8,10},{9,13},{10,... | collective-permute-start | bytes 835592 | tf_op jit(solution)/shard_map/ppermute | solution.py:343
  16.6 3.6 %collective-permute-done.4.block_ref.refs_0_ = bf16[64,2176]{1,0:T(8,128)(2,1)S(1)} collective-permute-done((bf16[64,2176]{1,0:T(8,128)(2,1)S(1)}, bf16[64,2176]{1,0:T(8,128)(2,1)S(1)}, u32[]{:S(2)}, u32[]{:S(2)}) %collective-permute-start.4) | collective-permute-done | bytes 278560 | tf_op jit(solution)/shard_map/ppermute | solution.py:343
  20.2 0.1 collective-permute-start.5
  20.3 0.5 collective-permute-start.6
  20.8 1.2 %collective-permute-start.16 = (bf16[64,2176]{1,0:T(8,128)(2,1)S(1)}, bf16[64,2176]{1,0:T(8,128)(2,1)S(1)}, u32[]{:S(2)}, u32[]{:S(2)}) collective-permute-start(bf16[64,2176]{1,0:T(8,128)(2,1)S(1)} %collective-permute-done.4.block_ref.refs_0_), channel_id=1, source_target_pairs={{0,5},{1,2},{2,7},{3,0},{4,1},{5,6},{6,3},{7,4},{8,13},{9,10},{10,... | collective-permute-start | bytes 835592 | tf_op jit(solution)/shard_map/ppermute | solution.py:343
  22.0 1.2 %collective-permute-done.10.block_ref.refs_0_ = bf16[64,2176]{1,0:T(8,128)(2,1)S(1)} collective-permute-done((bf16[64,2176]{1,0:T(8,128)(2,1)S(1)}, bf16[64,2176]{1,0:T(8,128)(2,1)S(1)}, u32[]{:S(2)}, u32[]{:S(2)}) %collective-permute-start.10) | collective-permute-done | bytes 278560 | tf_op jit(solution)/shard_map/ppermute | solution.py:343
  23.2 0.1 collective-permute-start.11
  23.3 0.5 collective-permute-start.12
  23.8 1.3 %expert.5 = (f32[64,2048]{1,0:T(8,128)S(1)}, bf16[32,2048]{1,0:T(8,128)(2,1)S(1)}, bf16[32,2048]{1,0:T(8,128)(2,1)S(1)}) custom-call(bf16[64,2176]{1,0:T(8,128)(2,1)S(1)} %collective-permute-done.4.block_ref.refs_0_, bf16[32,2176]{1,0:T(8,128)(2,1)S(1)} %collective-permute-done.5.refs_1_, bf16[32,2176]{1,0:T(8,128)(2,1)S(1)} %collective-permute-done.6.refs_2_, ...), custom_call_target="tpu_custom_call" | custom-call | flops 805306368 | bytes 1572864 | tf_op jit(solution)/shard_map/expert/pallas_call | solution.py:261
  25.1 0.1 collective-permute-start.7
  25.2 0.4 collective-permute-start.8
  25.6 0.8 %collective-permute-done.7.refs_1_ = bf16[32,2048]{1,0:T(8,128)(2,1)S(1)} collective-permute-done((bf16[32,2048]{1,0:T(8,128)(2,1)S(1)}, bf16[32,2048]{1,0:T(8,128)(2,1)S(1)}, u32[]{:S(2)}, u32[]{:S(2)}) %collective-permute-start.7) | collective-permute-done | bytes 131104 | tf_op jit(solution)/shard_map/ppermute | solution.py:348
  26.5 0.2 collective-permute-done.8.refs_2_
  26.7 0.1 add.68.refs_5_
  26.7 1.3 %expert.6 = (f32[64,2048]{1,0:T(8,128)S(1)}, bf16[32,2048]{1,0:T(8,128)(2,1)S(1)}, bf16[32,2048]{1,0:T(8,128)(2,1)S(1)}) custom-call(bf16[64,2176]{1,0:T(8,128)(2,1)S(1)} %collective-permute-done.10.block_ref.refs_0_, bf16[32,2176]{1,0:T(8,128)(2,1)S(1)} %collective-permute-done.11.refs_1_, bf16[32,2176]{1,0:T(8,128)(2,1)S(1)} %collective-permute-done.12.refs_2_, ...), custom_call_target="tpu_custom_call" | custom-call | flops 805306368 | bytes 1572864 | tf_op jit(solution)/shard_map/expert/pallas_call | solution.py:261
  28.0 0.4 collective-permute-start.13
  28.4 0.2 collective-permute-start.14
  28.6 0.4 collective-permute-start.17
  29.0 0.2 collective-permute-start.18
  29.2 1.5 %collective-permute-start.9 = (bf16[64,2048]{1,0:T(8,128)(2,1)S(1)}, bf16[64,2048]{1,0:T(8,128)(2,1)S(1)}, u32[]{:S(2)}, u32[]{:S(2)}) collective-permute-start(bf16[64,2048]{1,0:T(8,128)(2,1)S(1)} %add.68.refs_5_), channel_id=1, source_target_pairs={{0,2},{1,5},{2,0},{3,7},{4,6},{5,1},{6,4},{7,3},{8,10},{9,13},{10,... | collective-permute-start | bytes 786440 | tf_op jit(solution)/shard_map/ppermute | solution.py:343
  30.7 0.1 add.69.refs_5_
  30.8 0.6 %collective-permute-start.15 = (bf16[64,2048]{1,0:T(8,128)(2,1)S(1)}, bf16[64,2048]{1,0:T(8,128)(2,1)S(1)}, u32[]{:S(2)}, u32[]{:S(2)}) collective-permute-start(bf16[64,2048]{1,0:T(8,128)(2,1)S(1)} %add.69.refs_5_), channel_id=1, source_target_pairs={{0,2},{1,5},{2,0},{3,7},{4,6},{5,1},{6,4},{7,3},{8,10},{9,13},{10,... | collective-permute-start | bytes 786440 | tf_op jit(solution)/shard_map/ppermute | solution.py:343
  31.4 1.3 %expert.7 = (f32[64,2048]{1,0:T(8,128)S(1)}, bf16[32,2048]{1,0:T(8,128)(2,1)S(1)}, bf16[32,2048]{1,0:T(8,128)(2,1)S(1)}) custom-call(bf16[64,2176]{1,0:T(8,128)(2,1)S(1)} %collective-permute-done.16.block_ref.refs_0_, bf16[32,2176]{1,0:T(8,128)(2,1)S(1)} %collective-permute-done.17.refs_1_, bf16[32,2176]{1,0:T(8,128)(2,1)S(1)} %collective-permute-done.18.refs_2_, ...), custom_call_target="tpu_custom_call" | custom-call | flops 805306368 | bytes 1572864 | tf_op jit(solution)/shard_map/expert/pallas_call | solution.py:261
  32.7 0.1 collective-permute-start.19
  32.7 0.5 collective-permute-start.20
  33.2 1.3 %expert.4 = (f32[64,2048]{1,0:T(8,128)S(1)}, f32[64,2048]{1,0:T(8,128)S(1)}) custom-call(bf16[64,2176]{1,0:T(8,128)(2,1)S(1)} %stack.1.refs_0_, bf16[64,2176]{1,0:T(8,128)(2,1)S(1)} %collective-permute-done.3.refs_1_, bf16[2048,768]{1,0:T(8,128)(2,1)S(1)} %get-tuple-element.23.refs_2_.refs_3_, bf16[768,2048]{1,0:T(8,128)(2,1)S(1)} %get-tuple-element.24.refs_3_.refs_4_), custom_call_target="tpu_custom_call" | custom-call | flops 805306368 | bytes 1572864 | tf_op jit(solution)/shard_map/expert/pallas_call | solution.py:261
  34.5 0.1 add.70.refs_3_
  34.6 2.2 %collective-permute-start.23 = (bf16[32,2048]{1,0:T(8,128)(2,1)S(1)}, bf16[32,2048]{1,0:T(8,128)(2,1)S(1)}, u32[]{:S(2)}, u32[]{:S(2)}) collective-permute-start(bf16[32,2048]{1,0:T(8,128)(2,1)S(1)} %slice.37), channel_id=1, source_target_pairs={{0,7},{1,6},{2,5},{3,4},{4,3},{5,2},{6,1},{7,0},{8,15},{9,14},{10,... | collective-permute-start | bytes 393224 | tf_op jit(solution)/shard_map/ppermute | solution.py:348
  36.8 1.6 %collective-permute-done.15.refs_1_ = bf16[64,2048]{1,0:T(8,128)(2,1)S(1)} collective-permute-done((bf16[64,2048]{1,0:T(8,128)(2,1)S(1)}, bf16[64,2048]{1,0:T(8,128)(2,1)S(1)}, u32[]{:S(2)}, u32[]{:S(2)}) %collective-permute-start.15) | collective-permute-done | bytes 262176 | tf_op jit(solution)/shard_map/ppermute | solution.py:343
  38.4 0.1 collective-permute-start.21
  38.5 3.3 %collective-permute-start.26 = (bf16[16,2048]{1,0:T(8,128)(2,1)S(1)}, bf16[16,2048]{1,0:T(8,128)(2,1)S(1)}, u32[]{:S(2)}, u32[]{:S(2)}) collective-permute-start(bf16[16,2048]{1,0:T(8,128)(2,1)S(1)} %get-tuple-element.43), channel_id=1, source_target_pairs={{0,7},{1,6},{2,5},{3,4},{4,3},{5,2},{6,1},{7,0},{8,15},{9,14},{10,... | collective-permute-start | bytes 196616 | tf_op jit(solution)/shard_map/ppermute | solution.py:348
  41.9 0.1 collective-permute-start.22
  41.9 0.1 convert_add_fusion
  42.1 3.0 %collective-permute-start.24 = (bf16[16,2048]{1,0:T(8,128)(2,1)S(1)}, bf16[16,2048]{1,0:T(8,128)(2,1)S(1)}, u32[]{:S(2)}, u32[]{:S(2)}) collective-permute-start(bf16[16,2048]{1,0:T(8,128)(2,1)S(1)} %get-tuple-element.44), channel_id=1, source_target_pairs={{0,24},{1,25},{2,26},{3,27},{4,28},{5,29},{6,30},{7,31},{8,16},{9,... | collective-permute-start | bytes 196616 | tf_op jit(solution)/shard_map/ppermute | solution.py:348
  45.1 1.6 %collective-permute-start.27 = (bf16[16,2048]{1,0:T(8,128)(2,1)S(1)}, bf16[16,2048]{1,0:T(8,128)(2,1)S(1)}, u32[]{:S(2)}, u32[]{:S(2)}) collective-permute-start(bf16[16,2048]{1,0:T(8,128)(2,1)S(1)} %fusion.1), channel_id=1, source_target_pairs={{0,8},{1,9},{2,10},{3,11},{4,12},{5,13},{6,14},{7,15},{8,0},{9,1},... | collective-permute-start | bytes 196616 | tf_op jit(solution)/shard_map/ppermute | solution.py:348
  46.6 0.6 %copy.13 = bf16[1,1,64,128]{3,1,2,0:T(2,128)(2,1)} copy(bf16[1,1,64,128]{3,2,1,0:T(8,128)(2,1)S(1)} %bitcast.11) | data formatting | bytes 32768
  47.3 1.5 %collective-permute-done.24 = bf16[16,2048]{1,0:T(8,128)(2,1)S(1)} collective-permute-done((bf16[16,2048]{1,0:T(8,128)(2,1)S(1)}, bf16[16,2048]{1,0:T(8,128)(2,1)S(1)}, u32[]{:S(2)}, u32[]{:S(2)}) %collective-permute-start.24) | collective-permute-done | bytes 65568 | tf_op jit(solution)/shard_map/ppermute | solution.py:348
  48.8 2.1 %collective-permute-done.25 = bf16[16,2048]{1,0:T(8,128)(2,1)S(1)} collective-permute-done((bf16[16,2048]{1,0:T(8,128)(2,1)S(1)}, bf16[16,2048]{1,0:T(8,128)(2,1)S(1)}, u32[]{:S(2)}, u32[]{:S(2)}) %collective-permute-start.25) | collective-permute-done | bytes 65568 | tf_op jit(solution)/shard_map/ppermute | solution.py:348
  50.9 0.0 collective-permute-done.27
  51.0 0.7 %fusion.5 = bf16[16,2048]{1,0:T(8,128)(2,1)} fusion(f32[64,2048]{1,0:T(8,128)S(1)} %convert_add_fusion, bf16[16,2048]{1,0:T(8,128)(2,1)S(1)} %collective-permute-done.27, bf16[16,2048]{1,0:T(8,128)(2,1)S(1)} %collective-permute-done.25, bf16[16,2048]{1,0:T(8,128)(2,1)S(1)} %collective-permute-done.24, bf16[16,2048]{1,0:T(8,128)(2,1)S(1)} %collective-permute-done.22), kind=kLoop, calls=%fused_computation.9 | loop fusion | flops 294912 | bytes 458752 | tf_op jit(solution)/shard_map/convert_element_type | solution.py:404
  (32 shorter events, 0.3 us)
Async XLA Ops:
  1.6 10.9 %collective-permute-start = (bf16[16,2176]{1,0:T(8,128)(2,1)S(1)}, bf16[16,2176]{1,0:T(8,128)(2,1)S(1)}, u32[]{:S(2)}, u32[]{:S(2)}) collective-permute-start(bf16[16,2176]{1,0:T(8,128)(2,1)S(1)} %label.1.refs_0_), channel_id=1, source_target_pairs={{0,8},{1,9},{2,10},{3,11},{4,12},{5,13},{6,14},{7,15},{8,0},{9,1},... | collective-permute-start | bytes 208904 | tf_op jit(solution)/shard_map/ppermute | solution.py:348
  4.7 7.8 %collective-permute-start.1 = (bf16[16,2176]{1,0:T(8,128)(2,1)S(1)}, bf16[16,2176]{1,0:T(8,128)(2,1)S(1)}, u32[]{:S(2)}, u32[]{:S(2)}) collective-permute-start(bf16[16,2176]{1,0:T(8,128)(2,1)S(1)} %label.1.refs_0_), channel_id=1, source_target_pairs={{0,16},{1,17},{2,18},{3,19},{4,20},{5,21},{6,22},{7,23},{8,24},{9,... | collective-permute-start | bytes 208904 | tf_op jit(solution)/shard_map/ppermute | solution.py:348
  7.3 6.2 %collective-permute-start.2 = (bf16[16,2176]{1,0:T(8,128)(2,1)S(1)}, bf16[16,2176]{1,0:T(8,128)(2,1)S(1)}, u32[]{:S(2)}, u32[]{:S(2)}) collective-permute-start(bf16[16,2176]{1,0:T(8,128)(2,1)S(1)} %label.1.refs_0_), channel_id=1, source_target_pairs={{0,24},{1,25},{2,26},{3,27},{4,28},{5,29},{6,30},{7,31},{8,16},{9,... | collective-permute-start | bytes 208904 | tf_op jit(solution)/shard_map/ppermute | solution.py:348
  7.9 0.8 %copy-start = (bf16[1,8192]{1,0:T(2,128)(2,1)S(1)}, bf16[1,8192]{1,0:T(2,128)(2,1)}, u32[]{:S(2)}) copy-start(bf16[1,8192]{1,0:T(2,128)(2,1)} %query_ref.1) | copy-start | bytes 49156
  13.5 1.6 %collective-permute-start.3 = (bf16[64,2176]{1,0:T(8,128)(2,1)S(1)}, bf16[64,2176]{1,0:T(8,128)(2,1)S(1)}, u32[]{:S(2)}, u32[]{:S(2)}) collective-permute-start(bf16[64,2176]{1,0:T(8,128)(2,1)S(1)} %stack.1.refs_0_), channel_id=1, source_target_pairs={{0,1},{1,0},{2,3},{3,2},{4,5},{5,4},{6,7},{7,6},{8,9},{9,8},{10,11... | collective-permute-start | bytes 835592 | tf_op jit(solution)/shard_map/ppermute | solution.py:348
  13.6 6.6 %collective-permute-start.4 = (bf16[64,2176]{1,0:T(8,128)(2,1)S(1)}, bf16[64,2176]{1,0:T(8,128)(2,1)S(1)}, u32[]{:S(2)}, u32[]{:S(2)}) collective-permute-start(bf16[64,2176]{1,0:T(8,128)(2,1)S(1)} %stack.1.refs_0_), channel_id=1, source_target_pairs={{0,2},{1,5},{2,0},{3,7},{4,6},{5,1},{6,4},{7,3},{8,10},{9,13},{10,... | collective-permute-start | bytes 835592 | tf_op jit(solution)/shard_map/ppermute | solution.py:343
  15.1 8.0 %collective-permute-start.10 = (bf16[64,2176]{1,0:T(8,128)(2,1)S(1)}, bf16[64,2176]{1,0:T(8,128)(2,1)S(1)}, u32[]{:S(2)}, u32[]{:S(2)}) collective-permute-start(bf16[64,2176]{1,0:T(8,128)(2,1)S(1)} %collective-permute-done.3.refs_1_), channel_id=1, source_target_pairs={{0,2},{1,5},{2,0},{3,7},{4,6},{5,1},{6,4},{7,3},{8,10},{9,13},{10,... | collective-permute-start | bytes 835592 | tf_op jit(solution)/shard_map/ppermute | solution.py:343
  20.2 3.6 %collective-permute-start.5 = (bf16[32,2176]{1,0:T(8,128)(2,1)S(1)}, bf16[32,2176]{1,0:T(8,128)(2,1)S(1)}, u32[]{:S(2)}, u32[]{:S(2)}) collective-permute-start(bf16[32,2176]{1,0:T(8,128)(2,1)S(1)} %get-tuple-element.26), channel_id=1, source_target_pairs={{0,1},{1,0},{2,3},{3,2},{4,5},{5,4},{6,7},{7,6},{8,9},{9,8},{10,11... | collective-permute-start | bytes 417800 | tf_op jit(solution)/shard_map/ppermute | solution.py:348
  20.3 3.5 %collective-permute-start.6 = (bf16[32,2176]{1,0:T(8,128)(2,1)S(1)}, bf16[32,2176]{1,0:T(8,128)(2,1)S(1)}, u32[]{:S(2)}, u32[]{:S(2)}) collective-permute-start(bf16[32,2176]{1,0:T(8,128)(2,1)S(1)} %get-tuple-element.27), channel_id=1, source_target_pairs={{0,1},{1,0},{2,3},{3,2},{4,5},{5,4},{6,7},{7,6},{8,9},{9,8},{10,11... | collective-permute-start | bytes 417800 | tf_op jit(solution)/shard_map/ppermute | solution.py:348
  20.8 7.8 %collective-permute-start.16 = (bf16[64,2176]{1,0:T(8,128)(2,1)S(1)}, bf16[64,2176]{1,0:T(8,128)(2,1)S(1)}, u32[]{:S(2)}, u32[]{:S(2)}) collective-permute-start(bf16[64,2176]{1,0:T(8,128)(2,1)S(1)} %collective-permute-done.4.block_ref.refs_0_), channel_id=1, source_target_pairs={{0,5},{1,2},{2,7},{3,0},{4,1},{5,6},{6,3},{7,4},{8,13},{9,10},{10,... | collective-permute-start | bytes 835592 | tf_op jit(solution)/shard_map/ppermute | solution.py:343
  23.2 3.5 %collective-permute-start.11 = (bf16[32,2176]{1,0:T(8,128)(2,1)S(1)}, bf16[32,2176]{1,0:T(8,128)(2,1)S(1)}, u32[]{:S(2)}, u32[]{:S(2)}) collective-permute-start(bf16[32,2176]{1,0:T(8,128)(2,1)S(1)} %get-tuple-element.32), channel_id=1, source_target_pairs={{0,1},{1,0},{2,3},{3,2},{4,5},{5,4},{6,7},{7,6},{8,9},{9,8},{10,11... | collective-permute-start | bytes 417800 | tf_op jit(solution)/shard_map/ppermute | solution.py:348
  23.3 3.4 %collective-permute-start.12 = (bf16[32,2176]{1,0:T(8,128)(2,1)S(1)}, bf16[32,2176]{1,0:T(8,128)(2,1)S(1)}, u32[]{:S(2)}, u32[]{:S(2)}) collective-permute-start(bf16[32,2176]{1,0:T(8,128)(2,1)S(1)} %get-tuple-element.33), channel_id=1, source_target_pairs={{0,1},{1,0},{2,3},{3,2},{4,5},{5,4},{6,7},{7,6},{8,9},{9,8},{10,11... | collective-permute-start | bytes 417800 | tf_op jit(solution)/shard_map/ppermute | solution.py:348
  25.1 1.4 %collective-permute-start.7 = (bf16[32,2048]{1,0:T(8,128)(2,1)S(1)}, bf16[32,2048]{1,0:T(8,128)(2,1)S(1)}, u32[]{:S(2)}, u32[]{:S(2)}) collective-permute-start(bf16[32,2048]{1,0:T(8,128)(2,1)S(1)} %get-tuple-element.29), channel_id=1, source_target_pairs={{0,1},{1,0},{2,3},{3,2},{4,5},{5,4},{6,7},{7,6},{8,9},{9,8},{10,11... | collective-permute-start | bytes 393224 | tf_op jit(solution)/shard_map/ppermute | solution.py:348
  25.2 1.5 %collective-permute-start.8 = (bf16[32,2048]{1,0:T(8,128)(2,1)S(1)}, bf16[32,2048]{1,0:T(8,128)(2,1)S(1)}, u32[]{:S(2)}, u32[]{:S(2)}) collective-permute-start(bf16[32,2048]{1,0:T(8,128)(2,1)S(1)} %get-tuple-element.30), channel_id=1, source_target_pairs={{0,1},{1,0},{2,3},{3,2},{4,5},{5,4},{6,7},{7,6},{8,9},{9,8},{10,11... | collective-permute-start | bytes 393224 | tf_op jit(solution)/shard_map/ppermute | solution.py:348
  28.0 2.7 %collective-permute-start.13 = (bf16[32,2048]{1,0:T(8,128)(2,1)S(1)}, bf16[32,2048]{1,0:T(8,128)(2,1)S(1)}, u32[]{:S(2)}, u32[]{:S(2)}) collective-permute-start(bf16[32,2048]{1,0:T(8,128)(2,1)S(1)} %get-tuple-element.35), channel_id=1, source_target_pairs={{0,1},{1,0},{2,3},{3,2},{4,5},{5,4},{6,7},{7,6},{8,9},{9,8},{10,11... | collective-permute-start | bytes 393224 | tf_op jit(solution)/shard_map/ppermute | solution.py:348
  28.4 2.3 %collective-permute-start.14 = (bf16[32,2048]{1,0:T(8,128)(2,1)S(1)}, bf16[32,2048]{1,0:T(8,128)(2,1)S(1)}, u32[]{:S(2)}, u32[]{:S(2)}) collective-permute-start(bf16[32,2048]{1,0:T(8,128)(2,1)S(1)} %get-tuple-element.36), channel_id=1, source_target_pairs={{0,1},{1,0},{2,3},{3,2},{4,5},{5,4},{6,7},{7,6},{8,9},{9,8},{10,11... | collective-permute-start | bytes 393224 | tf_op jit(solution)/shard_map/ppermute | solution.py:348
  28.6 2.8 %collective-permute-start.17 = (bf16[32,2176]{1,0:T(8,128)(2,1)S(1)}, bf16[32,2176]{1,0:T(8,128)(2,1)S(1)}, u32[]{:S(2)}, u32[]{:S(2)}) collective-permute-start(bf16[32,2176]{1,0:T(8,128)(2,1)S(1)} %get-tuple-element.37), channel_id=1, source_target_pairs={{0,1},{1,0},{2,3},{3,2},{4,5},{5,4},{6,7},{7,6},{8,9},{9,8},{10,11... | collective-permute-start | bytes 417800 | tf_op jit(solution)/shard_map/ppermute | solution.py:348
  29.0 2.4 %collective-permute-start.18 = (bf16[32,2176]{1,0:T(8,128)(2,1)S(1)}, bf16[32,2176]{1,0:T(8,128)(2,1)S(1)}, u32[]{:S(2)}, u32[]{:S(2)}) collective-permute-start(bf16[32,2176]{1,0:T(8,128)(2,1)S(1)} %get-tuple-element.38), channel_id=1, source_target_pairs={{0,1},{1,0},{2,3},{3,2},{4,5},{5,4},{6,7},{7,6},{8,9},{9,8},{10,11... | collective-permute-start | bytes 417800 | tf_op jit(solution)/shard_map/ppermute | solution.py:348
  29.2 7.6 %collective-permute-start.9 = (bf16[64,2048]{1,0:T(8,128)(2,1)S(1)}, bf16[64,2048]{1,0:T(8,128)(2,1)S(1)}, u32[]{:S(2)}, u32[]{:S(2)}) collective-permute-start(bf16[64,2048]{1,0:T(8,128)(2,1)S(1)} %add.68.refs_5_), channel_id=1, source_target_pairs={{0,2},{1,5},{2,0},{3,7},{4,6},{5,1},{6,4},{7,3},{8,10},{9,13},{10,... | collective-permute-start | bytes 786440 | tf_op jit(solution)/shard_map/ppermute | solution.py:343
  30.8 7.6 %collective-permute-start.15 = (bf16[64,2048]{1,0:T(8,128)(2,1)S(1)}, bf16[64,2048]{1,0:T(8,128)(2,1)S(1)}, u32[]{:S(2)}, u32[]{:S(2)}) collective-permute-start(bf16[64,2048]{1,0:T(8,128)(2,1)S(1)} %add.69.refs_5_), channel_id=1, source_target_pairs={{0,2},{1,5},{2,0},{3,7},{4,6},{5,1},{6,4},{7,3},{8,10},{9,13},{10,... | collective-permute-start | bytes 786440 | tf_op jit(solution)/shard_map/ppermute | solution.py:343
  32.7 1.9 %collective-permute-start.19 = (bf16[32,2048]{1,0:T(8,128)(2,1)S(1)}, bf16[32,2048]{1,0:T(8,128)(2,1)S(1)}, u32[]{:S(2)}, u32[]{:S(2)}) collective-permute-start(bf16[32,2048]{1,0:T(8,128)(2,1)S(1)} %get-tuple-element.40), channel_id=1, source_target_pairs={{0,1},{1,0},{2,3},{3,2},{4,5},{5,4},{6,7},{7,6},{8,9},{9,8},{10,11... | collective-permute-start | bytes 393224 | tf_op jit(solution)/shard_map/ppermute | solution.py:348
  32.7 1.8 %collective-permute-start.20 = (bf16[32,2048]{1,0:T(8,128)(2,1)S(1)}, bf16[32,2048]{1,0:T(8,128)(2,1)S(1)}, u32[]{:S(2)}, u32[]{:S(2)}) collective-permute-start(bf16[32,2048]{1,0:T(8,128)(2,1)S(1)} %get-tuple-element.41), channel_id=1, source_target_pairs={{0,1},{1,0},{2,3},{3,2},{4,5},{5,4},{6,7},{7,6},{8,9},{9,8},{10,11... | collective-permute-start | bytes 393224 | tf_op jit(solution)/shard_map/ppermute | solution.py:348
  34.6 7.4 %collective-permute-start.23 = (bf16[32,2048]{1,0:T(8,128)(2,1)S(1)}, bf16[32,2048]{1,0:T(8,128)(2,1)S(1)}, u32[]{:S(2)}, u32[]{:S(2)}) collective-permute-start(bf16[32,2048]{1,0:T(8,128)(2,1)S(1)} %slice.37), channel_id=1, source_target_pairs={{0,7},{1,6},{2,5},{3,4},{4,3},{5,2},{6,1},{7,0},{8,15},{9,14},{10,... | collective-permute-start | bytes 393224 | tf_op jit(solution)/shard_map/ppermute | solution.py:348
  38.4 3.5 %collective-permute-start.21 = (bf16[64,2048]{1,0:T(8,128)(2,1)S(1)}, bf16[64,2048]{1,0:T(8,128)(2,1)S(1)}, u32[]{:S(2)}, u32[]{:S(2)}) collective-permute-start(bf16[64,2048]{1,0:T(8,128)(2,1)S(1)} %add.71), channel_id=1, source_target_pairs={{0,1},{1,0},{2,3},{3,2},{4,5},{5,4},{6,7},{7,6},{8,9},{9,8},{10,11... | collective-permute-start | bytes 786440 | tf_op jit(solution)/shard_map/ppermute | solution.py:348
  38.5 6.5 %collective-permute-start.26 = (bf16[16,2048]{1,0:T(8,128)(2,1)S(1)}, bf16[16,2048]{1,0:T(8,128)(2,1)S(1)}, u32[]{:S(2)}, u32[]{:S(2)}) collective-permute-start(bf16[16,2048]{1,0:T(8,128)(2,1)S(1)} %get-tuple-element.43), channel_id=1, source_target_pairs={{0,7},{1,6},{2,5},{3,4},{4,3},{5,2},{6,1},{7,0},{8,15},{9,14},{10,... | collective-permute-start | bytes 196616 | tf_op jit(solution)/shard_map/ppermute | solution.py:348
  41.9 5.4 %collective-permute-start.22 = (bf16[16,2048]{1,0:T(8,128)(2,1)S(1)}, bf16[16,2048]{1,0:T(8,128)(2,1)S(1)}, u32[]{:S(2)}, u32[]{:S(2)}) collective-permute-start(bf16[16,2048]{1,0:T(8,128)(2,1)S(1)} %get-tuple-element.42), channel_id=1, source_target_pairs={{0,7},{1,6},{2,5},{3,4},{4,3},{5,2},{6,1},{7,0},{8,15},{9,14},{10,... | collective-permute-start | bytes 196616 | tf_op jit(solution)/shard_map/ppermute | solution.py:348
  42.1 6.7 %collective-permute-start.24 = (bf16[16,2048]{1,0:T(8,128)(2,1)S(1)}, bf16[16,2048]{1,0:T(8,128)(2,1)S(1)}, u32[]{:S(2)}, u32[]{:S(2)}) collective-permute-start(bf16[16,2048]{1,0:T(8,128)(2,1)S(1)} %get-tuple-element.44), channel_id=1, source_target_pairs={{0,24},{1,25},{2,26},{3,27},{4,28},{5,29},{6,30},{7,31},{8,16},{9,... | collective-permute-start | bytes 196616 | tf_op jit(solution)/shard_map/ppermute | solution.py:348
  45.0 5.9 %collective-permute-start.25 = (bf16[16,2048]{1,0:T(8,128)(2,1)S(1)}, bf16[16,2048]{1,0:T(8,128)(2,1)S(1)}, u32[]{:S(2)}, u32[]{:S(2)}) collective-permute-start(bf16[16,2048]{1,0:T(8,128)(2,1)S(1)} %get-tuple-element.45), channel_id=1, source_target_pairs={{0,16},{1,17},{2,18},{3,19},{4,20},{5,21},{6,22},{7,23},{8,24},{9,... | collective-permute-start | bytes 196616 | tf_op jit(solution)/shard_map/ppermute | solution.py:348
  45.1 5.9 %collective-permute-start.27 = (bf16[16,2048]{1,0:T(8,128)(2,1)S(1)}, bf16[16,2048]{1,0:T(8,128)(2,1)S(1)}, u32[]{:S(2)}, u32[]{:S(2)}) collective-permute-start(bf16[16,2048]{1,0:T(8,128)(2,1)S(1)} %fusion.1), channel_id=1, source_target_pairs={{0,8},{1,9},{2,10},{3,11},{4,12},{5,13},{6,14},{7,15},{8,0},{9,1},... | collective-permute-start | bytes 196616 | tf_op jit(solution)/shard_map/ppermute | solution.py:348

commit v5 on v4

--- a/solution.py
+++ b/solution.py
@@ -380,7 +380,7 @@
     kept_a, *sent_a = gated([side_a] + to_pair(side_a, []), split)
     sum_a = add_parts(kept_a, [swap(part, 1) for part in sent_a])
     got_a = cross(sum_a, 2, 4)
-    kept_b, *sent_b = gated([side_b] + to_pair(side_b, []), split, [sum_a])
+    kept_b, *sent_b = gated([side_b] + to_pair(side_b, [kept_a]), split, [sum_a])
     sum_b = add_parts(kept_b, [swap(part, 1) for part in sent_b])
     got_b = cross(sum_b, 2, 4)
     kept_c, *sent_c = gated([corner] + to_pair(corner), split, [sum_b])

time: 51.9 us -> 50.7 us (0.977)
  waiting for transfers between devices: 12.1 us -> 11.5 us
  starting transfers between devices: 25.7 us -> 25.1 us
    ppermute x5, waiting for transfers between devices: 6.35 us -> 5.41 us  [cross(): return lax.ppermute(block, 'expert', pairs)]
    ppermute x23, starting transfers between devices: 19.3 us -> 18.8 us  [swap(): lax.ppermute(block, 'expert', [(i, i ^ distance) for i in range(count)])]
  transfers between devices with their start and end apart: 28 -> 28, of which waited for: 8 -> 7; matrix products, arithmetic and copies ran while one was open for 2% -> 2% of each run, Pallas kernels for 18% -> 18%
where the time goes in v5:
time: 50.7 us; the launch traced here: 50.4 us
  starting transfers between devices  25.1 us (50%)
  waiting for transfers between devices  11.5 us (23%)
  Pallas kernels  10.1 us (20%)
  between operations  1.53 us (3%)
  local copies, waits for them, and re-layouts  1.43 us (3%)
  other arithmetic  0.79 us (2%)
    ppermute x23, starting transfers between devices, swap(): lax.ppermute(block, 'expert', [(i, i ^ distance) for i in range(count)])  18.8 us
    ppermute x5, starting transfers between devices, cross(): return lax.ppermute(block, 'expert', pairs)  6.33 us
    ppermute x23, waiting for transfers between devices, swap(): lax.ppermute(block, 'expert', [(i, i ^ distance) for i in range(count)])  6.05 us
    ppermute x5, waiting for transfers between devices, cross(): return lax.ppermute(block, 'expert', pairs)  5.41 us
    pallas_call x4, Pallas kernels, run_expert(): pl.pallas_call(functools.partial(expert_kernel, len(parts), len(after)),...  5.09 us
    pallas_call x1, Pallas kernels, attend_and_fetch(): pl.pallas_call(attend_kernel, out_shape=[jax.ShapeDtypeStruct((head_count...  3.79 us
    unnamed x3, local copies, waits for them, and re-layouts  1.39 us
  transfers between devices with their start and end apart: 28, of which 7 were waited for; matrix products, arithmetic and copies ran while one was open for 2% of the time, Pallas kernels for 18%

profile of v5, /device:TPU:0, one launch (start us, length us, event | category | flops | bytes accessed | tf_op | source)
XLA Modules:
  0.0 50.4 jit_solution(16621262082675733386)
XLA Ops:
  0.6 1.0 %label.1.refs_0_ = bf16[16,2176]{1,0:T(8,128)(2,1)S(1)} custom-call(bf16[16,2048]{1,0:T(8,128)(2,1)} %tokens_hbm.1, s32[8,16]{1,0:T(8,128)} %bitcast.17, bf16[8,16]{1,0:T(8,128)(2,1)} %bitcast.18), custom_call_target="tpu_custom_call" | custom-call | tf_op jit(solution)/shard_map/label/pallas_call | solution.py:136
  1.6 3.1 %collective-permute-start = (bf16[16,2176]{1,0:T(8,128)(2,1)S(1)}, bf16[16,2176]{1,0:T(8,128)(2,1)S(1)}, u32[]{:S(2)}, u32[]{:S(2)}) collective-permute-start(bf16[16,2176]{1,0:T(8,128)(2,1)S(1)} %label.1.refs_0_), channel_id=1, source_target_pairs={{0,8},{1,9},{2,10},{3,11},{4,12},{5,13},{6,14},{7,15},{8,0},{9,1},... | collective-permute-start | bytes 208904 | tf_op jit(solution)/shard_map/ppermute | solution.py:348
  4.7 2.6 %collective-permute-start.1 = (bf16[16,2176]{1,0:T(8,128)(2,1)S(1)}, bf16[16,2176]{1,0:T(8,128)(2,1)S(1)}, u32[]{:S(2)}, u32[]{:S(2)}) collective-permute-start(bf16[16,2176]{1,0:T(8,128)(2,1)S(1)} %label.1.refs_0_), channel_id=1, source_target_pairs={{0,16},{1,17},{2,18},{3,19},{4,20},{5,21},{6,22},{7,23},{8,24},{9,... | collective-permute-start | bytes 208904 | tf_op jit(solution)/shard_map/ppermute | solution.py:348
  7.9 0.0 copy-start
  7.9 0.7 %copy-done = bf16[1,8192]{1,0:T(2,128)(2,1)S(1)} copy-done((bf16[1,8192]{1,0:T(2,128)(2,1)S(1)}, bf16[1,8192]{1,0:T(2,128)(2,1)}, u32[]{:S(2)}) %copy-start) | copy-done | bytes 16408
  8.7 3.8 %attention.1 = (bf16[64,128]{1,0:T(8,128)(2,1)S(1)}, bf16[2048,768]{1,0:T(8,128)(2,1)S(1)}, bf16[768,2048]{1,0:T(8,128)(2,1)S(1)}) custom-call(s32[1]{0:T(128)S(6)} %copy.14.lengths_ref, bf16[1,8192]{1,0:T(2,128)(2,1)S(1)} %copy-done, bf16[1536,512]{1,0:T(8,128)(2,1)} %bitcast.14, bf16[1536,512]{1,0:T(8,128)(2,1)} %bitcast.15, bf16[2048,768]{1,0:T(8,128)(2,1)} %bitcast.12, ...), custom_call_target="tpu_custom_call" | custom-call | flops 50331648 | bytes 15728640 | tf_op jit(solution)/shard_map/attention/pallas_call | solution.py:191
  12.5 1.0 %collective-permute-done.2.refs_3_ = bf16[16,2176]{1,0:T(8,128)(2,1)S(1)} collective-permute-done((bf16[16,2176]{1,0:T(8,128)(2,1)S(1)}, bf16[16,2176]{1,0:T(8,128)(2,1)S(1)}, u32[]{:S(2)}, u32[]{:S(2)}) %collective-permute-start.2) | collective-permute-done | bytes 69664 | tf_op jit(solution)/shard_map/ppermute | solution.py:348
  13.5 0.1 collective-permute-start.3
  13.6 1.6 %collective-permute-start.4 = (bf16[64,2176]{1,0:T(8,128)(2,1)S(1)}, bf16[64,2176]{1,0:T(8,128)(2,1)S(1)}, u32[]{:S(2)}, u32[]{:S(2)}) collective-permute-start(bf16[64,2176]{1,0:T(8,128)(2,1)S(1)} %stack.1.refs_0_), channel_id=1, source_target_pairs={{0,2},{1,5},{2,0},{3,7},{4,6},{5,1},{6,4},{7,3},{8,10},{9,13},{10,... | collective-permute-start | bytes 835592 | tf_op jit(solution)/shard_map/ppermute | solution.py:343
  15.1 1.5 %collective-permute-start.10 = (bf16[64,2176]{1,0:T(8,128)(2,1)S(1)}, bf16[64,2176]{1,0:T(8,128)(2,1)S(1)}, u32[]{:S(2)}, u32[]{:S(2)}) collective-permute-start(bf16[64,2176]{1,0:T(8,128)(2,1)S(1)} %collective-permute-done.3.refs_1_), channel_id=1, source_target_pairs={{0,2},{1,5},{2,0},{3,7},{4,6},{5,1},{6,4},{7,3},{8,10},{9,13},{10,... | collective-permute-start | bytes 835592 | tf_op jit(solution)/shard_map/ppermute | solution.py:343
  16.6 3.6 %collective-permute-done.4.block_ref.refs_0_ = bf16[64,2176]{1,0:T(8,128)(2,1)S(1)} collective-permute-done((bf16[64,2176]{1,0:T(8,128)(2,1)S(1)}, bf16[64,2176]{1,0:T(8,128)(2,1)S(1)}, u32[]{:S(2)}, u32[]{:S(2)}) %collective-permute-start.4) | collective-permute-done | bytes 278560 | tf_op jit(solution)/shard_map/ppermute | solution.py:343
  20.2 0.1 collective-permute-start.5
  20.3 0.5 collective-permute-start.6
  20.8 1.2 %collective-permute-start.16 = (bf16[64,2176]{1,0:T(8,128)(2,1)S(1)}, bf16[64,2176]{1,0:T(8,128)(2,1)S(1)}, u32[]{:S(2)}, u32[]{:S(2)}) collective-permute-start(bf16[64,2176]{1,0:T(8,128)(2,1)S(1)} %collective-permute-done.4.block_ref.refs_0_), channel_id=1, source_target_pairs={{0,5},{1,2},{2,7},{3,0},{4,1},{5,6},{6,3},{7,4},{8,13},{9,10},{10,... | collective-permute-start | bytes 835592 | tf_op jit(solution)/shard_map/ppermute | solution.py:343
  22.0 1.3 %expert.5 = (f32[64,2048]{1,0:T(8,128)S(1)}, bf16[32,2048]{1,0:T(8,128)(2,1)S(1)}, bf16[32,2048]{1,0:T(8,128)(2,1)S(1)}) custom-call(bf16[64,2176]{1,0:T(8,128)(2,1)S(1)} %collective-permute-done.4.block_ref.refs_0_, bf16[32,2176]{1,0:T(8,128)(2,1)S(1)} %collective-permute-done.5.refs_1_, bf16[32,2176]{1,0:T(8,128)(2,1)S(1)} %collective-permute-done.6.refs_2_, ...), custom_call_target="tpu_custom_call" | custom-call | flops 805306368 | bytes 1572864 | tf_op jit(solution)/shard_map/expert/pallas_call | solution.py:261
  23.3 0.5 collective-permute-start.11
  23.8 0.1 collective-permute-start.12
  23.9 0.4 collective-permute-start.7
  24.3 0.1 collective-permute-start.8
  24.4 0.9 %collective-permute-done.7.refs_1_ = bf16[32,2048]{1,0:T(8,128)(2,1)S(1)} collective-permute-done((bf16[32,2048]{1,0:T(8,128)(2,1)S(1)}, bf16[32,2048]{1,0:T(8,128)(2,1)S(1)}, u32[]{:S(2)}, u32[]{:S(2)}) %collective-permute-start.7) | collective-permute-done | bytes 131104 | tf_op jit(solution)/shard_map/ppermute | solution.py:348
  25.3 0.3 collective-permute-done.8.refs_2_
  25.6 0.1 add.68.refs_5_
  25.7 1.3 %expert.6 = (f32[64,2048]{1,0:T(8,128)S(1)}, bf16[32,2048]{1,0:T(8,128)(2,1)S(1)}, bf16[32,2048]{1,0:T(8,128)(2,1)S(1)}) custom-call(bf16[64,2176]{1,0:T(8,128)(2,1)S(1)} %collective-permute-done.10.block_ref.refs_0_, bf16[32,2176]{1,0:T(8,128)(2,1)S(1)} %collective-permute-done.11.refs_1_, bf16[32,2176]{1,0:T(8,128)(2,1)S(1)} %collective-permute-done.12.refs_2_, ...), custom_call_target="tpu_custom_call" | custom-call | flops 805306368 | bytes 1572864 | tf_op jit(solution)/shard_map/expert/pallas_call | solution.py:261
  27.0 0.3 collective-permute-start.13
  27.3 0.3 collective-permute-start.14
  27.6 0.3 collective-permute-start.17
  27.9 0.3 collective-permute-start.18
  28.2 1.3 %collective-permute-start.9 = (bf16[64,2048]{1,0:T(8,128)(2,1)S(1)}, bf16[64,2048]{1,0:T(8,128)(2,1)S(1)}, u32[]{:S(2)}, u32[]{:S(2)}) collective-permute-start(bf16[64,2048]{1,0:T(8,128)(2,1)S(1)} %add.68.refs_5_), channel_id=1, source_target_pairs={{0,2},{1,5},{2,0},{3,7},{4,6},{5,1},{6,4},{7,3},{8,10},{9,13},{10,... | collective-permute-start | bytes 786440 | tf_op jit(solution)/shard_map/ppermute | solution.py:343
  29.5 0.1 add.69.refs_5_
  29.5 0.8 %collective-permute-start.15 = (bf16[64,2048]{1,0:T(8,128)(2,1)S(1)}, bf16[64,2048]{1,0:T(8,128)(2,1)S(1)}, u32[]{:S(2)}, u32[]{:S(2)}) collective-permute-start(bf16[64,2048]{1,0:T(8,128)(2,1)S(1)} %add.69.refs_5_), channel_id=1, source_target_pairs={{0,2},{1,5},{2,0},{3,7},{4,6},{5,1},{6,4},{7,3},{8,10},{9,13},{10,... | collective-permute-start | bytes 786440 | tf_op jit(solution)/shard_map/ppermute | solution.py:343
  30.4 1.3 %expert.7 = (f32[64,2048]{1,0:T(8,128)S(1)}, bf16[32,2048]{1,0:T(8,128)(2,1)S(1)}, bf16[32,2048]{1,0:T(8,128)(2,1)S(1)}) custom-call(bf16[64,2176]{1,0:T(8,128)(2,1)S(1)} %collective-permute-done.16.block_ref.refs_0_, bf16[32,2176]{1,0:T(8,128)(2,1)S(1)} %collective-permute-done.17.refs_1_, bf16[32,2176]{1,0:T(8,128)(2,1)S(1)} %collective-permute-done.18.refs_2_, ...), custom_call_target="tpu_custom_call" | custom-call | flops 805306368 | bytes 1572864 | tf_op jit(solution)/shard_map/expert/pallas_call | solution.py:261
  31.6 0.1 collective-permute-start.19
  31.7 0.5 collective-permute-start.20
  32.2 1.3 %expert.4 = (f32[64,2048]{1,0:T(8,128)S(1)}, f32[64,2048]{1,0:T(8,128)S(1)}) custom-call(bf16[64,2176]{1,0:T(8,128)(2,1)S(1)} %stack.1.refs_0_, bf16[64,2176]{1,0:T(8,128)(2,1)S(1)} %collective-permute-done.3.refs_1_, bf16[2048,768]{1,0:T(8,128)(2,1)S(1)} %get-tuple-element.23.refs_2_.refs_3_, bf16[768,2048]{1,0:T(8,128)(2,1)S(1)} %get-tuple-element.24.refs_3_.refs_4_), custom_call_target="tpu_custom_call" | custom-call | flops 805306368 | bytes 1572864 | tf_op jit(solution)/shard_map/expert/pallas_call | solution.py:261
  33.5 0.1 add.70.refs_3_
  33.6 1.9 %collective-permute-start.23 = (bf16[32,2048]{1,0:T(8,128)(2,1)S(1)}, bf16[32,2048]{1,0:T(8,128)(2,1)S(1)}, u32[]{:S(2)}, u32[]{:S(2)}) collective-permute-start(bf16[32,2048]{1,0:T(8,128)(2,1)S(1)} %slice.37), channel_id=1, source_target_pairs={{0,7},{1,6},{2,5},{3,4},{4,3},{5,2},{6,1},{7,0},{8,15},{9,14},{10,... | collective-permute-start | bytes 393224 | tf_op jit(solution)/shard_map/ppermute | solution.py:348
  35.5 1.8 %collective-permute-done.15.refs_1_ = bf16[64,2048]{1,0:T(8,128)(2,1)S(1)} collective-permute-done((bf16[64,2048]{1,0:T(8,128)(2,1)S(1)}, bf16[64,2048]{1,0:T(8,128)(2,1)S(1)}, u32[]{:S(2)}, u32[]{:S(2)}) %collective-permute-start.15) | collective-permute-done | bytes 262176 | tf_op jit(solution)/shard_map/ppermute | solution.py:343
  37.4 0.1 collective-permute-start.21
  37.5 3.0 %collective-permute-start.26 = (bf16[16,2048]{1,0:T(8,128)(2,1)S(1)}, bf16[16,2048]{1,0:T(8,128)(2,1)S(1)}, u32[]{:S(2)}, u32[]{:S(2)}) collective-permute-start(bf16[16,2048]{1,0:T(8,128)(2,1)S(1)} %get-tuple-element.43), channel_id=1, source_target_pairs={{0,7},{1,6},{2,5},{3,4},{4,3},{5,2},{6,1},{7,0},{8,15},{9,14},{10,... | collective-permute-start | bytes 196616 | tf_op jit(solution)/shard_map/ppermute | solution.py:348
  40.6 0.1 collective-permute-start.22
  40.7 0.1 convert_add_fusion
  40.8 2.9 %collective-permute-start.24 = (bf16[16,2048]{1,0:T(8,128)(2,1)S(1)}, bf16[16,2048]{1,0:T(8,128)(2,1)S(1)}, u32[]{:S(2)}, u32[]{:S(2)}) collective-permute-start(bf16[16,2048]{1,0:T(8,128)(2,1)S(1)} %get-tuple-element.44), channel_id=1, source_target_pairs={{0,24},{1,25},{2,26},{3,27},{4,28},{5,29},{6,30},{7,31},{8,16},{9,... | collective-permute-start | bytes 196616 | tf_op jit(solution)/shard_map/ppermute | solution.py:348
  43.7 1.6 %collective-permute-start.27 = (bf16[16,2048]{1,0:T(8,128)(2,1)S(1)}, bf16[16,2048]{1,0:T(8,128)(2,1)S(1)}, u32[]{:S(2)}, u32[]{:S(2)}) collective-permute-start(bf16[16,2048]{1,0:T(8,128)(2,1)S(1)} %fusion.1), channel_id=1, source_target_pairs={{0,8},{1,9},{2,10},{3,11},{4,12},{5,13},{6,14},{7,15},{8,0},{9,1},... | collective-permute-start | bytes 196616 | tf_op jit(solution)/shard_map/ppermute | solution.py:348
  45.3 0.6 %copy.13 = bf16[1,1,64,128]{3,1,2,0:T(2,128)(2,1)} copy(bf16[1,1,64,128]{3,2,1,0:T(8,128)(2,1)S(1)} %bitcast.11) | data formatting | bytes 32768
  46.0 1.6 %collective-permute-done.24 = bf16[16,2048]{1,0:T(8,128)(2,1)S(1)} collective-permute-done((bf16[16,2048]{1,0:T(8,128)(2,1)S(1)}, bf16[16,2048]{1,0:T(8,128)(2,1)S(1)}, u32[]{:S(2)}, u32[]{:S(2)}) %collective-permute-start.24) | collective-permute-done | bytes 65568 | tf_op jit(solution)/shard_map/ppermute | solution.py:348
  47.6 2.1 %collective-permute-done.25 = bf16[16,2048]{1,0:T(8,128)(2,1)S(1)} collective-permute-done((bf16[16,2048]{1,0:T(8,128)(2,1)S(1)}, bf16[16,2048]{1,0:T(8,128)(2,1)S(1)}, u32[]{:S(2)}, u32[]{:S(2)}) %collective-permute-start.25) | collective-permute-done | bytes 65568 | tf_op jit(solution)/shard_map/ppermute | solution.py:348
  49.7 0.0 collective-permute-done.27
  49.8 0.7 %fusion.5 = bf16[16,2048]{1,0:T(8,128)(2,1)} fusion(f32[64,2048]{1,0:T(8,128)S(1)} %convert_add_fusion, bf16[16,2048]{1,0:T(8,128)(2,1)S(1)} %collective-permute-done.27, bf16[16,2048]{1,0:T(8,128)(2,1)S(1)} %collective-permute-done.25, bf16[16,2048]{1,0:T(8,128)(2,1)S(1)} %collective-permute-done.24, bf16[16,2048]{1,0:T(8,128)(2,1)S(1)} %collective-permute-done.22), kind=kLoop, calls=%fused_computation.9 | loop fusion | flops 294912 | bytes 458752 | tf_op jit(solution)/shard_map/convert_element_type | solution.py:404
  (32 shorter events, 0.3 us)
Async XLA Ops:
  1.6 10.9 %collective-permute-start = (bf16[16,2176]{1,0:T(8,128)(2,1)S(1)}, bf16[16,2176]{1,0:T(8,128)(2,1)S(1)}, u32[]{:S(2)}, u32[]{:S(2)}) collective-permute-start(bf16[16,2176]{1,0:T(8,128)(2,1)S(1)} %label.1.refs_0_), channel_id=1, source_target_pairs={{0,8},{1,9},{2,10},{3,11},{4,12},{5,13},{6,14},{7,15},{8,0},{9,1},... | collective-permute-start | bytes 208904 | tf_op jit(solution)/shard_map/ppermute | solution.py:348
  4.7 7.8 %collective-permute-start.1 = (bf16[16,2176]{1,0:T(8,128)(2,1)S(1)}, bf16[16,2176]{1,0:T(8,128)(2,1)S(1)}, u32[]{:S(2)}, u32[]{:S(2)}) collective-permute-start(bf16[16,2176]{1,0:T(8,128)(2,1)S(1)} %label.1.refs_0_), channel_id=1, source_target_pairs={{0,16},{1,17},{2,18},{3,19},{4,20},{5,21},{6,22},{7,23},{8,24},{9,... | collective-permute-start | bytes 208904 | tf_op jit(solution)/shard_map/ppermute | solution.py:348
  7.3 6.2 %collective-permute-start.2 = (bf16[16,2176]{1,0:T(8,128)(2,1)S(1)}, bf16[16,2176]{1,0:T(8,128)(2,1)S(1)}, u32[]{:S(2)}, u32[]{:S(2)}) collective-permute-start(bf16[16,2176]{1,0:T(8,128)(2,1)S(1)} %label.1.refs_0_), channel_id=1, source_target_pairs={{0,24},{1,25},{2,26},{3,27},{4,28},{5,29},{6,30},{7,31},{8,16},{9,... | collective-permute-start | bytes 208904 | tf_op jit(solution)/shard_map/ppermute | solution.py:348
  7.9 0.8 %copy-start = (bf16[1,8192]{1,0:T(2,128)(2,1)S(1)}, bf16[1,8192]{1,0:T(2,128)(2,1)}, u32[]{:S(2)}) copy-start(bf16[1,8192]{1,0:T(2,128)(2,1)} %query_ref.1) | copy-start | bytes 49156
  13.5 1.6 %collective-permute-start.3 = (bf16[64,2176]{1,0:T(8,128)(2,1)S(1)}, bf16[64,2176]{1,0:T(8,128)(2,1)S(1)}, u32[]{:S(2)}, u32[]{:S(2)}) collective-permute-start(bf16[64,2176]{1,0:T(8,128)(2,1)S(1)} %stack.1.refs_0_), channel_id=1, source_target_pairs={{0,1},{1,0},{2,3},{3,2},{4,5},{5,4},{6,7},{7,6},{8,9},{9,8},{10,11... | collective-permute-start | bytes 835592 | tf_op jit(solution)/shard_map/ppermute | solution.py:348
  13.6 6.6 %collective-permute-start.4 = (bf16[64,2176]{1,0:T(8,128)(2,1)S(1)}, bf16[64,2176]{1,0:T(8,128)(2,1)S(1)}, u32[]{:S(2)}, u32[]{:S(2)}) collective-permute-start(bf16[64,2176]{1,0:T(8,128)(2,1)S(1)} %stack.1.refs_0_), channel_id=1, source_target_pairs={{0,2},{1,5},{2,0},{3,7},{4,6},{5,1},{6,4},{7,3},{8,10},{9,13},{10,... | collective-permute-start | bytes 835592 | tf_op jit(solution)/shard_map/ppermute | solution.py:343
  15.1 8.1 %collective-permute-start.10 = (bf16[64,2176]{1,0:T(8,128)(2,1)S(1)}, bf16[64,2176]{1,0:T(8,128)(2,1)S(1)}, u32[]{:S(2)}, u32[]{:S(2)}) collective-permute-start(bf16[64,2176]{1,0:T(8,128)(2,1)S(1)} %collective-permute-done.3.refs_1_), channel_id=1, source_target_pairs={{0,2},{1,5},{2,0},{3,7},{4,6},{5,1},{6,4},{7,3},{8,10},{9,13},{10,... | collective-permute-start | bytes 835592 | tf_op jit(solution)/shard_map/ppermute | solution.py:343
  20.2 1.8 %collective-permute-start.5 = (bf16[32,2176]{1,0:T(8,128)(2,1)S(1)}, bf16[32,2176]{1,0:T(8,128)(2,1)S(1)}, u32[]{:S(2)}, u32[]{:S(2)}) collective-permute-start(bf16[32,2176]{1,0:T(8,128)(2,1)S(1)} %get-tuple-element.26), channel_id=1, source_target_pairs={{0,1},{1,0},{2,3},{3,2},{4,5},{5,4},{6,7},{7,6},{8,9},{9,8},{10,11... | collective-permute-start | bytes 417800 | tf_op jit(solution)/shard_map/ppermute | solution.py:348
  20.3 1.7 %collective-permute-start.6 = (bf16[32,2176]{1,0:T(8,128)(2,1)S(1)}, bf16[32,2176]{1,0:T(8,128)(2,1)S(1)}, u32[]{:S(2)}, u32[]{:S(2)}) collective-permute-start(bf16[32,2176]{1,0:T(8,128)(2,1)S(1)} %get-tuple-element.27), channel_id=1, source_target_pairs={{0,1},{1,0},{2,3},{3,2},{4,5},{5,4},{6,7},{7,6},{8,9},{9,8},{10,11... | collective-permute-start | bytes 417800 | tf_op jit(solution)/shard_map/ppermute | solution.py:348
  20.8 6.8 %collective-permute-start.16 = (bf16[64,2176]{1,0:T(8,128)(2,1)S(1)}, bf16[64,2176]{1,0:T(8,128)(2,1)S(1)}, u32[]{:S(2)}, u32[]{:S(2)}) collective-permute-start(bf16[64,2176]{1,0:T(8,128)(2,1)S(1)} %collective-permute-done.4.block_ref.refs_0_), channel_id=1, source_target_pairs={{0,5},{1,2},{2,7},{3,0},{4,1},{5,6},{6,3},{7,4},{8,13},{9,10},{10,... | collective-permute-start | bytes 835592 | tf_op jit(solution)/shard_map/ppermute | solution.py:343
  23.3 2.4 %collective-permute-start.11 = (bf16[32,2176]{1,0:T(8,128)(2,1)S(1)}, bf16[32,2176]{1,0:T(8,128)(2,1)S(1)}, u32[]{:S(2)}, u32[]{:S(2)}) collective-permute-start(bf16[32,2176]{1,0:T(8,128)(2,1)S(1)} %get-tuple-element.32), channel_id=1, source_target_pairs={{0,1},{1,0},{2,3},{3,2},{4,5},{5,4},{6,7},{7,6},{8,9},{9,8},{10,11... | collective-permute-start | bytes 417800 | tf_op jit(solution)/shard_map/ppermute | solution.py:348
  23.8 1.9 %collective-permute-start.12 = (bf16[32,2176]{1,0:T(8,128)(2,1)S(1)}, bf16[32,2176]{1,0:T(8,128)(2,1)S(1)}, u32[]{:S(2)}, u32[]{:S(2)}) collective-permute-start(bf16[32,2176]{1,0:T(8,128)(2,1)S(1)} %get-tuple-element.33), channel_id=1, source_target_pairs={{0,1},{1,0},{2,3},{3,2},{4,5},{5,4},{6,7},{7,6},{8,9},{9,8},{10,11... | collective-permute-start | bytes 417800 | tf_op jit(solution)/shard_map/ppermute | solution.py:348
  23.9 1.4 %collective-permute-start.7 = (bf16[32,2048]{1,0:T(8,128)(2,1)S(1)}, bf16[32,2048]{1,0:T(8,128)(2,1)S(1)}, u32[]{:S(2)}, u32[]{:S(2)}) collective-permute-start(bf16[32,2048]{1,0:T(8,128)(2,1)S(1)} %get-tuple-element.29), channel_id=1, source_target_pairs={{0,1},{1,0},{2,3},{3,2},{4,5},{5,4},{6,7},{7,6},{8,9},{9,8},{10,11... | collective-permute-start | bytes 393224 | tf_op jit(solution)/shard_map/ppermute | solution.py:348
  24.3 1.3 %collective-permute-start.8 = (bf16[32,2048]{1,0:T(8,128)(2,1)S(1)}, bf16[32,2048]{1,0:T(8,128)(2,1)S(1)}, u32[]{:S(2)}, u32[]{:S(2)}) collective-permute-start(bf16[32,2048]{1,0:T(8,128)(2,1)S(1)} %get-tuple-element.30), channel_id=1, source_target_pairs={{0,1},{1,0},{2,3},{3,2},{4,5},{5,4},{6,7},{7,6},{8,9},{9,8},{10,11... | collective-permute-start | bytes 393224 | tf_op jit(solution)/shard_map/ppermute | solution.py:348
  27.0 2.5 %collective-permute-start.13 = (bf16[32,2048]{1,0:T(8,128)(2,1)S(1)}, bf16[32,2048]{1,0:T(8,128)(2,1)S(1)}, u32[]{:S(2)}, u32[]{:S(2)}) collective-permute-start(bf16[32,2048]{1,0:T(8,128)(2,1)S(1)} %get-tuple-element.35), channel_id=1, source_target_pairs={{0,1},{1,0},{2,3},{3,2},{4,5},{5,4},{6,7},{7,6},{8,9},{9,8},{10,11... | collective-permute-start | bytes 393224 | tf_op jit(solution)/shard_map/ppermute | solution.py:348
  27.3 2.2 %collective-permute-start.14 = (bf16[32,2048]{1,0:T(8,128)(2,1)S(1)}, bf16[32,2048]{1,0:T(8,128)(2,1)S(1)}, u32[]{:S(2)}, u32[]{:S(2)}) collective-permute-start(bf16[32,2048]{1,0:T(8,128)(2,1)S(1)} %get-tuple-element.36), channel_id=1, source_target_pairs={{0,1},{1,0},{2,3},{3,2},{4,5},{5,4},{6,7},{7,6},{8,9},{9,8},{10,11... | collective-permute-start | bytes 393224 | tf_op jit(solution)/shard_map/ppermute | solution.py:348
  27.6 2.7 %collective-permute-start.17 = (bf16[32,2176]{1,0:T(8,128)(2,1)S(1)}, bf16[32,2176]{1,0:T(8,128)(2,1)S(1)}, u32[]{:S(2)}, u32[]{:S(2)}) collective-permute-start(bf16[32,2176]{1,0:T(8,128)(2,1)S(1)} %get-tuple-element.37), channel_id=1, source_target_pairs={{0,1},{1,0},{2,3},{3,2},{4,5},{5,4},{6,7},{7,6},{8,9},{9,8},{10,11... | collective-permute-start | bytes 417800 | tf_op jit(solution)/shard_map/ppermute | solution.py:348
  27.9 2.5 %collective-permute-start.18 = (bf16[32,2176]{1,0:T(8,128)(2,1)S(1)}, bf16[32,2176]{1,0:T(8,128)(2,1)S(1)}, u32[]{:S(2)}, u32[]{:S(2)}) collective-permute-start(bf16[32,2176]{1,0:T(8,128)(2,1)S(1)} %get-tuple-element.38), channel_id=1, source_target_pairs={{0,1},{1,0},{2,3},{3,2},{4,5},{5,4},{6,7},{7,6},{8,9},{9,8},{10,11... | collective-permute-start | bytes 417800 | tf_op jit(solution)/shard_map/ppermute | solution.py:348
  28.2 7.3 %collective-permute-start.9 = (bf16[64,2048]{1,0:T(8,128)(2,1)S(1)}, bf16[64,2048]{1,0:T(8,128)(2,1)S(1)}, u32[]{:S(2)}, u32[]{:S(2)}) collective-permute-start(bf16[64,2048]{1,0:T(8,128)(2,1)S(1)} %add.68.refs_5_), channel_id=1, source_target_pairs={{0,2},{1,5},{2,0},{3,7},{4,6},{5,1},{6,4},{7,3},{8,10},{9,13},{10,... | collective-permute-start | bytes 786440 | tf_op jit(solution)/shard_map/ppermute | solution.py:343
  29.5 7.8 %collective-permute-start.15 = (bf16[64,2048]{1,0:T(8,128)(2,1)S(1)}, bf16[64,2048]{1,0:T(8,128)(2,1)S(1)}, u32[]{:S(2)}, u32[]{:S(2)}) collective-permute-start(bf16[64,2048]{1,0:T(8,128)(2,1)S(1)} %add.69.refs_5_), channel_id=1, source_target_pairs={{0,2},{1,5},{2,0},{3,7},{4,6},{5,1},{6,4},{7,3},{8,10},{9,13},{10,... | collective-permute-start | bytes 786440 | tf_op jit(solution)/shard_map/ppermute | solution.py:343
  31.6 1.8 %collective-permute-start.19 = (bf16[32,2048]{1,0:T(8,128)(2,1)S(1)}, bf16[32,2048]{1,0:T(8,128)(2,1)S(1)}, u32[]{:S(2)}, u32[]{:S(2)}) collective-permute-start(bf16[32,2048]{1,0:T(8,128)(2,1)S(1)} %get-tuple-element.40), channel_id=1, source_target_pairs={{0,1},{1,0},{2,3},{3,2},{4,5},{5,4},{6,7},{7,6},{8,9},{9,8},{10,11... | collective-permute-start | bytes 393224 | tf_op jit(solution)/shard_map/ppermute | solution.py:348
  31.7 1.8 %collective-permute-start.20 = (bf16[32,2048]{1,0:T(8,128)(2,1)S(1)}, bf16[32,2048]{1,0:T(8,128)(2,1)S(1)}, u32[]{:S(2)}, u32[]{:S(2)}) collective-permute-start(bf16[32,2048]{1,0:T(8,128)(2,1)S(1)} %get-tuple-element.41), channel_id=1, source_target_pairs={{0,1},{1,0},{2,3},{3,2},{4,5},{5,4},{6,7},{7,6},{8,9},{9,8},{10,11... | collective-permute-start | bytes 393224 | tf_op jit(solution)/shard_map/ppermute | solution.py:348
  33.6 7.1 %collective-permute-start.23 = (bf16[32,2048]{1,0:T(8,128)(2,1)S(1)}, bf16[32,2048]{1,0:T(8,128)(2,1)S(1)}, u32[]{:S(2)}, u32[]{:S(2)}) collective-permute-start(bf16[32,2048]{1,0:T(8,128)(2,1)S(1)} %slice.37), channel_id=1, source_target_pairs={{0,7},{1,6},{2,5},{3,4},{4,3},{5,2},{6,1},{7,0},{8,15},{9,14},{10,... | collective-permute-start | bytes 393224 | tf_op jit(solution)/shard_map/ppermute | solution.py:348
  37.4 3.2 %collective-permute-start.21 = (bf16[64,2048]{1,0:T(8,128)(2,1)S(1)}, bf16[64,2048]{1,0:T(8,128)(2,1)S(1)}, u32[]{:S(2)}, u32[]{:S(2)}) collective-permute-start(bf16[64,2048]{1,0:T(8,128)(2,1)S(1)} %add.71), channel_id=1, source_target_pairs={{0,1},{1,0},{2,3},{3,2},{4,5},{5,4},{6,7},{7,6},{8,9},{9,8},{10,11... | collective-permute-start | bytes 786440 | tf_op jit(solution)/shard_map/ppermute | solution.py:348
  37.5 6.2 %collective-permute-start.26 = (bf16[16,2048]{1,0:T(8,128)(2,1)S(1)}, bf16[16,2048]{1,0:T(8,128)(2,1)S(1)}, u32[]{:S(2)}, u32[]{:S(2)}) collective-permute-start(bf16[16,2048]{1,0:T(8,128)(2,1)S(1)} %get-tuple-element.43), channel_id=1, source_target_pairs={{0,7},{1,6},{2,5},{3,4},{4,3},{5,2},{6,1},{7,0},{8,15},{9,14},{10,... | collective-permute-start | bytes 196616 | tf_op jit(solution)/shard_map/ppermute | solution.py:348
  40.6 5.4 %collective-permute-start.22 = (bf16[16,2048]{1,0:T(8,128)(2,1)S(1)}, bf16[16,2048]{1,0:T(8,128)(2,1)S(1)}, u32[]{:S(2)}, u32[]{:S(2)}) collective-permute-start(bf16[16,2048]{1,0:T(8,128)(2,1)S(1)} %get-tuple-element.42), channel_id=1, source_target_pairs={{0,7},{1,6},{2,5},{3,4},{4,3},{5,2},{6,1},{7,0},{8,15},{9,14},{10,... | collective-permute-start | bytes 196616 | tf_op jit(solution)/shard_map/ppermute | solution.py:348
  40.8 6.8 %collective-permute-start.24 = (bf16[16,2048]{1,0:T(8,128)(2,1)S(1)}, bf16[16,2048]{1,0:T(8,128)(2,1)S(1)}, u32[]{:S(2)}, u32[]{:S(2)}) collective-permute-start(bf16[16,2048]{1,0:T(8,128)(2,1)S(1)} %get-tuple-element.44), channel_id=1, source_target_pairs={{0,24},{1,25},{2,26},{3,27},{4,28},{5,29},{6,30},{7,31},{8,16},{9,... | collective-permute-start | bytes 196616 | tf_op jit(solution)/shard_map/ppermute | solution.py:348
  43.7 6.0 %collective-permute-start.25 = (bf16[16,2048]{1,0:T(8,128)(2,1)S(1)}, bf16[16,2048]{1,0:T(8,128)(2,1)S(1)}, u32[]{:S(2)}, u32[]{:S(2)}) collective-permute-start(bf16[16,2048]{1,0:T(8,128)(2,1)S(1)} %get-tuple-element.45), channel_id=1, source_target_pairs={{0,16},{1,17},{2,18},{3,19},{4,20},{5,21},{6,22},{7,23},{8,24},{9,... | collective-permute-start | bytes 196616 | tf_op jit(solution)/shard_map/ppermute | solution.py:348
  43.7 6.0 %collective-permute-start.27 = (bf16[16,2048]{1,0:T(8,128)(2,1)S(1)}, bf16[16,2048]{1,0:T(8,128)(2,1)S(1)}, u32[]{:S(2)}, u32[]{:S(2)}) collective-permute-start(bf16[16,2048]{1,0:T(8,128)(2,1)S(1)} %fusion.1), channel_id=1, source_target_pairs={{0,8},{1,9},{2,10},{3,11},{4,12},{5,13},{6,14},{7,15},{8,0},{9,1},... | collective-permute-start | bytes 196616 | tf_op jit(solution)/shard_map/ppermute | solution.py:348

commit v6 on v5

--- a/solution.py
+++ b/solution.py
@@ -149,20 +149,20 @@
 
 
 def attend_kernel(
-    lengths_ref, query_ref, key_hbm, value_hbm, in_hbm, proj_hbm, out_ref, in_ref, proj_ref,
-    key_ref, value_ref, sems
+    lengths_ref, query_hbm, key_hbm, value_hbm, out_ref, query_ref, key_ref, value_ref, sems
 ):
-    pairs = ((key_hbm, key_ref), (value_hbm, value_ref), (in_hbm, in_ref), (proj_hbm, proj_ref))
+    pairs = ((query_hbm, query_ref), (key_hbm, key_ref), (value_hbm, value_ref))
     copies = [pltpu.make_async_copy(a, b, sems.at[i]) for i, (a, b) in enumerate(pairs)]
     for copy in copies:
         copy.start()
     head_count = query_ref.shape[1] // HD
     span = key_ref.shape[0]
     group = head_count // KVH
+    live = lax.broadcasted_iota(jnp.int32, (group, span), 1) < lengths_ref[0]
+    copies[0].wait()
     query = query_ref[...].astype(jnp.float32)
     heads = [query[:, i * HD : (i + 1) * HD] for i in range(head_count)]
-    live = lax.broadcasted_iota(jnp.int32, (group, span), 1) < lengths_ref[0]
-    copies[0].wait()
+    copies[1].wait()
     for k in range(KVH):
         rows = slice(k * group, (k + 1) * group)
         columns = slice(k * HD, (k + 1) * HD)
@@ -177,44 +177,66 @@
         weights = jnp.exp(masked - top).astype(jnp.bfloat16)
         total = jnp.sum(weights.astype(jnp.float32), axis=1, keepdims=True)
         if k == 0:
-            copies[1].wait()
+            copies[2].wait()
         summed = jnp.dot(weights, value_ref[:, columns], preferred_element_type=jnp.float32)
         out_ref[rows, :] = (summed / total).astype(out_ref.dtype)
-    copies[2].wait()
-    copies[3].wait()
-
-
-def attend_and_fetch(queries, cached_keys, cached_values, lengths, expert_in, expert_out):
+
+
+def attend_whole(queries, cached_keys, cached_values, lengths):
     width = queries.shape[1]
     head_count = width // HD
     span = cached_keys.shape[1]
-    attended, near_in, near_out = pl.pallas_call(
+    return pl.pallas_call(
         attend_kernel,
-        out_shape=[
-            jax.ShapeDtypeStruct((head_count, HD), jnp.bfloat16),
-            pltpu.VMEM(expert_in.shape[1:], jnp.bfloat16),
-            pltpu.VMEM(expert_out.shape[1:], jnp.bfloat16),
-        ],
-        in_specs=[SMEM, VMEM] + [HBM] * 4,
-        out_specs=[VMEM] * 3,
+        out_shape=jax.ShapeDtypeStruct((head_count, HD), jnp.bfloat16),
+        in_specs=[SMEM] + [HBM] * 3,
+        out_specs=VMEM,
         scratch_shapes=[
+            pltpu.VMEM(queries.shape, jnp.bfloat16),
             pltpu.VMEM(cached_keys.shape[1:], jnp.bfloat16),
             pltpu.VMEM(cached_values.shape[1:], jnp.bfloat16),
-            pltpu.SemaphoreType.DMA((4,)),
+            pltpu.SemaphoreType.DMA((3,)),
         ],
-        compiler_params=pltpu.CompilerParams(vmem_limit_bytes=14 << 20),
+        compiler_params=pltpu.CompilerParams(vmem_limit_bytes=8 << 20),
         cost_estimate=pl.CostEstimate(
             flops=4 * head_count * HD * span,
-            bytes_accessed=4 * span * KVH * HD + 4 * expert_in.size + 4 * expert_out.size,
+            bytes_accessed=4 * span * KVH * HD,
             transcendentals=head_count * span,
         ),
         name="attention",
-    )(
-        lengths,
-        queries,
-        *(far_off(a[0]) for a in (cached_keys, cached_values, expert_in, expert_out)),
-    )
-    return attended, near_in, near_out
+    )(lengths, far_off(queries), far_off(cached_keys[0]), far_off(cached_values[0]))
+
+
+def fetch_kernel(in_hbm, proj_hbm, *refs):
+    in_ref, proj_ref, mark_ref, sems = refs[-4:]
+    copies = [
+        pltpu.make_async_copy(in_hbm, in_ref, sems.at[0]),
+        pltpu.make_async_copy(proj_hbm, proj_ref, sems.at[1]),
+    ]
+    for copy in copies:
+        copy.start()
+    mark_ref[...] = jnp.zeros_like(mark_ref)
+    for copy in copies:
+        copy.wait()
+
+
+def fetch_expert(expert_in, expert_out, after=()):
+    return pl.pallas_call(
+        fetch_kernel,
+        out_shape=[
+            pltpu.VMEM(expert_in.shape[1:], jnp.bfloat16),
+            pltpu.VMEM(expert_out.shape[1:], jnp.bfloat16),
+            jax.ShapeDtypeStruct((8, LANES), jnp.float32),
+        ],
+        in_specs=[HBM] * 2 + [ANYWHERE] * len(after),
+        out_specs=[VMEM] * 3,
+        scratch_shapes=[pltpu.SemaphoreType.DMA((2,))],
+        compiler_params=pltpu.CompilerParams(vmem_limit_bytes=14 << 20),
+        cost_estimate=pl.CostEstimate(
+            flops=0, bytes_accessed=2 * expert_in.size + 2 * expert_out.size, transcendentals=0
+        ),
+        name="fetch",
+    )(far_off(expert_in[0]), far_off(expert_out[0]), *after)
 
 
 def stack_kernel(part_count, *refs):
@@ -353,18 +375,17 @@
 ):
     tok_rows = tokens.shape[0]
     experts_here = lax.axis_size("expert")
-    far = [8 * k for k in range(1, experts_here // 8)]
+    far = [8 * k for k in range(experts_here // 8 - 1, 0, -1)]
     wide, half = jnp.float32, jnp.bfloat16
     own = label_tokens(tokens, routes, gate_values, experts_here)
     arrived = [swap(own, d) for d in far]
-    attended, near_in, near_out = attend_and_fetch(
-        queries, cached_keys, cached_values, lengths, expert_in, expert_out
-    )
+    attended = attend_whole(queries, cached_keys, cached_values, lengths)
+    column = stack_rows([own] + arrived, [attended])
+    near_in, near_out, mark = fetch_expert(expert_in, expert_out, [column])
 
     def gated(parts, results, after=()):
         return run_expert(parts, near_in, near_out, results, after)
 
-    column = stack_rows([own] + arrived, [attended])
     size = column.shape[0]
     pieces = 2
     split = [(size, wide)] + [(size // pieces, half)] * pieces
@@ -377,7 +398,7 @@
     side_b = cross(pair, 2, 4)
     corner = cross(side_a, 5, 3)
     kept_own, kept_pair = gated([column, pair], [(size, wide)] * 2, [])
-    kept_a, *sent_a = gated([side_a] + to_pair(side_a, []), split)
+    kept_a, *sent_a = gated([side_a] + to_pair(side_a, [mark]), split)
     sum_a = add_parts(kept_a, [swap(part, 1) for part in sent_a])
     got_a = cross(sum_a, 2, 4)
     kept_b, *sent_b = gated([side_b] + to_pair(side_b, [kept_a]), split, [sum_a])
@@ -387,9 +408,8 @@
     sum_c = add_parts(kept_c, [swap(part, 1) for part in sent_c], [])
     shared = add_parts(kept_pair, [got_b], [got_a, sum_c])
     total = kept_own + got_a.astype(wide) + swap(shared, 1).astype(wide)
-    bounds = (0, tok_rows, 2 * tok_rows, size)
     returned = []
-    for first, last in reversed(list(zip(bounds[:-1], bounds[1:]))):
+    for first, last in ((tok_rows, 3 * tok_rows), (3 * tok_rows, size), (0, tok_rows)):
         returned.append((first, last, swap(sum_c[first:last], 7)))
     sums = {}
     for first, last, block in returned:
@@ -397,7 +417,7 @@
         for k in range(first // tok_rows, last // tok_rows):
             sums[k] = block[k * tok_rows - first : (k + 1) * tok_rows - first]
     final = sums[0]
-    for k in (3, 2, 1):
+    for k in (1, 2, 3):
         block = sums[k].astype(half)
         got = [swap(part, far[k - 1]) for part in cut(block, 2 if k == 0 else 1)]
         final = final + (got[0] if len(got) == 1 else jnp.concatenate(got)).astype(wide)
@@ -414,7 +434,7 @@
 
 def solution(mesh):
     sizes = dict(mesh.shape)
-    spread = sizes["cuts"] == 1 and sizes["expert"] in (8, 16, 32)
+    spread = sizes["cuts"] == 1 and sizes["expert"] == 32
     in_specs = (
         P(("groups", "expert", "cuts"), None),
         P(("groups", "expert", "cuts"), None),

time: 50.7 us -> 49.8 us (0.982)
  waiting for transfers between devices: 11.5 us -> 9.09 us
  Pallas kernels: 10.1 us -> 12.3 us
  local copies, waits for them, and re-layouts: 1.43 us -> 0.67 us
    ppermute x5, waiting for transfers between devices: 5.41 us -> 2.55 us  [cross(): return lax.ppermute(block, 'expert', pairs)]
    pallas_call x1 -> x2, Pallas kernels: 3.79 us -> 6 us  [the longest x1 3.14 us: attend_whole(): pl.pallas_call(attend_kernel, out_shape=jax.ShapeDtypeStruct((head_count,...]
    unnamed x3 -> x1, local copies, waits for them, and re-layouts: 1.39 us -> 0.64 us
  transfers between devices with their start and end apart: 28 -> 28, of which waited for: 7 -> 7; matrix products, arithmetic and copies ran while one was open for 2% -> 2% of each run, Pallas kernels for 18% -> 23%
where the time goes in v6:
time: 49.8 us; the launch traced here: 49.6 us
  starting transfers between devices  25.2 us (51%)
  Pallas kernels  12.3 us (25%)
  waiting for transfers between devices  9.09 us (18%)
  between operations  1.52 us (3%)
  other arithmetic  0.79 us (2%)
  local copies, waits for them, and re-layouts  0.67 us (1%)
    ppermute x23, starting transfers between devices, swap(): lax.ppermute(block, 'expert', [(i, i ^ distance) for i in range(count)])  18.9 us
    ppermute x23, waiting for transfers between devices, swap(): lax.ppermute(block, 'expert', [(i, i ^ distance) for i in range(count)])  6.54 us
    ppermute x5, starting transfers between devices, cross(): return lax.ppermute(block, 'expert', pairs)  6.33 us
    pallas_call x4, Pallas kernels, run_expert(): pl.pallas_call(functools.partial(expert_kernel, len(parts), len(after)),...  5.07 us
    pallas_call x1, Pallas kernels, attend_whole(): pl.pallas_call(attend_kernel, out_shape=jax.ShapeDtypeStruct((head_count,...  3.14 us
    pallas_call x1, Pallas kernels, fetch_expert(): pl.pallas_call(fetch_kernel, out_shape=[pltpu.VMEM(expert_in.shape[1:], j...  2.86 us
    ppermute x5, waiting for transfers between devices, cross(): return lax.ppermute(block, 'expert', pairs)  2.55 us
  transfers between devices with their start and end apart: 28, of which 7 were waited for; matrix products, arithmetic and copies ran while one was open for 2% of the time, Pallas kernels for 23%

profile of v6, /device:TPU:0, one launch (start us, length us, event | category | flops | bytes accessed | tf_op | source)
XLA Modules:
  0.0 49.6 jit_solution(7360585714142838429)
XLA Ops:
  0.6 1.0 %label.1.refs_0_ = bf16[16,2176]{1,0:T(8,128)(2,1)S(1)} custom-call(bf16[16,2048]{1,0:T(8,128)(2,1)} %tokens_hbm.1, s32[8,16]{1,0:T(8,128)} %bitcast.17, bf16[8,16]{1,0:T(8,128)(2,1)} %bitcast.18), custom_call_target="tpu_custom_call" | custom-call | tf_op jit(solution)/shard_map/label/pallas_call | solution.py:136
  1.6 5.1 %collective-permute-start = (bf16[16,2176]{1,0:T(8,128)(2,1)S(1)}, bf16[16,2176]{1,0:T(8,128)(2,1)S(1)}, u32[]{:S(2)}, u32[]{:S(2)}) collective-permute-start(bf16[16,2176]{1,0:T(8,128)(2,1)S(1)} %label.1.refs_0_), channel_id=1, source_target_pairs={{0,24},{1,25},{2,26},{3,27},{4,28},{5,29},{6,30},{7,31},{8,16},{9,... | collective-permute-start | bytes 208904 | tf_op jit(solution)/shard_map/ppermute | solution.py:370
  6.7 0.0 collective-permute-start.1
  6.7 0.6 %collective-permute-start.2 = (bf16[16,2176]{1,0:T(8,128)(2,1)S(1)}, bf16[16,2176]{1,0:T(8,128)(2,1)S(1)}, u32[]{:S(2)}, u32[]{:S(2)}) collective-permute-start(bf16[16,2176]{1,0:T(8,128)(2,1)S(1)} %label.1.refs_0_), channel_id=1, source_target_pairs={{0,8},{1,9},{2,10},{3,11},{4,12},{5,13},{6,14},{7,15},{8,0},{9,1},... | collective-permute-start | bytes 208904 | tf_op jit(solution)/shard_map/ppermute | solution.py:370
  8.0 3.1 %attention.1.refs_4_ = bf16[64,128]{1,0:T(8,128)(2,1)S(1)} custom-call(s32[1]{0:T(128)S(6)} %copy.14.lengths_ref, bf16[1,8192]{1,0:T(2,128)(2,1)} %query_hbm.1, bf16[1536,512]{1,0:T(8,128)(2,1)} %bitcast.14, bf16[1536,512]{1,0:T(8,128)(2,1)} %bitcast.15), custom_call_target="tpu_custom_call" | custom-call | flops 50331648 | bytes 3145728 | tf_op jit(solution)/shard_map/attention/pallas_call | solution.py:189
  11.2 1.5 %collective-permute-done.1.refs_2_ = bf16[16,2176]{1,0:T(8,128)(2,1)S(1)} collective-permute-done((bf16[16,2176]{1,0:T(8,128)(2,1)S(1)}, bf16[16,2176]{1,0:T(8,128)(2,1)S(1)}, u32[]{:S(2)}, u32[]{:S(2)}) %collective-permute-start.1) | collective-permute-done | bytes 69664 | tf_op jit(solution)/shard_map/ppermute | solution.py:370
  12.6 0.1 collective-permute-start.3
  12.7 1.6 %collective-permute-start.4 = (bf16[64,2176]{1,0:T(8,128)(2,1)S(1)}, bf16[64,2176]{1,0:T(8,128)(2,1)S(1)}, u32[]{:S(2)}, u32[]{:S(2)}) collective-permute-start(bf16[64,2176]{1,0:T(8,128)(2,1)S(1)} %stack.1.refs_0_), channel_id=1, source_target_pairs={{0,2},{1,5},{2,0},{3,7},{4,6},{5,1},{6,4},{7,3},{8,10},{9,13},{10,... | collective-permute-start | bytes 835592 | tf_op jit(solution)/shard_map/ppermute | solution.py:365
  14.3 0.0 collective-permute-done.3.refs_1_
  14.3 1.5 %collective-permute-start.10 = (bf16[64,2176]{1,0:T(8,128)(2,1)S(1)}, bf16[64,2176]{1,0:T(8,128)(2,1)S(1)}, u32[]{:S(2)}, u32[]{:S(2)}) collective-permute-start(bf16[64,2176]{1,0:T(8,128)(2,1)S(1)} %collective-permute-done.3.refs_1_), channel_id=1, source_target_pairs={{0,2},{1,5},{2,0},{3,7},{4,6},{5,1},{6,4},{7,3},{8,10},{9,13},{10,... | collective-permute-start | bytes 835592 | tf_op jit(solution)/shard_map/ppermute | solution.py:365
  15.8 2.9 %fetch.1 = (bf16[2048,768]{1,0:T(8,128)(2,1)S(1)}, bf16[768,2048]{1,0:T(8,128)(2,1)S(1)}, f32[8,128]{1,0:T(8,128)S(1)}) custom-call(bf16[2048,768]{1,0:T(8,128)(2,1)} %bitcast.12, bf16[768,2048]{1,0:T(8,128)(2,1)} %bitcast.13, bf16[64,2176]{1,0:T(8,128)(2,1)S(1)} %stack.1.refs_0_), custom_call_target="tpu_custom_call" | custom-call | bytes 6291456 | tf_op jit(solution)/shard_map/fetch/pallas_call | solution.py:224
  18.6 0.7 %collective-permute-done.4.block_ref.refs_0_ = bf16[64,2176]{1,0:T(8,128)(2,1)S(1)} collective-permute-done((bf16[64,2176]{1,0:T(8,128)(2,1)S(1)}, bf16[64,2176]{1,0:T(8,128)(2,1)S(1)}, u32[]{:S(2)}, u32[]{:S(2)}) %collective-permute-start.4) | collective-permute-done | bytes 278560 | tf_op jit(solution)/shard_map/ppermute | solution.py:365
  19.4 0.1 collective-permute-start.5
  19.4 0.5 %collective-permute-start.6 = (bf16[32,2176]{1,0:T(8,128)(2,1)S(1)}, bf16[32,2176]{1,0:T(8,128)(2,1)S(1)}, u32[]{:S(2)}, u32[]{:S(2)}) collective-permute-start(bf16[32,2176]{1,0:T(8,128)(2,1)S(1)} %get-tuple-element.27), channel_id=1, source_target_pairs={{0,1},{1,0},{2,3},{3,2},{4,5},{5,4},{6,7},{7,6},{8,9},{9,8},{10,11... | collective-permute-start | bytes 417800 | tf_op jit(solution)/shard_map/ppermute | solution.py:370
  19.9 1.2 %collective-permute-start.16 = (bf16[64,2176]{1,0:T(8,128)(2,1)S(1)}, bf16[64,2176]{1,0:T(8,128)(2,1)S(1)}, u32[]{:S(2)}, u32[]{:S(2)}) collective-permute-start(bf16[64,2176]{1,0:T(8,128)(2,1)S(1)} %collective-permute-done.4.block_ref.refs_0_), channel_id=1, source_target_pairs={{0,5},{1,2},{2,7},{3,0},{4,1},{5,6},{6,3},{7,4},{8,13},{9,10},{10,... | collective-permute-start | bytes 835592 | tf_op jit(solution)/shard_map/ppermute | solution.py:365
  21.1 1.3 %expert.5 = (f32[64,2048]{1,0:T(8,128)S(1)}, bf16[32,2048]{1,0:T(8,128)(2,1)S(1)}, bf16[32,2048]{1,0:T(8,128)(2,1)S(1)}) custom-call(bf16[64,2176]{1,0:T(8,128)(2,1)S(1)} %collective-permute-done.4.block_ref.refs_0_, bf16[32,2176]{1,0:T(8,128)(2,1)S(1)} %collective-permute-done.5.refs_1_, bf16[32,2176]{1,0:T(8,128)(2,1)S(1)} %collective-permute-done.6.refs_2_, ...), custom_call_target="tpu_custom_call" | custom-call | flops 805306368 | bytes 1572864 | tf_op jit(solution)/shard_map/expert/pallas_call | solution.py:283
  22.5 0.5 collective-permute-start.11
  22.9 0.1 collective-permute-start.12
  23.0 0.4 collective-permute-start.7
  23.4 0.1 collective-permute-start.8
  23.5 0.9 %collective-permute-done.7.refs_1_ = bf16[32,2048]{1,0:T(8,128)(2,1)S(1)} collective-permute-done((bf16[32,2048]{1,0:T(8,128)(2,1)S(1)}, bf16[32,2048]{1,0:T(8,128)(2,1)S(1)}, u32[]{:S(2)}, u32[]{:S(2)}) %collective-permute-start.7) | collective-permute-done | bytes 131104 | tf_op jit(solution)/shard_map/ppermute | solution.py:370
  24.5 0.3 collective-permute-done.8.refs_2_
  24.8 0.1 add.68.refs_5_
  24.9 1.3 %expert.6 = (f32[64,2048]{1,0:T(8,128)S(1)}, bf16[32,2048]{1,0:T(8,128)(2,1)S(1)}, bf16[32,2048]{1,0:T(8,128)(2,1)S(1)}) custom-call(bf16[64,2176]{1,0:T(8,128)(2,1)S(1)} %collective-permute-done.10.block_ref.refs_0_, bf16[32,2176]{1,0:T(8,128)(2,1)S(1)} %collective-permute-done.11.refs_1_, bf16[32,2176]{1,0:T(8,128)(2,1)S(1)} %collective-permute-done.12.refs_2_, ...), custom_call_target="tpu_custom_call" | custom-call | flops 805306368 | bytes 1572864 | tf_op jit(solution)/shard_map/expert/pallas_call | solution.py:283
  26.1 0.2 collective-permute-start.13
  26.4 0.3 collective-permute-start.14
  26.7 0.2 collective-permute-start.17
  27.0 0.3 collective-permute-start.18
  27.3 1.3 %collective-permute-start.9 = (bf16[64,2048]{1,0:T(8,128)(2,1)S(1)}, bf16[64,2048]{1,0:T(8,128)(2,1)S(1)}, u32[]{:S(2)}, u32[]{:S(2)}) collective-permute-start(bf16[64,2048]{1,0:T(8,128)(2,1)S(1)} %add.68.refs_5_), channel_id=1, source_target_pairs={{0,2},{1,5},{2,0},{3,7},{4,6},{5,1},{6,4},{7,3},{8,10},{9,13},{10,... | collective-permute-start | bytes 786440 | tf_op jit(solution)/shard_map/ppermute | solution.py:365
  28.6 0.1 add.69.refs_5_
  28.7 0.8 %collective-permute-start.15 = (bf16[64,2048]{1,0:T(8,128)(2,1)S(1)}, bf16[64,2048]{1,0:T(8,128)(2,1)S(1)}, u32[]{:S(2)}, u32[]{:S(2)}) collective-permute-start(bf16[64,2048]{1,0:T(8,128)(2,1)S(1)} %add.69.refs_5_), channel_id=1, source_target_pairs={{0,2},{1,5},{2,0},{3,7},{4,6},{5,1},{6,4},{7,3},{8,10},{9,13},{10,... | collective-permute-start | bytes 786440 | tf_op jit(solution)/shard_map/ppermute | solution.py:365
  29.5 1.3 %expert.7 = (f32[64,2048]{1,0:T(8,128)S(1)}, bf16[32,2048]{1,0:T(8,128)(2,1)S(1)}, bf16[32,2048]{1,0:T(8,128)(2,1)S(1)}) custom-call(bf16[64,2176]{1,0:T(8,128)(2,1)S(1)} %collective-permute-done.16.block_ref.refs_0_, bf16[32,2176]{1,0:T(8,128)(2,1)S(1)} %collective-permute-done.17.refs_1_, bf16[32,2176]{1,0:T(8,128)(2,1)S(1)} %collective-permute-done.18.refs_2_, ...), custom_call_target="tpu_custom_call" | custom-call | flops 805306368 | bytes 1572864 | tf_op jit(solution)/shard_map/expert/pallas_call | solution.py:283
  30.8 0.1 collective-permute-start.19
  30.9 0.5 %collective-permute-start.20 = (bf16[32,2048]{1,0:T(8,128)(2,1)S(1)}, bf16[32,2048]{1,0:T(8,128)(2,1)S(1)}, u32[]{:S(2)}, u32[]{:S(2)}) collective-permute-start(bf16[32,2048]{1,0:T(8,128)(2,1)S(1)} %get-tuple-element.41), channel_id=1, source_target_pairs={{0,1},{1,0},{2,3},{3,2},{4,5},{5,4},{6,7},{7,6},{8,9},{9,8},{10,11... | collective-permute-start | bytes 393224 | tf_op jit(solution)/shard_map/ppermute | solution.py:370
  31.4 1.3 %expert.4 = (f32[64,2048]{1,0:T(8,128)S(1)}, f32[64,2048]{1,0:T(8,128)S(1)}) custom-call(bf16[64,2176]{1,0:T(8,128)(2,1)S(1)} %stack.1.refs_0_, bf16[64,2176]{1,0:T(8,128)(2,1)S(1)} %collective-permute-done.3.refs_1_, bf16[2048,768]{1,0:T(8,128)(2,1)S(1)} %get-tuple-element.22.refs_2_.refs_3_, bf16[768,2048]{1,0:T(8,128)(2,1)S(1)} %get-tuple-element.23.refs_3_.refs_4_), custom_call_target="tpu_custom_call" | custom-call | flops 805306368 | bytes 1572864 | tf_op jit(solution)/shard_map/expert/pallas_call | solution.py:283
  32.6 0.1 add.70.refs_3_
  32.7 1.9 %collective-permute-start.23 = (bf16[32,2048]{1,0:T(8,128)(2,1)S(1)}, bf16[32,2048]{1,0:T(8,128)(2,1)S(1)}, u32[]{:S(2)}, u32[]{:S(2)}) collective-permute-start(bf16[32,2048]{1,0:T(8,128)(2,1)S(1)} %slice.37), channel_id=1, source_target_pairs={{0,7},{1,6},{2,5},{3,4},{4,3},{5,2},{6,1},{7,0},{8,15},{9,14},{10,... | collective-permute-start | bytes 393224 | tf_op jit(solution)/shard_map/ppermute | solution.py:370
  34.7 1.8 %collective-permute-done.15.refs_1_ = bf16[64,2048]{1,0:T(8,128)(2,1)S(1)} collective-permute-done((bf16[64,2048]{1,0:T(8,128)(2,1)S(1)}, bf16[64,2048]{1,0:T(8,128)(2,1)S(1)}, u32[]{:S(2)}, u32[]{:S(2)}) %collective-permute-start.15) | collective-permute-done | bytes 262176 | tf_op jit(solution)/shard_map/ppermute | solution.py:365
  36.6 0.1 collective-permute-start.21
  36.7 3.0 %collective-permute-start.26 = (bf16[16,2048]{1,0:T(8,128)(2,1)S(1)}, bf16[16,2048]{1,0:T(8,128)(2,1)S(1)}, u32[]{:S(2)}, u32[]{:S(2)}) collective-permute-start(bf16[16,2048]{1,0:T(8,128)(2,1)S(1)} %get-tuple-element.43), channel_id=1, source_target_pairs={{0,7},{1,6},{2,5},{3,4},{4,3},{5,2},{6,1},{7,0},{8,15},{9,14},{10,... | collective-permute-start | bytes 196616 | tf_op jit(solution)/shard_map/ppermute | solution.py:370
  39.7 0.1 collective-permute-start.22
  39.8 0.1 convert_add_fusion
  39.9 2.8 %collective-permute-start.24 = (bf16[16,2048]{1,0:T(8,128)(2,1)S(1)}, bf16[16,2048]{1,0:T(8,128)(2,1)S(1)}, u32[]{:S(2)}, u32[]{:S(2)}) collective-permute-start(bf16[16,2048]{1,0:T(8,128)(2,1)S(1)} %get-tuple-element.44), channel_id=1, source_target_pairs={{0,24},{1,25},{2,26},{3,27},{4,28},{5,29},{6,30},{7,31},{8,16},{9,... | collective-permute-start | bytes 196616 | tf_op jit(solution)/shard_map/ppermute | solution.py:370
  42.7 1.7 %collective-permute-start.27 = (bf16[16,2048]{1,0:T(8,128)(2,1)S(1)}, bf16[16,2048]{1,0:T(8,128)(2,1)S(1)}, u32[]{:S(2)}, u32[]{:S(2)}) collective-permute-start(bf16[16,2048]{1,0:T(8,128)(2,1)S(1)} %fusion.1), channel_id=1, source_target_pairs={{0,8},{1,9},{2,10},{3,11},{4,12},{5,13},{6,14},{7,15},{8,0},{9,1},... | collective-permute-start | bytes 196616 | tf_op jit(solution)/shard_map/ppermute | solution.py:370
  44.5 0.6 %copy.13 = bf16[1,1,64,128]{3,1,2,0:T(2,128)(2,1)} copy(bf16[1,1,64,128]{3,2,1,0:T(8,128)(2,1)S(1)} %bitcast.11) | data formatting | bytes 32768
  45.1 1.7 %collective-permute-done.24 = bf16[16,2048]{1,0:T(8,128)(2,1)S(1)} collective-permute-done((bf16[16,2048]{1,0:T(8,128)(2,1)S(1)}, bf16[16,2048]{1,0:T(8,128)(2,1)S(1)}, u32[]{:S(2)}, u32[]{:S(2)}) %collective-permute-start.24) | collective-permute-done | bytes 65568 | tf_op jit(solution)/shard_map/ppermute | solution.py:370
  46.8 2.1 %collective-permute-done.25 = bf16[16,2048]{1,0:T(8,128)(2,1)S(1)} collective-permute-done((bf16[16,2048]{1,0:T(8,128)(2,1)S(1)}, bf16[16,2048]{1,0:T(8,128)(2,1)S(1)}, u32[]{:S(2)}, u32[]{:S(2)}) %collective-permute-start.25) | collective-permute-done | bytes 65568 | tf_op jit(solution)/shard_map/ppermute | solution.py:370
  48.9 0.7 %fusion.5 = bf16[16,2048]{1,0:T(8,128)(2,1)} fusion(f32[64,2048]{1,0:T(8,128)S(1)} %convert_add_fusion, bf16[16,2048]{1,0:T(8,128)(2,1)S(1)} %collective-permute-done.27, bf16[16,2048]{1,0:T(8,128)(2,1)S(1)} %collective-permute-done.25, bf16[16,2048]{1,0:T(8,128)(2,1)S(1)} %collective-permute-done.24, bf16[16,2048]{1,0:T(8,128)(2,1)S(1)} %collective-permute-done.22), kind=kLoop, calls=%fused_computation.9 | loop fusion | flops 294912 | bytes 458752 | tf_op jit(solution)/shard_map/convert_element_type | solution.py:424
  (31 shorter events, 0.3 us)
Async XLA Ops:
  1.6 9.6 %collective-permute-start = (bf16[16,2176]{1,0:T(8,128)(2,1)S(1)}, bf16[16,2176]{1,0:T(8,128)(2,1)S(1)}, u32[]{:S(2)}, u32[]{:S(2)}) collective-permute-start(bf16[16,2176]{1,0:T(8,128)(2,1)S(1)} %label.1.refs_0_), channel_id=1, source_target_pairs={{0,24},{1,25},{2,26},{3,27},{4,28},{5,29},{6,30},{7,31},{8,16},{9,... | collective-permute-start | bytes 208904 | tf_op jit(solution)/shard_map/ppermute | solution.py:370
  6.7 5.9 %collective-permute-start.1 = (bf16[16,2176]{1,0:T(8,128)(2,1)S(1)}, bf16[16,2176]{1,0:T(8,128)(2,1)S(1)}, u32[]{:S(2)}, u32[]{:S(2)}) collective-permute-start(bf16[16,2176]{1,0:T(8,128)(2,1)S(1)} %label.1.refs_0_), channel_id=1, source_target_pairs={{0,16},{1,17},{2,18},{3,19},{4,20},{5,21},{6,22},{7,23},{8,24},{9,... | collective-permute-start | bytes 208904 | tf_op jit(solution)/shard_map/ppermute | solution.py:370
  6.7 5.9 %collective-permute-start.2 = (bf16[16,2176]{1,0:T(8,128)(2,1)S(1)}, bf16[16,2176]{1,0:T(8,128)(2,1)S(1)}, u32[]{:S(2)}, u32[]{:S(2)}) collective-permute-start(bf16[16,2176]{1,0:T(8,128)(2,1)S(1)} %label.1.refs_0_), channel_id=1, source_target_pairs={{0,8},{1,9},{2,10},{3,11},{4,12},{5,13},{6,14},{7,15},{8,0},{9,1},... | collective-permute-start | bytes 208904 | tf_op jit(solution)/shard_map/ppermute | solution.py:370
  12.6 1.6 %collective-permute-start.3 = (bf16[64,2176]{1,0:T(8,128)(2,1)S(1)}, bf16[64,2176]{1,0:T(8,128)(2,1)S(1)}, u32[]{:S(2)}, u32[]{:S(2)}) collective-permute-start(bf16[64,2176]{1,0:T(8,128)(2,1)S(1)} %stack.1.refs_0_), channel_id=1, source_target_pairs={{0,1},{1,0},{2,3},{3,2},{4,5},{5,4},{6,7},{7,6},{8,9},{9,8},{10,11... | collective-permute-start | bytes 835592 | tf_op jit(solution)/shard_map/ppermute | solution.py:370
  12.7 6.6 %collective-permute-start.4 = (bf16[64,2176]{1,0:T(8,128)(2,1)S(1)}, bf16[64,2176]{1,0:T(8,128)(2,1)S(1)}, u32[]{:S(2)}, u32[]{:S(2)}) collective-permute-start(bf16[64,2176]{1,0:T(8,128)(2,1)S(1)} %stack.1.refs_0_), channel_id=1, source_target_pairs={{0,2},{1,5},{2,0},{3,7},{4,6},{5,1},{6,4},{7,3},{8,10},{9,13},{10,... | collective-permute-start | bytes 835592 | tf_op jit(solution)/shard_map/ppermute | solution.py:365
  14.3 8.1 %collective-permute-start.10 = (bf16[64,2176]{1,0:T(8,128)(2,1)S(1)}, bf16[64,2176]{1,0:T(8,128)(2,1)S(1)}, u32[]{:S(2)}, u32[]{:S(2)}) collective-permute-start(bf16[64,2176]{1,0:T(8,128)(2,1)S(1)} %collective-permute-done.3.refs_1_), channel_id=1, source_target_pairs={{0,2},{1,5},{2,0},{3,7},{4,6},{5,1},{6,4},{7,3},{8,10},{9,13},{10,... | collective-permute-start | bytes 835592 | tf_op jit(solution)/shard_map/ppermute | solution.py:365
  19.4 1.8 %collective-permute-start.5 = (bf16[32,2176]{1,0:T(8,128)(2,1)S(1)}, bf16[32,2176]{1,0:T(8,128)(2,1)S(1)}, u32[]{:S(2)}, u32[]{:S(2)}) collective-permute-start(bf16[32,2176]{1,0:T(8,128)(2,1)S(1)} %get-tuple-element.26), channel_id=1, source_target_pairs={{0,1},{1,0},{2,3},{3,2},{4,5},{5,4},{6,7},{7,6},{8,9},{9,8},{10,11... | collective-permute-start | bytes 417800 | tf_op jit(solution)/shard_map/ppermute | solution.py:370
  19.4 1.7 %collective-permute-start.6 = (bf16[32,2176]{1,0:T(8,128)(2,1)S(1)}, bf16[32,2176]{1,0:T(8,128)(2,1)S(1)}, u32[]{:S(2)}, u32[]{:S(2)}) collective-permute-start(bf16[32,2176]{1,0:T(8,128)(2,1)S(1)} %get-tuple-element.27), channel_id=1, source_target_pairs={{0,1},{1,0},{2,3},{3,2},{4,5},{5,4},{6,7},{7,6},{8,9},{9,8},{10,11... | collective-permute-start | bytes 417800 | tf_op jit(solution)/shard_map/ppermute | solution.py:370
  19.9 6.8 %collective-permute-start.16 = (bf16[64,2176]{1,0:T(8,128)(2,1)S(1)}, bf16[64,2176]{1,0:T(8,128)(2,1)S(1)}, u32[]{:S(2)}, u32[]{:S(2)}) collective-permute-start(bf16[64,2176]{1,0:T(8,128)(2,1)S(1)} %collective-permute-done.4.block_ref.refs_0_), channel_id=1, source_target_pairs={{0,5},{1,2},{2,7},{3,0},{4,1},{5,6},{6,3},{7,4},{8,13},{9,10},{10,... | collective-permute-start | bytes 835592 | tf_op jit(solution)/shard_map/ppermute | solution.py:365
  22.5 2.4 %collective-permute-start.11 = (bf16[32,2176]{1,0:T(8,128)(2,1)S(1)}, bf16[32,2176]{1,0:T(8,128)(2,1)S(1)}, u32[]{:S(2)}, u32[]{:S(2)}) collective-permute-start(bf16[32,2176]{1,0:T(8,128)(2,1)S(1)} %get-tuple-element.32), channel_id=1, source_target_pairs={{0,1},{1,0},{2,3},{3,2},{4,5},{5,4},{6,7},{7,6},{8,9},{9,8},{10,11... | collective-permute-start | bytes 417800 | tf_op jit(solution)/shard_map/ppermute | solution.py:370
  22.9 1.9 %collective-permute-start.12 = (bf16[32,2176]{1,0:T(8,128)(2,1)S(1)}, bf16[32,2176]{1,0:T(8,128)(2,1)S(1)}, u32[]{:S(2)}, u32[]{:S(2)}) collective-permute-start(bf16[32,2176]{1,0:T(8,128)(2,1)S(1)} %get-tuple-element.33), channel_id=1, source_target_pairs={{0,1},{1,0},{2,3},{3,2},{4,5},{5,4},{6,7},{7,6},{8,9},{9,8},{10,11... | collective-permute-start | bytes 417800 | tf_op jit(solution)/shard_map/ppermute | solution.py:370
  23.0 1.4 %collective-permute-start.7 = (bf16[32,2048]{1,0:T(8,128)(2,1)S(1)}, bf16[32,2048]{1,0:T(8,128)(2,1)S(1)}, u32[]{:S(2)}, u32[]{:S(2)}) collective-permute-start(bf16[32,2048]{1,0:T(8,128)(2,1)S(1)} %get-tuple-element.29), channel_id=1, source_target_pairs={{0,1},{1,0},{2,3},{3,2},{4,5},{5,4},{6,7},{7,6},{8,9},{9,8},{10,11... | collective-permute-start | bytes 393224 | tf_op jit(solution)/shard_map/ppermute | solution.py:370
  23.4 1.3 %collective-permute-start.8 = (bf16[32,2048]{1,0:T(8,128)(2,1)S(1)}, bf16[32,2048]{1,0:T(8,128)(2,1)S(1)}, u32[]{:S(2)}, u32[]{:S(2)}) collective-permute-start(bf16[32,2048]{1,0:T(8,128)(2,1)S(1)} %get-tuple-element.30), channel_id=1, source_target_pairs={{0,1},{1,0},{2,3},{3,2},{4,5},{5,4},{6,7},{7,6},{8,9},{9,8},{10,11... | collective-permute-start | bytes 393224 | tf_op jit(solution)/shard_map/ppermute | solution.py:370
  26.1 2.5 %collective-permute-start.13 = (bf16[32,2048]{1,0:T(8,128)(2,1)S(1)}, bf16[32,2048]{1,0:T(8,128)(2,1)S(1)}, u32[]{:S(2)}, u32[]{:S(2)}) collective-permute-start(bf16[32,2048]{1,0:T(8,128)(2,1)S(1)} %get-tuple-element.35), channel_id=1, source_target_pairs={{0,1},{1,0},{2,3},{3,2},{4,5},{5,4},{6,7},{7,6},{8,9},{9,8},{10,11... | collective-permute-start | bytes 393224 | tf_op jit(solution)/shard_map/ppermute | solution.py:370
  26.4 2.2 %collective-permute-start.14 = (bf16[32,2048]{1,0:T(8,128)(2,1)S(1)}, bf16[32,2048]{1,0:T(8,128)(2,1)S(1)}, u32[]{:S(2)}, u32[]{:S(2)}) collective-permute-start(bf16[32,2048]{1,0:T(8,128)(2,1)S(1)} %get-tuple-element.36), channel_id=1, source_target_pairs={{0,1},{1,0},{2,3},{3,2},{4,5},{5,4},{6,7},{7,6},{8,9},{9,8},{10,11... | collective-permute-start | bytes 393224 | tf_op jit(solution)/shard_map/ppermute | solution.py:370
  26.7 2.7 %collective-permute-start.17 = (bf16[32,2176]{1,0:T(8,128)(2,1)S(1)}, bf16[32,2176]{1,0:T(8,128)(2,1)S(1)}, u32[]{:S(2)}, u32[]{:S(2)}) collective-permute-start(bf16[32,2176]{1,0:T(8,128)(2,1)S(1)} %get-tuple-element.37), channel_id=1, source_target_pairs={{0,1},{1,0},{2,3},{3,2},{4,5},{5,4},{6,7},{7,6},{8,9},{9,8},{10,11... | collective-permute-start | bytes 417800 | tf_op jit(solution)/shard_map/ppermute | solution.py:370
  27.0 2.5 %collective-permute-start.18 = (bf16[32,2176]{1,0:T(8,128)(2,1)S(1)}, bf16[32,2176]{1,0:T(8,128)(2,1)S(1)}, u32[]{:S(2)}, u32[]{:S(2)}) collective-permute-start(bf16[32,2176]{1,0:T(8,128)(2,1)S(1)} %get-tuple-element.38), channel_id=1, source_target_pairs={{0,1},{1,0},{2,3},{3,2},{4,5},{5,4},{6,7},{7,6},{8,9},{9,8},{10,11... | collective-permute-start | bytes 417800 | tf_op jit(solution)/shard_map/ppermute | solution.py:370
  27.3 7.3 %collective-permute-start.9 = (bf16[64,2048]{1,0:T(8,128)(2,1)S(1)}, bf16[64,2048]{1,0:T(8,128)(2,1)S(1)}, u32[]{:S(2)}, u32[]{:S(2)}) collective-permute-start(bf16[64,2048]{1,0:T(8,128)(2,1)S(1)} %add.68.refs_5_), channel_id=1, source_target_pairs={{0,2},{1,5},{2,0},{3,7},{4,6},{5,1},{6,4},{7,3},{8,10},{9,13},{10,... | collective-permute-start | bytes 786440 | tf_op jit(solution)/shard_map/ppermute | solution.py:365
  28.7 7.8 %collective-permute-start.15 = (bf16[64,2048]{1,0:T(8,128)(2,1)S(1)}, bf16[64,2048]{1,0:T(8,128)(2,1)S(1)}, u32[]{:S(2)}, u32[]{:S(2)}) collective-permute-start(bf16[64,2048]{1,0:T(8,128)(2,1)S(1)} %add.69.refs_5_), channel_id=1, source_target_pairs={{0,2},{1,5},{2,0},{3,7},{4,6},{5,1},{6,4},{7,3},{8,10},{9,13},{10,... | collective-permute-start | bytes 786440 | tf_op jit(solution)/shard_map/ppermute | solution.py:365
  30.8 1.8 %collective-permute-start.19 = (bf16[32,2048]{1,0:T(8,128)(2,1)S(1)}, bf16[32,2048]{1,0:T(8,128)(2,1)S(1)}, u32[]{:S(2)}, u32[]{:S(2)}) collective-permute-start(bf16[32,2048]{1,0:T(8,128)(2,1)S(1)} %get-tuple-element.40), channel_id=1, source_target_pairs={{0,1},{1,0},{2,3},{3,2},{4,5},{5,4},{6,7},{7,6},{8,9},{9,8},{10,11... | collective-permute-start | bytes 393224 | tf_op jit(solution)/shard_map/ppermute | solution.py:370
  30.9 1.8 %collective-permute-start.20 = (bf16[32,2048]{1,0:T(8,128)(2,1)S(1)}, bf16[32,2048]{1,0:T(8,128)(2,1)S(1)}, u32[]{:S(2)}, u32[]{:S(2)}) collective-permute-start(bf16[32,2048]{1,0:T(8,128)(2,1)S(1)} %get-tuple-element.41), channel_id=1, source_target_pairs={{0,1},{1,0},{2,3},{3,2},{4,5},{5,4},{6,7},{7,6},{8,9},{9,8},{10,11... | collective-permute-start | bytes 393224 | tf_op jit(solution)/shard_map/ppermute | solution.py:370
  32.7 7.1 %collective-permute-start.23 = (bf16[32,2048]{1,0:T(8,128)(2,1)S(1)}, bf16[32,2048]{1,0:T(8,128)(2,1)S(1)}, u32[]{:S(2)}, u32[]{:S(2)}) collective-permute-start(bf16[32,2048]{1,0:T(8,128)(2,1)S(1)} %slice.37), channel_id=1, source_target_pairs={{0,7},{1,6},{2,5},{3,4},{4,3},{5,2},{6,1},{7,0},{8,15},{9,14},{10,... | collective-permute-start | bytes 393224 | tf_op jit(solution)/shard_map/ppermute | solution.py:370
  36.6 3.2 %collective-permute-start.21 = (bf16[64,2048]{1,0:T(8,128)(2,1)S(1)}, bf16[64,2048]{1,0:T(8,128)(2,1)S(1)}, u32[]{:S(2)}, u32[]{:S(2)}) collective-permute-start(bf16[64,2048]{1,0:T(8,128)(2,1)S(1)} %add.71), channel_id=1, source_target_pairs={{0,1},{1,0},{2,3},{3,2},{4,5},{5,4},{6,7},{7,6},{8,9},{9,8},{10,11... | collective-permute-start | bytes 786440 | tf_op jit(solution)/shard_map/ppermute | solution.py:370
  36.7 6.1 %collective-permute-start.26 = (bf16[16,2048]{1,0:T(8,128)(2,1)S(1)}, bf16[16,2048]{1,0:T(8,128)(2,1)S(1)}, u32[]{:S(2)}, u32[]{:S(2)}) collective-permute-start(bf16[16,2048]{1,0:T(8,128)(2,1)S(1)} %get-tuple-element.43), channel_id=1, source_target_pairs={{0,7},{1,6},{2,5},{3,4},{4,3},{5,2},{6,1},{7,0},{8,15},{9,14},{10,... | collective-permute-start | bytes 196616 | tf_op jit(solution)/shard_map/ppermute | solution.py:370
  39.7 5.4 %collective-permute-start.22 = (bf16[16,2048]{1,0:T(8,128)(2,1)S(1)}, bf16[16,2048]{1,0:T(8,128)(2,1)S(1)}, u32[]{:S(2)}, u32[]{:S(2)}) collective-permute-start(bf16[16,2048]{1,0:T(8,128)(2,1)S(1)} %get-tuple-element.42), channel_id=1, source_target_pairs={{0,7},{1,6},{2,5},{3,4},{4,3},{5,2},{6,1},{7,0},{8,15},{9,14},{10,... | collective-permute-start | bytes 196616 | tf_op jit(solution)/shard_map/ppermute | solution.py:370
  39.9 6.9 %collective-permute-start.24 = (bf16[16,2048]{1,0:T(8,128)(2,1)S(1)}, bf16[16,2048]{1,0:T(8,128)(2,1)S(1)}, u32[]{:S(2)}, u32[]{:S(2)}) collective-permute-start(bf16[16,2048]{1,0:T(8,128)(2,1)S(1)} %get-tuple-element.44), channel_id=1, source_target_pairs={{0,24},{1,25},{2,26},{3,27},{4,28},{5,29},{6,30},{7,31},{8,16},{9,... | collective-permute-start | bytes 196616 | tf_op jit(solution)/shard_map/ppermute | solution.py:370
  42.7 6.2 %collective-permute-start.25 = (bf16[16,2048]{1,0:T(8,128)(2,1)S(1)}, bf16[16,2048]{1,0:T(8,128)(2,1)S(1)}, u32[]{:S(2)}, u32[]{:S(2)}) collective-permute-start(bf16[16,2048]{1,0:T(8,128)(2,1)S(1)} %get-tuple-element.45), channel_id=1, source_target_pairs={{0,16},{1,17},{2,18},{3,19},{4,20},{5,21},{6,22},{7,23},{8,24},{9,... | collective-permute-start | bytes 196616 | tf_op jit(solution)/shard_map/ppermute | solution.py:370
  42.7 6.2 %collective-permute-start.27 = (bf16[16,2048]{1,0:T(8,128)(2,1)S(1)}, bf16[16,2048]{1,0:T(8,128)(2,1)S(1)}, u32[]{:S(2)}, u32[]{:S(2)}) collective-permute-start(bf16[16,2048]{1,0:T(8,128)(2,1)S(1)} %fusion.1), channel_id=1, source_target_pairs={{0,8},{1,9},{2,10},{3,11},{4,12},{5,13},{6,14},{7,15},{8,0},{9,1},... | collective-permute-start | bytes 196616 | tf_op jit(solution)/shard_map/ppermute | solution.py:370
